TPU v7x, 256 devices: a whole 4x4x8 slice. The times are simulated.
256 devices in a mesh: batch: 2 (over core), gz: 8 (over z), gy: 16 (over x, y).
Axes of the slice: x: 4, y: 4, z: 8, core: 2. Of those that a mesh axis runs over, the one named last changes fastest.
Arguments:
- volume: float32 [2, 4, 64, 256, 512], P('batch', None, 'gz', 'gy'), may hold values from -20 to 20
- conv_one: bfloat16 [16, 4, 3, 3, 3], replicated, may hold values from -0.625 to 0.625
- conv_two: bfloat16 [32, 16, 3, 3, 3], replicated, may hold values from -0.3125 to 0.3125
- conv_three: bfloat16 [64, 32, 3, 3, 3], replicated, may hold values from -0.21875 to 0.21875
- head_weight: float32 [4, 64], replicated, may hold values from -3 to 3
- targets: float32 [2, 4], P('batch'), may hold values from -4 to 4
Outputs:
- update_one: float32 [16, 4, 3, 3, 3], replicated
- update_two: float32 [32, 16, 3, 3, 3], replicated
- update_three: float32 [64, 32, 3, 3, 3], replicated
- update_head: float32 [4, 64], replicated
- total_loss: float32 [], replicated
All inputs are finite; a program needn't handle non-finite values.
Results may differ from a plain program's by a relative error of at most 0.012.
Values may be sent and summed in bfloat16 or wider, within the bound.
No kernel may reach another device: no remote copies, remote signals or barrier semaphores. Data moves between devices by JAX's collectives and lax.ppermute only.
A program may use at most 192 MiB of HBM per device.

v0:
```python
import jax
import jax.numpy as jnp
from jax import lax
from jax.sharding import PartitionSpec as P

epsilon = 1e-06
highest = lax.Precision.HIGHEST
layout = ("NCDHW", "OIDHW", "NCDHW")


def passed_along(x, axis, by):
    count = lax.axis_size(axis)
    pairs = [(i, i + by) for i in range(count) if 0 <= i + by < count]
    return lax.ppermute(x, axis, pairs)


def as_sent(x):
    return jax.tree.map(lambda a: a.astype(jnp.bfloat16) if a.dtype == jnp.float32 else a, x)


def activate(pre_act):
    return 0.65 * pre_act + 0.35 * (jnp.sqrt(pre_act * pre_act + 1.0) - 1.0)


def slope_of(pre_act):
    return 0.65 + 0.35 * pre_act / jnp.sqrt(pre_act * pre_act + 1.0)


def normalized(gradient):
    return gradient / jnp.sqrt(jnp.mean(gradient * gradient) + epsilon)


def extend(source):
    got_row = passed_along(source[:, :, -1:, :], "gy", 1)
    widened = jnp.concatenate([got_row, source], axis=2)
    lower = passed_along(widened[:, -1:, :, :], "gz", 1)
    extended = jnp.concatenate([lower, widened], axis=1)
    return jnp.pad(extended, ((0, 0), (0, 0), (0, 0), (1, 0)))


def local_conv(extended, kernel):
    return lax.conv_general_dilated(
        extended[None],
        kernel,
        (2, 2, 2),
        [(0, 0), (0, 0), (0, 0)],
        dimension_numbers=layout,
        preferred_element_type=jnp.float32,
    )[0]


def exact_conv(extended, kernel):
    return lax.conv_general_dilated(
        extended[None],
        kernel,
        (2, 2, 2),
        [(0, 0), (0, 0), (0, 0)],
        dimension_numbers=layout,
        precision=highest,
    )[0]


def forward_layer(source, kernel):
    extended = extend(source)
    return (extended, local_conv(extended, kernel))


def return_rims(grid):
    got_plane = passed_along(grid[:, 0:1, :, :].astype(jnp.bfloat16), "gz", -1).astype(jnp.float32)
    remain = grid[:, 1:, :, :]
    remain = remain + jnp.pad(got_plane, ((0, 0), (remain.shape[1] - 1, 0), (0, 0), (0, 0)))
    got_row = passed_along(as_sent(remain[:, :, 0:1, :]), "gy", -1)
    remain = remain[:, :, 1:, :]
    return remain + jnp.pad(got_row, ((0, 0), (0, 0), (remain.shape[2] - 1, 0), (0, 0)))


def input_grad(kernel, errors, extended):
    kernel_f = kernel.astype(jnp.float32)
    _, pullback = jax.vjp(lambda values: exact_conv(values, kernel_f), extended.astype(jnp.float32))
    grid = pullback(errors.astype(jnp.float32))[0]
    return return_rims(grid[:, :, :, 1:])


def weight_grad(errors, extended, kernel):
    source_f = extended.astype(jnp.float32)
    _, pullback = jax.vjp(lambda weights: exact_conv(source_f, weights), kernel.astype(jnp.float32))
    return pullback(errors.astype(jnp.float32))[0]


def local(volume, conv_one, conv_two, conv_three, head_weight, targets):
    inputs = volume[0].astype(jnp.bfloat16)
    ext_one, pre_one = forward_layer(inputs, conv_one)
    act_one = activate(pre_one).astype(jnp.bfloat16)
    ext_two, pre_two = forward_layer(act_one, conv_two)
    act_two = activate(pre_two).astype(jnp.bfloat16)
    ext_three, pre_three = forward_layer(act_two, conv_three)
    act_three = activate(pre_three).astype(jnp.bfloat16)
    local_cells = pre_three.shape[1] * pre_three.shape[2] * pre_three.shape[3]
    cell_count = local_cells * lax.axis_size("gz") * lax.axis_size("gy")
    channel_sums = jnp.sum(act_three.astype(jnp.float32), axis=(1, 2, 3))
    pooled = lax.psum(channel_sums, ("gz", "gy")) / cell_count
    predicted = jnp.dot(head_weight, pooled, precision=highest)
    errors = predicted - targets[0]
    leader = (lax.axis_index("gz") == 0) & (lax.axis_index("gy") == 0)
    weight_share = jnp.where(leader, 1.0, 0.0).astype(jnp.float32)
    loss_term = weight_share * (0.5 * jnp.sum(errors * errors))
    head_term = weight_share * jnp.outer(errors, pooled)
    back_pool = jnp.dot(errors, head_weight, precision=highest) / cell_count
    err_three = (back_pool[:, None, None, None] * slope_of(pre_three)).astype(jnp.bfloat16)
    grad_three = weight_grad(err_three, ext_three, conv_three)
    back_two = input_grad(conv_three, err_three, ext_three)
    err_two = (back_two * slope_of(pre_two)).astype(jnp.bfloat16)
    grad_two = weight_grad(err_two, ext_two, conv_two)
    back_one = input_grad(conv_two, err_two, ext_two)
    err_one = (back_one * slope_of(pre_one)).astype(jnp.bfloat16)
    grad_one = weight_grad(err_one, ext_one, conv_one)
    head_sum, three_sum, two_sum, one_sum, total_loss = lax.psum(
        (head_term, grad_three, grad_two, grad_one, loss_term), ("batch", "gz", "gy")
    )
    return (
        normalized(one_sum),
        normalized(two_sum),
        normalized(three_sum),
        normalized(head_sum),
        total_loss,
    )


def solution(mesh):
    in_specs = (P("batch", None, "gz", "gy", None), P(), P(), P(), P(), P("batch", None))
    out_specs = (P(), P(), P(), P(), P())
    return jax.shard_map(local, mesh=mesh, in_specs=in_specs, out_specs=out_specs, check_vma=False)
```

profile of v0, /device:TPU:32, one launch (start us, length us, event | category | flops | bytes accessed | tf_op | source)
XLA Modules:
  0.0 1028.6 jit_solution(3001992697342417378)
XLA Ops:
  8.7 3.5 collective-permute-start
  14.1 3.8 collective-permute-start.1
  25.5 10.8 %copy.124 = bf16[4,9,17,1,8,66]{4,0,5,2,1,3:T(4,128)(2,1)} copy(bf16[4,9,17,1,8,66]{5,4,2,1,0,3:T(8,128)(2,1)S(1)} %reshape.218) | data formatting | bytes 1292544 | tf_op jit(solution)/shard_map/conv_general_dilated | solution.py:42
  37.6 32.7 %fusion.3 = f32[4,8,8,33,16]{4,2,3,1,0:T(8,128)} fusion(bf16[16,4,3,3,3]{0,1,4,3,2:T(4,128)(2,1)S(1)} %copy-done.19, bf16[4,9,17,1,7,2]{4,0,5,2,1,3:T(4,128)(2,1)S(1)} %slice.88, bf16[4,9,17,1,8,66]{4,0,5,2,1,3:T(4,128)(2,1)} %copy.124), kind=kOutput, calls=%fused_computation.4 | convolution fusion | flops 31193856 | bytes 1207536 | tf_op jit(solution)/shard_map/conv_general_dilated | solution.py:42
  70.3 4.7 copy.125
  75.0 3.0 select_multiply_fusion
  87.7 4.3 collective-permute-start.2
  93.5 3.8 collective-permute-start.3
  102.2 3.9 copy.129
  107.1 4.7 multiply_divide_fusion.1
  113.8 4.9 collective-permute-start.4
  121.8 4.1 collective-permute-start.5
  131.1 68.4 %copy.147 = bf16[1,4,9,17,513]{1,0,4,3,2:T(2,128)(2,1)} copy(bf16[1,4,9,17,513]{4,3,2,1,0:T(8,128)(2,1)S(1)} %get-tuple-element.13) | data formatting | bytes 1255824 | tf_op jit(solution)/shard_map/jvp()/broadcast_in_dim | solution.py:54
  200.6 11.9 %copy.149 = bf16[1,16,5,9,257]{1,0,4,3,2:T(2,128)(2,1)} copy(bf16[1,16,5,9,257]{4,1,3,2,0:T(8,128)(2,1)S(1)} %copy-done.4) | data formatting | bytes 740160 | tf_op jit(solution)/shard_map/broadcast_in_dim | solution.py:43
  218.6 311.7 %psum.42 = f32[64]{0:T(128)S(1)} all-reduce(f32[64]{0:T(128)S(1)} %convert_reduce_fusion), channel_id=1, replica_groups=mesh['batch'=2,'gz'=8,'gy'=16] {'gz','gy'}, use_global_device_ids=true, to_apply=%region_1.2 | all-reduce | flops 64 | bytes 512 | tf_op jit(solution)/shard_map/psum | solution.py:101
  535.4 41.2 %collective-permute-start.6 = (bf16[32,1,5,128]{3,0,2,1:T(8,128)(2,1)S(1)}, bf16[32,1,5,128]{3,0,2,1:T(8,128)(2,1)S(1)}, u32[]{:S(2)}, u32[]{:S(2)}) collective-permute-start(bf16[32,1,5,128]{3,0,2,1:T(8,128)(2,1)S(1)} %slice.175), channel_id=1, source_target_pairs={{16,0},{32,16},{48,32},{64,48},{80,64},{96,80},{112,96},{17,1},{33... | collective-permute-start | bytes 122888 | tf_op jit(solution)/shard_map/ppermute | solution.py:14
  585.8 7.4 broadcast_select_fusion
  593.2 5.0 copy.144
  601.5 4.5 collective-permute-start.8
  606.0 13.7 %fusion.117 = f32[32,16,3,3,3]{0,1,4,3,2:T(8,128)S(1)} fusion(bf16[1,16,5,9,257]{1,0,4,3,2:T(2,128)(2,1)} %copy.149, bf16[1,32,2,4,128]{1,0,4,3,2:T(2,128)(2,1)S(1)} %copy-done.12), kind=kOutput, calls=%fused_computation.160 | convolution fusion | flops 28311552 | bytes 490912 | tf_op jit(solution)/shard_map/transpose(jvp())/conv_general_dilated | solution.py:53
  619.8 212.0 %all-reduce.10.cloned.1.call-done = f32[64,32,3,3,3]{0,1,4,3,2:T(8,128)} async-done(((f32[64,32,3,3,3]{0,1,4,3,2:T(8,128)}), f32[64,32,3,3,3]{0,1,4,3,2:T(8,128)}) %all-reduce.10.cloned.1.call-update) | async-done | bytes 221200 | tf_op jit(solution)/shard_map/psum | solution.py:117
  840.3 7.2 copy.148
  847.5 87.2 %fusion.116 = f32[16,4,3,3,3]{0,1,4,3,2:T(4,128)S(1)} fusion(bf16[1,4,9,17,513]{1,0,4,3,2:T(2,128)(2,1)} %copy.147, bf16[1,16,4,8,256]{1,0,4,3,2:T(2,128)(2,1)} %copy.148), kind=kOutput, calls=%fused_computation.159 | convolution fusion | flops 28311552 | bytes 896968 | tf_op jit(solution)/shard_map/transpose(jvp())/conv_general_dilated | solution.py:53
  934.8 80.6 %all-reduce.7 = (f32[16,4,3,3,3]{0,1,4,3,2:T(4,128)S(1)}, f32[32,16,3,3,3]{0,1,4,3,2:T(8,128)S(1)}, f32[4,64]{1,0:T(4,128)S(1)}, f32[]{:T(128)}) all-reduce(f32[16,4,3,3,3]{0,1,4,3,2:T(4,128)S(1)} %fusion.116, f32[32,16,3,3,3]{0,1,4,3,2:T(8,128)S(1)} %fusion.117, ...), channel_id=1, replica_groups=mesh['batch'=2,'gz'=8,'gy'=16] {'batch','gz','gy'}, use_global_device_ids=true, to_apply=%region_2.3 | all-reduce | flops 15809 | bytes 126472 | tf_op jit(solution)/shard_map/psum | solution.py:117
  (140 shorter events, 75.1 us)
Async XLA Ops:
  7.2 210.5 %copy-start = (bf16[64,32,3,3,3]{0,1,4,3,2:T(8,128)(2,1)S(1)}, bf16[64,32,3,3,3]{0,1,4,3,2:T(8,128)(2,1)}, u32[]{:S(2)}) copy-start(bf16[64,32,3,3,3]{0,1,4,3,2:T(8,128)(2,1)} %param.9) | copy-start | bytes 331780
  7.2 824.6 %all-reduce.10.cloned.1.call-start = ((), (), s32[]{:S(2)}) async-start(), calls=%async_computation | async-start | bytes 884736 | tf_op jit(solution)/shard_map/psum | solution.py:117
  8.7 5.4 collective-permute-start
  14.1 6.5 collective-permute-start.1
  25.5 12.0 %copy-start.19 = (bf16[16,4,3,3,3]{0,1,4,3,2:T(4,128)(2,1)S(1)}, bf16[16,4,3,3,3]{0,1,4,3,2:T(4,128)(2,1)}, u32[]{:S(2)}) copy-start(bf16[16,4,3,3,3]{0,1,4,3,2:T(4,128)(2,1)} %param.7) | copy-start | bytes 10372
  87.7 5.9 collective-permute-start.2
  93.5 6.2 collective-permute-start.3
  111.8 14.2 %copy-start.2 = (f32[4,8,8,33,16]{3,4,2,1,0:T(8,128)S(1)}, f32[4,8,8,33,16]{3,4,2,1,0:T(8,128)}, u32[]{:S(2)}) copy-start(f32[4,8,8,33,16]{3,4,2,1,0:T(8,128)} %get-tuple-element.11) | copy-start | bytes 1622020
  113.8 7.0 collective-permute-start.4
  121.8 90.6 %collective-permute-start.5 = (bf16[32,1,5,128]{3,0,2,1:T(8,128)(2,1)S(1)}, bf16[32,1,5,128]{3,0,2,1:T(8,128)(2,1)}, u32[]{:S(2)}, u32[]{:S(2)}) collective-permute-start(bf16[32,1,5,128]{3,0,2,1:T(8,128)(2,1)S(1)} %pad_maximum_fusion.2), channel_id=1, source_target_pairs={{0,16},{16,32},{32,48},{48,64},{64,80},{80,96},{96,112},{1,17},{17... | collective-permute-start | bytes 122888 | tf_op jit(solution)/shard_map/ppermute | solution.py:14
  131.1 68.4 %copy-start.9 = (f32[2,4,8,17,32]{4,2,3,1,0:T(8,128)S(1)}, f32[2,4,8,17,32]{4,2,3,1,0:T(8,128)}, u32[]{:S(2)}) copy-start(f32[2,4,8,17,32]{4,2,3,1,0:T(8,128)} %get-tuple-element.14) | copy-start | bytes 417796
  215.9 314.3 %copy-start.20 = (f32[4,64]{1,0:T(4,128)S(1)}, f32[4,64]{1,0:T(4,128)}, u32[]{:S(2)}) copy-start(f32[4,64]{1,0:T(4,128)} %param.10) | copy-start | bytes 3076
  215.9 314.3 %copy-start.21 = (f32[1,4]{1,0:T(1,128)S(1)}, f32[1,4]{1,0:T(1,128)}, u32[]{:S(2)}) copy-start(f32[1,4]{1,0:T(1,128)} %param.11) | copy-start | bytes 52
  534.7 41.9 %copy-start.7 = (bf16[32,3,5,1,8,17]{0,4,5,2,1,3:T(8,128)(2,1)S(1)}, bf16[32,3,5,1,8,17]{0,4,5,2,1,3:T(8,128)(2,1)}, u32[]{:S(2)}) copy-start(bf16[32,3,5,1,8,17]{0,4,5,2,1,3:T(8,128)(2,1)} %slice.115) | copy-start | bytes 391684
  535.2 41.5 %copy-start.10 = (bf16[32,3,5,8,18,1]{0,3,5,4,2,1:T(8,128)(2,1)S(1)}, bf16[32,3,5,8,18,1]{0,3,5,4,2,1:T(8,128)(2,1)}, u32[]{:S(2)}) copy-start(bf16[32,3,5,8,18,1]{0,3,5,4,2,1:T(8,128)(2,1)} %copy.154) | copy-start | bytes 414724
  535.3 41.5 %copy-start.11 = (bf16[32,3,5,8,18,1]{0,3,5,4,2,1:T(8,128)(2,1)S(1)}, bf16[32,3,5,8,18,1]{0,3,5,4,2,1:T(8,128)(2,1)}, u32[]{:S(2)}) copy-start(bf16[32,3,5,8,18,1]{0,3,5,4,2,1:T(8,128)(2,1)} %get-tuple-element.17) | copy-start | bytes 414724
  535.4 42.9 %collective-permute-start.6 = (bf16[32,1,5,128]{3,0,2,1:T(8,128)(2,1)S(1)}, bf16[32,1,5,128]{3,0,2,1:T(8,128)(2,1)S(1)}, u32[]{:S(2)}, u32[]{:S(2)}) collective-permute-start(bf16[32,1,5,128]{3,0,2,1:T(8,128)(2,1)S(1)} %slice.175), channel_id=1, source_target_pairs={{16,0},{32,16},{48,32},{64,48},{80,64},{96,80},{112,96},{17,1},{33... | collective-permute-start | bytes 122888 | tf_op jit(solution)/shard_map/ppermute | solution.py:14
  578.1 7.7 copy-start.15
  578.4 5.6 collective-permute-start.7
  601.5 232.6 %collective-permute-start.8 = (bf16[16,1,9,256]{3,0,2,1:T(8,128)(2,1)S(1)}, bf16[16,1,9,256]{3,0,2,1:T(8,128)(2,1)S(1)}, u32[]{:S(2)}, u32[]{:S(2)}) collective-permute-start(bf16[16,1,9,256]{3,0,2,1:T(8,128)(2,1)S(1)} %slice.174), channel_id=1, source_target_pairs={{16,0},{32,16},{48,32},{64,48},{80,64},{96,80},{112,96},{17,1},{33... | collective-permute-start | bytes 221192 | tf_op jit(solution)/shard_map/ppermute | solution.py:14
  619.8 220.5 %copy-start.6 = (f32[4,8,1,264,16]{3,4,1,0,2:T(8,128)S(1)}, f32[4,8,1,264,16]{3,4,1,0,2:T(8,128)}, u32[]{:S(2)}) copy-start(f32[4,8,1,264,16]{3,4,1,0,2:T(8,128)} %reshape.118) | copy-start | bytes 1622020
  834.4 5.8 collective-permute-start.9
  847.5 87.2 %copy-start.16 = (f32[4,64]{1,0:T(4,128)S(1)}, f32[4,64]{1,0:T(4,128)}, u32[]{:S(2)}) copy-start(f32[4,64]{1,0:T(4,128)} %multiply_multiply_fusion) | copy-start | bytes 3076
  847.5 173.7 %copy-start.1 = (bf16[64,32,3,3,3]{0,1,4,3,2:T(8,128)(2,1)S(1)}, bf16[64,32,3,3,3]{0,1,4,3,2:T(8,128)(2,1)}, u32[]{:S(2)}) copy-start(bf16[64,32,3,3,3]{0,1,4,3,2:T(8,128)(2,1)} %param.9) | copy-start | bytes 331780
  (10 other events, 37.9 us)
Sparse Core Ops, SparseCore 0:
  581.1 250.5 all-reduce.9
where the time goes:
time: 1040 us; the launch traced here: 1030 us
  blocking collectives  392 us (38%)
  waiting for transfers between devices  227 us (22%)
  local copies, waits for them, and re-layouts  151 us (15%)
  matrix products  149 us (14%)
  starting transfers between devices  73 us (7%)
  between operations  18.6 us (2%)
  other arithmetic  17.4 us (2%)
    psum x1, blocking collectives, local(): pooled = lax.psum(channel_sums, ('gz', 'gy')) / cell_count  312 us
    psum x1, waiting for transfers between devices, local(): lax.psum((head_term, grad_three, grad_two, grad_one, loss_term), ('batch'...  212 us
    conv_general_dilated x5, matrix products, exact_conv(): lax.conv_general_dilated(extended[None], kernel, (2, 2, 2), [(0, 0), (0,...  110 us
    psum x1, blocking collectives, local(): lax.psum((head_term, grad_three, grad_two, grad_one, loss_term), ('batch'...  80.6 us
    ppermute x10, starting transfers between devices, passed_along(): return lax.ppermute(x, axis, pairs)  72.9 us
    broadcast_in_dim x2, local copies, waits for them, and re-layouts, exact_conv(): extended[None]  69.5 us
    conv_general_dilated x3, matrix products, local_conv(): lax.conv_general_dilated(extended[None], kernel, (2, 2, 2), [(0, 0), (0,...  38.1 us
    conv_general_dilated x10, local copies, waits for them, and re-layouts, local_conv(): lax.conv_general_dilated(extended[None], kernel, (2, 2, 2), [(0, 0), (0,...  27.3 us
  transfers between devices with their start and end apart: 11, of which 9 were waited for; matrix products, arithmetic and copies ran while one was open for 12% of the time, Pallas kernels for 0%

commit v1 on v0

--- a/solution.py
+++ b/solution.py
@@ -28,6 +28,32 @@
 
 def normalized(gradient):
     return gradient / jnp.sqrt(jnp.mean(gradient * gradient) + epsilon)
+
+
+def gathered(x, axes):
+    count = lax.axis_size(axes)
+    return lax.all_to_all(jnp.broadcast_to(x[None], (count,) + x.shape), axes, 0, 0)
+
+
+def summed_over_volume(x):
+    return jnp.sum(gathered(x, ("gz", "gy")), axis=0)
+
+
+def summed_over_all(terms):
+    sizes = [t.size for t in terms]
+    total = sum(sizes)
+    columns = lax.axis_size("gy")
+    width = -(-total // (columns * 1024)) * 8
+    flat = jnp.concatenate([t.reshape(-1) for t in terms])
+    flat = jnp.pad(flat, (0, columns * width * 128 - total)).reshape(columns, width, 128)
+    own = jnp.sum(lax.all_to_all(flat, "gy", 0, 0), axis=0)
+    own = jnp.sum(gathered(own, ("batch", "gz")), axis=0)
+    flat = gathered(own, "gy").reshape(-1)
+    out, at = [], 0
+    for term, size in zip(terms, sizes):
+        out.append(flat[at : at + size].reshape(term.shape))
+        at += size
+    return out
 
 
 def extend(source):
@@ -98,7 +124,7 @@
     local_cells = pre_three.shape[1] * pre_three.shape[2] * pre_three.shape[3]
     cell_count = local_cells * lax.axis_size("gz") * lax.axis_size("gy")
     channel_sums = jnp.sum(act_three.astype(jnp.float32), axis=(1, 2, 3))
-    pooled = lax.psum(channel_sums, ("gz", "gy")) / cell_count
+    pooled = summed_over_volume(channel_sums) / cell_count
     predicted = jnp.dot(head_weight, pooled, precision=highest)
     errors = predicted - targets[0]
     leader = (lax.axis_index("gz") == 0) & (lax.axis_index("gy") == 0)
@@ -114,8 +140,8 @@
     back_one = input_grad(conv_two, err_two, ext_two)
     err_one = (back_one * slope_of(pre_one)).astype(jnp.bfloat16)
     grad_one = weight_grad(err_one, ext_one, conv_one)
-    head_sum, three_sum, two_sum, one_sum, total_loss = lax.psum(
-        (head_term, grad_three, grad_two, grad_one, loss_term), ("batch", "gz", "gy")
+    head_sum, three_sum, two_sum, one_sum, total_loss = summed_over_all(
+        (head_term, grad_three, grad_two, grad_one, loss_term)
     )
     return (
         normalized(one_sum),

time: 1040 us -> 512 us (0.49)
  blocking collectives: 392 us -> 46.3 us
  waiting for transfers between devices: 227 us -> 23.4 us
  local copies, waits for them, and re-layouts: 151 us -> 208 us
  starting transfers between devices: 73 us -> 54.2 us
  between operations: 18.6 us -> 5.3 us
    psum x2 -> x0, blocking collectives: 392 us -> none  [the longest x1 312 us: local(): pooled = lax.psum(channel_sums, ('gz', 'gy')) / cell_count]
    psum x1 -> x0, waiting for transfers between devices: 212 us -> none  [local(): lax.psum((head_term, grad_three, grad_two, grad_one, loss_term), ('batch'...]
    broadcast_in_dim x2 -> x3, local copies, waits for them, and re-layouts: 69.5 us -> 0.71 us  [gathered(): jnp.broadcast_to(x[None], (count,) + x.shape)]
    broadcast_in_dim x8 -> x10, local copies, waits for them, and re-layouts: 15.3 us -> 83.8 us  [local_conv(): extended[None]]
    all_to_all x0 -> x3, blocking collectives: none -> 46.3 us  [the longest x2 31 us: gathered(): lax.all_to_all(jnp.broadcast_to(x[None], (count,) + x.shape), axes, 0, 0)]
    ppermute x10, starting transfers between devices: 72.9 us -> 33.9 us  [passed_along(): return lax.ppermute(x, axis, pairs)]
    all_to_all x0 -> x1, starting transfers between devices: none -> 20.4 us  [gathered(): lax.all_to_all(jnp.broadcast_to(x[None], (count,) + x.shape), axes, 0, 0)]
    conv_general_dilated x6 -> x9, local copies, waits for them, and re-layouts: 8.32 us -> 24.6 us  [exact_conv(): lax.conv_general_dilated(extended[None], kernel, (2, 2, 2), [(0, 0), (0,...]
  transfers between devices with their start and end apart: 11 -> 11, of which waited for: 9 -> 8; matrix products, arithmetic and copies ran while one was open for 12% -> 27% of each run, Pallas kernels for 0% -> 0%
where the time goes in v1:
time: 512 us; the launch traced here: 502 us
  local copies, waits for them, and re-layouts  208 us (41%)
  matrix products  151 us (29%)
  starting transfers between devices  54.2 us (11%)
  blocking collectives  46.3 us (9%)
  waiting for transfers between devices  23.4 us (5%)
  other arithmetic  14.8 us (3%)
  between operations  5.3 us (1%)
    conv_general_dilated x5, matrix products, exact_conv(): lax.conv_general_dilated(extended[None], kernel, (2, 2, 2), [(0, 0), (0,...  112 us
    broadcast_in_dim x10, local copies, waits for them, and re-layouts, local_conv(): extended[None]  83.8 us
    conv_general_dilated x3, matrix products, local_conv(): lax.conv_general_dilated(extended[None], kernel, (2, 2, 2), [(0, 0), (0,...  38.1 us
    ppermute x10, starting transfers between devices, passed_along(): return lax.ppermute(x, axis, pairs)  33.9 us
    all_to_all x2, blocking collectives, gathered(): lax.all_to_all(jnp.broadcast_to(x[None], (count,) + x.shape), axes, 0, 0)  31 us
    conv_general_dilated x10, local copies, waits for them, and re-layouts, local_conv(): lax.conv_general_dilated(extended[None], kernel, (2, 2, 2), [(0, 0), (0,...  26.9 us
    conv_general_dilated x9, local copies, waits for them, and re-layouts, exact_conv(): lax.conv_general_dilated(extended[None], kernel, (2, 2, 2), [(0, 0), (0,...  24.6 us
    all_to_all x1, starting transfers between devices, gathered(): lax.all_to_all(jnp.broadcast_to(x[None], (count,) + x.shape), axes, 0, 0)  20.4 us
  transfers between devices with their start and end apart: 11, of which 8 were waited for; matrix products, arithmetic and copies ran while one was open for 27% of the time, Pallas kernels for 0%

profile of v1, /device:TPU:32, one launch (start us, length us, event | category | flops | bytes accessed | tf_op | source)
XLA Modules:
  0.0 502.0 jit_solution(14001129157800490382)
XLA Ops:
  18.9 10.7 %copy.183 = bf16[4,9,17,1,8,66]{4,0,5,2,1,3:T(4,128)(2,1)} copy(bf16[4,9,17,1,8,66]{5,4,2,1,0,3:T(8,128)(2,1)S(1)} %reshape.275) | data formatting | bytes 1292544 | tf_op jit(solution)/shard_map/conv_general_dilated | solution.py:68
  30.9 32.8 %fusion.3 = f32[4,8,8,33,16]{4,2,3,1,0:T(8,128)} fusion(bf16[16,4,3,3,3]{0,1,4,3,2:T(4,128)(2,1)S(1)} %copy-done.18, bf16[4,9,17,1,7,2]{4,0,5,2,1,3:T(4,128)(2,1)S(1)} %slice.112, bf16[4,9,17,1,8,66]{4,0,5,2,1,3:T(4,128)(2,1)} %copy.183), kind=kOutput, calls=%fused_computation.4 | convolution fusion | flops 31193856 | bytes 1207536 | tf_op jit(solution)/shard_map/conv_general_dilated | solution.py:68
  63.6 4.4 copy.184
  80.8 4.3 collective-permute-start.2
  100.2 4.6 multiply_divide_fusion.1
  106.8 4.9 collective-permute-start.4
  114.9 4.1 collective-permute-start.5
  124.4 68.1 %copy.218 = bf16[1,4,9,17,513]{1,0,4,3,2:T(2,128)(2,1)} copy(bf16[1,4,9,17,513]{4,3,2,1,0:T(8,128)(2,1)S(1)} %get-tuple-element.33) | data formatting | bytes 1255824 | tf_op jit(solution)/shard_map/broadcast_in_dim | solution.py:69
  193.6 11.9 %copy.208 = bf16[1,16,5,9,257]{1,0,4,3,2:T(2,128)(2,1)} copy(bf16[1,16,5,9,257]{4,1,3,2,0:T(8,128)(2,1)S(1)} %copy-done.5) | data formatting | bytes 740160 | tf_op jit(solution)/shard_map/broadcast_in_dim | solution.py:69
  212.3 20.4 %all-to-all-start = ((f32[128,1,64]{2,1,0:T(1,128)}), f32[128,1,64]{2,1,0:T(1,128)S(1)}, u32[]{:S(2)}, u32[]{:S(2)}) async-start(f32[128,1,64]{2,1,0:T(1,128)} %broadcast_in_dim.19), calls=%async_computation | async-start | bytes 131072 | tf_op jit(solution)/shard_map/all_to_all | solution.py:35
  234.6 9.4 %all-to-all-done = f32[128,1,64]{2,1,0:T(1,128)S(1)} async-done(((f32[128,1,64]{2,1,0:T(1,128)}), f32[128,1,64]{2,1,0:T(1,128)S(1)}, u32[]{:S(2)}, u32[]{:S(2)}) %all-to-all-start) | async-done | bytes 32800 | tf_op jit(solution)/shard_map/all_to_all | solution.py:35
  255.0 4.1 collective-permute-done.7
  259.6 7.4 %broadcast_select_fusion = f32[5,9,8,34,16]{4,2,3,1,0:T(8,128)} fusion(pred[8,34]{0,1:T(8,128)(4,1)S(1)} %copy-done.14, bf16[32,16,3,3,3]{0,1,4,3,2:T(8,128)(2,1)S(1)} %copy-done.13, bf16[32,2,4,1,7,1]{0,4,5,2,1,3:T(8,128)(2,1)S(1)} %slice.134, bf16[32,2,4,1,8,17]{0,4,5,2,1,3:T(8,128)(2,1)S(1)} %copy.214), kind=kOutput, calls=%fused_computation.11 | convolution fusion | flops 30498048 | bytes 884496 | tf_op jit(solution)/shard_map/transpose(jvp())/conv_general_dilated | solution.py:79
  267.0 5.0 copy.215
  279.9 12.2 %copy.204 = f32[64,32,3,3,3,1]{4,3,2,1,0,5:T(4,128)} copy(f32[64,32,3,3,3,1]{0,1,4,5,3,2:T(8,128)S(1)} %copy-done.11) | data formatting | bytes 442368 | tf_op jit(solution)/shard_map/transpose(jvp())/conv_general_dilated | solution.py:79
  292.1 11.0 %reshape.157 = f32[55296]{0:T(1024)} reshape(f32[64,32,3,3,3,1]{4,3,2,1,0,5:T(4,128)} %copy.204) | data formatting | bytes 442368 | tf_op jit(solution)/shard_map/reshape | solution.py:47
  305.9 13.7 %fusion.113 = f32[32,16,3,3,3]{0,1,4,3,2:T(8,128)S(1)} fusion(bf16[1,16,5,9,257]{1,0,4,3,2:T(2,128)(2,1)} %copy.208, bf16[1,32,2,4,128]{1,0,4,3,2:T(2,128)(2,1)S(1)} %copy.209), kind=kOutput, calls=%fused_computation.158 | convolution fusion | flops 28311552 | bytes 490912 | tf_op jit(solution)/shard_map/transpose(jvp())/conv_general_dilated | solution.py:79
  326.8 7.3 %copy.219 = bf16[1,16,4,8,256]{1,0,4,3,2:T(2,128)(2,1)} copy(bf16[1,16,4,8,256]{4,1,3,2,0:T(8,128)(2,1)S(1)} %fusion.67) | data formatting | bytes 524288 | tf_op jit(solution)/shard_map/transpose(jvp())/broadcast_in_dim | solution.py:79
  334.1 87.2 %fusion.114 = f32[16,4,3,3,3]{0,1,4,3,2:T(4,128)S(1)} fusion(bf16[1,4,9,17,513]{1,0,4,3,2:T(2,128)(2,1)} %copy.218, bf16[1,16,4,8,256]{1,0,4,3,2:T(2,128)(2,1)} %copy.219), kind=kOutput, calls=%fused_computation.159 | convolution fusion | flops 28311552 | bytes 896968 | tf_op jit(solution)/shard_map/transpose(jvp())/conv_general_dilated | solution.py:79
  423.1 15.3 %all_to_all.21 = f32[16,40,128]{2,1,0:T(8,128)S(1)} all-to-all(f32[16,40,128]{2,1,0:T(8,128)S(1)} %bitcast.165), channel_id=1, replica_groups=mesh['batch'=2,'gz'=8,'gy'=16] {'gy'}, dimensions={0} | all-to-all | bytes 655360 | tf_op jit(solution)/shard_map/all_to_all | solution.py:49
  438.5 18.4 %all_to_all.22 = f32[16,40,128]{2,1,0:T(8,128)S(1)} all-to-all(f32[16,40,128]{2,1,0:T(8,128)S(1)} %broadcast_in_dim.22), channel_id=1, replica_groups=mesh['batch'=2,'gz'=8,'gy'=16] {'batch','gz'}, dimensions={0} | all-to-all | bytes 655360 | tf_op jit(solution)/shard_map/all_to_all | solution.py:35
  457.0 12.6 %all_to_all.23 = f32[16,40,128]{2,1,0:T(8,128)S(1)} all-to-all(f32[16,40,128]{2,1,0:T(8,128)S(1)} %broadcast_in_dim.23), channel_id=1, replica_groups=mesh['batch'=2,'gz'=8,'gy'=16] {'gy'}, dimensions={0} | all-to-all | bytes 655360 | tf_op jit(solution)/shard_map/all_to_all | solution.py:35
  481.5 8.3 %div.87 = f32[64,32,3,3,3]{4,3,2,1,0:T(4,128)} reshape(f32[55296]{0:T(1024)S(1)} %slice_divide_fusion) | data formatting | bytes 442368 | tf_op jit(solution)/shard_map/div | solution.py:30
  489.8 11.7 %copy.223 = f32[64,32,3,3,3]{0,1,4,3,2:T(8,128)} copy(f32[64,32,3,3,3]{4,3,2,1,0:T(4,128)} %div.87) | data formatting | bytes 442368
  (161 shorter events, 107.1 us)
Async XLA Ops:
  0.6 210.1 %copy-start = (bf16[64,32,3,3,3]{0,1,4,3,2:T(8,128)(2,1)S(1)}, bf16[64,32,3,3,3]{0,1,4,3,2:T(8,128)(2,1)}, u32[]{:S(2)}) copy-start(bf16[64,32,3,3,3]{0,1,4,3,2:T(8,128)(2,1)} %param.9) | copy-start | bytes 331780
  2.1 5.4 %collective-permute-start = (bf16[4,8,1,512]{3,2,1,0:T(2,128)(2,1)S(1)}, bf16[4,8,1,512]{3,2,1,0:T(2,128)(2,1)S(1)}, u32[]{:S(2)}, u32[]{:S(2)}) collective-permute-start(bf16[4,8,1,512]{3,2,1,0:T(2,128)(2,1)S(1)} %slice.111), channel_id=1, source_target_pairs={{0,1},{1,2},{2,3},{3,4},{4,5},{5,6},{6,7},{7,8},{8,9},{9,10},{10,1... | collective-permute-start | bytes 98312 | tf_op jit(solution)/shard_map/ppermute | solution.py:14
  7.5 6.5 %collective-permute-start.1 = (bf16[4,1,17,512]{3,2,1,0:T(8,128)(2,1)S(1)}, bf16[4,1,17,512]{3,2,1,0:T(8,128)(2,1)S(1)}, u32[]{:S(2)}, u32[]{:S(2)}) collective-permute-start(bf16[4,1,17,512]{3,2,1,0:T(8,128)(2,1)S(1)} %pad_maximum_fusion), channel_id=1, source_target_pairs={{0,16},{16,32},{32,48},{48,64},{64,80},{80,96},{96,112},{1,17},{17... | collective-permute-start | bytes 208904 | tf_op jit(solution)/shard_map/ppermute | solution.py:14
  18.9 11.9 %copy-start.18 = (bf16[16,4,3,3,3]{0,1,4,3,2:T(4,128)(2,1)S(1)}, bf16[16,4,3,3,3]{0,1,4,3,2:T(4,128)(2,1)}, u32[]{:S(2)}) copy-start(bf16[16,4,3,3,3]{0,1,4,3,2:T(4,128)(2,1)} %param.7) | copy-start | bytes 10372
  80.8 5.9 %collective-permute-start.2 = (bf16[16,4,1,256]{3,0,2,1:T(8,128)(2,1)S(1)}, bf16[16,4,1,256]{3,0,2,1:T(8,128)(2,1)S(1)}, u32[]{:S(2)}, u32[]{:S(2)}) collective-permute-start(bf16[16,4,1,256]{3,0,2,1:T(8,128)(2,1)S(1)} %slice.115), channel_id=1, source_target_pairs={{0,1},{1,2},{2,3},{3,4},{4,5},{5,6},{6,7},{7,8},{8,9},{9,10},{10,1... | collective-permute-start | bytes 98312 | tf_op jit(solution)/shard_map/ppermute | solution.py:14
  86.7 6.2 %collective-permute-start.3 = (bf16[16,1,9,256]{3,0,2,1:T(8,128)(2,1)S(1)}, bf16[16,1,9,256]{3,0,2,1:T(8,128)(2,1)S(1)}, u32[]{:S(2)}, u32[]{:S(2)}) collective-permute-start(bf16[16,1,9,256]{3,0,2,1:T(8,128)(2,1)S(1)} %pad_maximum_fusion.1), channel_id=1, source_target_pairs={{0,16},{16,32},{32,48},{48,64},{64,80},{80,96},{96,112},{1,17},{17... | collective-permute-start | bytes 221192 | tf_op jit(solution)/shard_map/ppermute | solution.py:14
  95.3 4.9 copy-start.12
  104.8 14.2 %copy-start.2 = (f32[4,8,8,33,16]{3,4,2,1,0:T(8,128)S(1)}, f32[4,8,8,33,16]{3,4,2,1,0:T(8,128)}, u32[]{:S(2)}) copy-start(f32[4,8,8,33,16]{3,4,2,1,0:T(8,128)} %get-tuple-element.30) | copy-start | bytes 1622020
  106.8 7.0 %collective-permute-start.4 = (bf16[32,2,1,128]{0,2,3,1:T(2,128)(2,1)}, bf16[32,2,1,128]{0,2,3,1:T(2,128)(2,1)}, u32[]{:S(2)}, u32[]{:S(2)}) collective-permute-start(bf16[32,2,1,128]{0,2,3,1:T(2,128)(2,1)} %slice.119), channel_id=1, source_target_pairs={{0,1},{1,2},{2,3},{3,4},{4,5},{5,6},{6,7},{7,8},{8,9},{9,10},{10,1... | collective-permute-start | bytes 49160 | tf_op jit(solution)/shard_map/ppermute | solution.py:14
  114.9 90.6 %collective-permute-start.5 = (bf16[32,1,5,128]{3,0,2,1:T(8,128)(2,1)S(1)}, bf16[32,1,5,128]{3,0,2,1:T(8,128)(2,1)}, u32[]{:S(2)}, u32[]{:S(2)}) collective-permute-start(bf16[32,1,5,128]{3,0,2,1:T(8,128)(2,1)S(1)} %pad_maximum_fusion.2), channel_id=1, source_target_pairs={{0,16},{16,32},{32,48},{48,64},{64,80},{80,96},{96,112},{1,17},{17... | collective-permute-start | bytes 122888 | tf_op jit(solution)/shard_map/ppermute | solution.py:14
  124.4 68.1 %copy-start.9 = (f32[2,4,8,17,32]{4,2,3,1,0:T(8,128)S(1)}, f32[2,4,8,17,32]{4,2,3,1,0:T(8,128)}, u32[]{:S(2)}) copy-start(f32[2,4,8,17,32]{4,2,3,1,0:T(8,128)} %get-tuple-element.35) | copy-start | bytes 417796
  211.5 32.7 %copy-start.19 = (f32[4,64]{1,0:T(4,128)S(1)}, f32[4,64]{1,0:T(4,128)}, u32[]{:S(2)}) copy-start(f32[4,64]{1,0:T(4,128)} %param.10) | copy-start | bytes 3076
  211.5 32.7 %copy-start.20 = (f32[1,4]{1,0:T(1,128)S(1)}, f32[1,4]{1,0:T(1,128)}, u32[]{:S(2)}) copy-start(f32[1,4]{1,0:T(1,128)} %param.11) | copy-start | bytes 52
  212.3 31.7 %all-to-all-start = ((f32[128,1,64]{2,1,0:T(1,128)}), f32[128,1,64]{2,1,0:T(1,128)S(1)}, u32[]{:S(2)}, u32[]{:S(2)}) async-start(f32[128,1,64]{2,1,0:T(1,128)} %broadcast_in_dim.19), calls=%async_computation | async-start | bytes 131072 | tf_op jit(solution)/shard_map/all_to_all | solution.py:35
  247.5 5.9 %collective-permute-start.6 = (bf16[32,1,5,128]{3,0,2,1:T(8,128)(2,1)S(1)}, bf16[32,1,5,128]{3,0,2,1:T(8,128)(2,1)S(1)}, u32[]{:S(2)}, u32[]{:S(2)}) collective-permute-start(bf16[32,1,5,128]{3,0,2,1:T(8,128)(2,1)S(1)} %slice.212), channel_id=1, source_target_pairs={{16,0},{32,16},{48,32},{64,48},{80,64},{96,80},{112,96},{17,1},{33... | collective-permute-start | bytes 122888 | tf_op jit(solution)/shard_map/ppermute | solution.py:14
  253.3 6.3 %copy-start.13 = (bf16[32,16,3,3,3]{0,1,4,3,2:T(8,128)(2,1)S(1)}, bf16[32,16,3,3,3]{0,1,4,3,2:T(8,128)(2,1)}, u32[]{:S(2)}) copy-start(bf16[32,16,3,3,3]{0,1,4,3,2:T(8,128)(2,1)} %param.8) | copy-start | bytes 82948
  253.3 6.3 %copy-start.14 = (pred[8,34]{0,1:T(8,128)(4,1)S(1)}, pred[8,34]{0,1:T(8,128)(4,1)}, u32[]{:S(2)}) copy-start(pred[8,34]{0,1:T(8,128)(4,1)} %constant.101) | copy-start | bytes 820
  253.5 5.6 %collective-permute-start.7 = (bf16[32,2,1,128]{3,0,2,1:T(8,128)(2,1)S(1)}, bf16[32,2,1,128]{3,0,2,1:T(8,128)(2,1)S(1)}, u32[]{:S(2)}, u32[]{:S(2)}) collective-permute-start(bf16[32,2,1,128]{3,0,2,1:T(8,128)(2,1)S(1)} %slice.214), channel_id=1, source_target_pairs={{1,0},{2,1},{3,2},{4,3},{5,4},{6,5},{7,6},{8,7},{9,8},{10,9},{11,1... | collective-permute-start | bytes 49160 | tf_op jit(solution)/shard_map/ppermute | solution.py:14
  273.8 6.1 %copy-start.11 = (f32[64,32,3,3,3,1]{0,1,4,5,3,2:T(8,128)S(1)}, f32[64,32,3,3,3,1]{0,1,4,5,3,2:T(8,128)}, u32[]{:S(2)}) copy-start(f32[64,32,3,3,3,1]{0,1,4,5,3,2:T(8,128)} %fusion.16) | copy-start | bytes 663556
  275.2 28.2 %collective-permute-start.8 = (bf16[16,1,9,256]{3,0,2,1:T(8,128)(2,1)S(1)}, bf16[16,1,9,256]{3,0,2,1:T(8,128)(2,1)S(1)}, u32[]{:S(2)}, u32[]{:S(2)}) collective-permute-start(bf16[16,1,9,256]{3,0,2,1:T(8,128)(2,1)S(1)} %slice.211), channel_id=1, source_target_pairs={{16,0},{32,16},{48,32},{64,48},{80,64},{96,80},{112,96},{17,1},{33... | collective-permute-start | bytes 221192 | tf_op jit(solution)/shard_map/ppermute | solution.py:14
  304.4 21.0 %collective-permute-start.9 = (bf16[16,4,1,256]{3,0,2,1:T(8,128)(2,1)S(1)}, bf16[16,4,1,256]{3,0,2,1:T(8,128)(2,1)S(1)}, u32[]{:S(2)}, u32[]{:S(2)}) collective-permute-start(bf16[16,4,1,256]{3,0,2,1:T(8,128)(2,1)S(1)} %slice.213), channel_id=1, source_target_pairs={{1,0},{2,1},{3,2},{4,3},{5,4},{6,5},{7,6},{8,7},{9,8},{10,9},{11,1... | collective-permute-start | bytes 98312 | tf_op jit(solution)/shard_map/ppermute | solution.py:14
  334.1 87.8 %copy-start.8 = (f32[55296]{0:T(1024)S(1)}, f32[55296]{0:T(1024)}, u32[]{:S(2)}) copy-start(f32[55296]{0:T(1024)} %reshape.157) | copy-start | bytes 663556
  334.1 87.8 %copy-start.15 = (f32[256]{0:T(256)S(1)}, f32[256]{0:T(256)}, u32[]{:S(2)}) copy-start(f32[256]{0:T(256)} %mul.162) | copy-start | bytes 3076
  489.8 11.7 %copy-start.1 = (bf16[64,32,3,3,3]{0,1,4,3,2:T(8,128)(2,1)S(1)}, bf16[64,32,3,3,3]{0,1,4,3,2:T(8,128)(2,1)}, u32[]{:S(2)}) copy-start(bf16[64,32,3,3,3]{0,1,4,3,2:T(8,128)(2,1)} %param.9) | copy-start | bytes 331780
  (9 other events, 23.7 us)

commit v2 on v0

v2 whole, which is shorter than its diff:
```python
import functools
import jax
import jax.numpy as jnp
from jax import lax
from jax.experimental import pallas as pl
from jax.experimental.pallas import tpu as pltpu
from jax.sharding import PartitionSpec as P

epsilon = 1e-06
f32 = jnp.float32
bf16 = jnp.bfloat16
LANES = 128
HALF = 64
G3, G2, G1, GH, GL, ROWS = 0, 448, 560, 592, 600, 640


def call(body, outs, args, scratch=()):
    return pl.pallas_call(
        body,
        out_shape=[jax.ShapeDtypeStruct(s, d) for s, d in outs],
        in_specs=[pl.BlockSpec(memory_space=pltpu.VMEM)] * len(args),
        out_specs=[pl.BlockSpec(memory_space=pltpu.VMEM)] * len(outs),
        scratch_shapes=[pltpu.VMEM(s, d) for s, d in scratch],
        compiler_params=pltpu.CompilerParams(vmem_limit_bytes=48 * 1024 * 1024),
    )(*args)


def lane_of(shape):
    return lax.broadcasted_iota(jnp.int32, shape, len(shape) - 1)


def dot(a, b):
    return lax.dot_general(a, b, (((1,), (0,)), ((), ())), preferred_element_type=f32)


def dot_nt(a, b):
    return lax.dot_general(a, b, (((1,), (1,)), ((), ())), preferred_element_type=f32)


def from_below(own, received):
    mixed = jnp.where(lane_of(own.shape) >= HALF, received.astype(f32), own.astype(f32))
    return pltpu.roll(mixed, HALF, 1)


def from_above(own, received):
    mixed = jnp.where(lane_of(own.shape) < HALF, received.astype(f32), own.astype(f32))
    return pltpu.roll(mixed, HALF, 1)


def x_before(rows):
    return jnp.where(lane_of(rows.shape) % HALF == 0, 0.0, pltpu.roll(rows, 1, 1))


def x_after(rows):
    return jnp.where(lane_of(rows.shape) % HALF == HALF - 1, 0.0, pltpu.roll(rows, LANES - 1, 1))


def at(group):
    return slice(group * LANES, (group + 1) * LANES)


def arrange_body(vol, a0, row, plane, corner, rows):
    for z in range(8):
        tops = [c * 128 + z * 16 + yb * 8 for yb in range(2) for c in range(4)]
        cube = jnp.stack([vol[top : top + 8, :] for top in tops], axis=0)
        rows[z * 64 : z * 64 + 64, :] = jnp.transpose(cube, (1, 0, 2)).reshape(64, 512)
    x_at = lax.broadcasted_iota(jnp.int32, (512, 512), 0)
    to = lax.broadcasted_iota(jnp.int32, (512, 512), 1)
    move = jnp.where(x_at == (to % HALF) * 8 + to // HALF, 1.0, 0.0).astype(bf16)
    phased = dot(rows[...].astype(bf16), move)
    parts = []
    for j in range(4):
        part = phased[:, at(j)].reshape(64, 8, LANES)
        turned = pltpu.roll(pltpu.roll(part, 4, 1), HALF, 2)
        sub = lax.broadcasted_iota(jnp.int32, part.shape, 1)
        parts.append(jnp.where((sub < 4) == (lane_of(part.shape) < HALF), part, turned))
    whole = jnp.concatenate(parts, axis=1).astype(bf16)
    a0[...] = whole.reshape(8, 8, 32, LANES)
    for z in range(8):
        row[z] = a0[z, 7]
    plane[...] = a0[7]
    corner[...] = a0[7, 7]


def weights_body(w1, w2, w3, t1, t2, t3, tt2, tt3):
    eye = jnp.where(
        lax.broadcasted_iota(jnp.int32, (HALF, LANES), 0) == lane_of((HALF, LANES)), 1.0, 0.0
    ).astype(bf16)
    blocks = []
    for ab in range(9):
        both, low = w1[ab, 0], w1[ab, 1]
        for m in range(4):
            block = pltpu.roll(both, 16 * m, 1) if m else both
            if m < 3:
                block = block + pltpu.roll(low, 16 * (m + 1), 1)
            blocks.append(block)
        blocks += [jnp.zeros_like(low), low]
    t1[...] = dot_nt(eye, jnp.concatenate(blocks, axis=0).astype(bf16)).astype(bf16)
    blocks = []
    for ab in range(9):
        e0, e1, e2 = w2[3 * ab], w2[3 * ab + 1], w2[3 * ab + 2]
        blocks += [e1, e2 + pltpu.roll(e0, 32, 1), pltpu.roll(e1, 32, 1), pltpu.roll(e2, 32, 1), e0]
    tt2[...] = jnp.concatenate(blocks, axis=0).astype(bf16)
    t2[...] = dot_nt(eye, tt2[...]).astype(bf16)
    blocks = []
    for ab in range(9):
        blocks += [w3[3 * ab + 1], w3[3 * ab + 2], w3[3 * ab]]
    tt3[...] = jnp.concatenate(blocks, axis=0).astype(bf16)
    t3[...] = dot_nt(eye, tt3[...]).astype(bf16)


def fill_patches(tile, n, rows, moved, out):
    step, groups = rows + moved, n // 2
    for zz in range(-1, n):
        for yy in range(-1, n):
            cell = tile(zz, yy)
            shifted = x_before(cell[rows - moved :].astype(f32)).astype(bf16)
            for a in range(3):
                for b in range(3):
                    i, j = zz + 1 - a, yy + 1 - b
                    if i % 2 or j % 2 or not (0 <= i < n and 0 <= j < n):
                        continue
                    top = (a * 3 + b) * step
                    g = at((i // 2) * groups + j // 2)
                    out[top : top + rows, g] = cell
                    out[top + rows : top + step, g] = shifted


def finish(pre):
    root = jnp.sqrt(pre * pre + 1.0)
    return 0.65 * pre + 0.35 * (root - 1.0), 0.65 + 0.35 * pre / root


def one_body(a0, row, plane, corner, t1, p1, a1, slope, row_out, plane_out, corner_out):
    def tile(zz, yy):
        own = a0[zz, yy if yy >= 0 else 7] if zz >= 0 else plane[yy if yy >= 0 else 7]
        if yy >= 0:
            return own
        return from_below(own, row[zz] if zz >= 0 else corner[...]).astype(bf16)

    fill_patches(tile, 8, 32, 16, p1)
    act, slope[...] = finish(dot(t1[...], p1[...]))
    a1[...] = act.astype(bf16)
    for z in range(4):
        row_out[:, at(z)] = a1[:, at(z * 4 + 3)]
    plane_out[...] = a1[:, 12 * LANES :]
    corner_out[...] = a1[:, at(15)]


def two_body(a1, row, plane, corner, t2, p2, a2, slope, row_out, plane_out, corner_out):
    def tile(zz, yy):
        y_own = yy if yy >= 0 else 3
        own = a1[:, at(zz * 4 + y_own)] if zz >= 0 else plane[:, at(y_own)]
        if yy >= 0:
            return own
        return from_below(own, row[:, at(zz)] if zz >= 0 else corner[...]).astype(bf16)

    fill_patches(tile, 4, 64, 16, p2)
    act, slope[...] = finish(dot(t2[...], p2[...]))
    a2[...] = act.astype(bf16)
    for z in range(2):
        row_out[:, at(z)] = a2[:, at(z * 2 + 1)]
    plane_out[...] = a2[:, 2 * LANES :]
    corner_out[...] = a2[:, at(3)]


def three_body(a2, row, plane, corner, t3, slope2, p3, slope, sums, to_z, to_y, to_corner):
    def tile(zz, yy):
        y_own = yy if yy >= 0 else 1
        own = a2[:, at(zz * 2 + y_own)] if zz >= 0 else plane[:, at(y_own)]
        if yy >= 0:
            return own
        return from_below(own, row[:, at(zz)] if zz >= 0 else corner[...]).astype(bf16)

    fill_patches(tile, 2, 64, 32, p3)
    act, slope3 = finish(dot(t3[...], p3[...]))
    slope[...] = slope3
    column = jnp.sum(act.astype(bf16).astype(f32), axis=1, keepdims=True)
    spot = lax.broadcasted_iota(jnp.int32, (HALF, LANES), 0) == lane_of((HALF, LANES))
    line = jnp.sum(jnp.where(spot, column, 0.0), axis=0, keepdims=True)
    sums[...] = jnp.broadcast_to(line, sums.shape)
    third = slope3.astype(bf16)
    second = slope2[...].astype(bf16)
    to_z[:, : 2 * LANES] = second[:, : 2 * LANES]
    to_z[:, 2 * LANES :] = third
    to_y[:, at(0)] = second[:, at(0)]
    to_y[:, at(1)] = second[:, at(2)]
    to_y[:, at(2)] = third
    to_corner[:, at(0)] = second[:, at(0)]
    to_corner[:, at(1)] = third


def reach(index):
    return [(1, index // 2)] if index % 2 == 0 else [(2, index // 2), (0, index // 2 + 1)]


def back_cell(terms, z, y, step, rows, place):
    total = None
    for a, i in reach(z):
        for b, j in reach(y):
            top = (a * 3 + b) * step
            part = terms[top : top + step, at(place(i, j))]
            total = part if total is None else total + part
    moved = step - rows
    low = total[rows - moved : rows] + x_after(total[rows:])
    return jnp.concatenate([total[: rows - moved], low], axis=0)


def backward_body(cells, share, gathered, head, targets, s1, s2, s3, of_z, of_y, of_corner,
                  p1, p2, p3, tt2, tt3, out, err3, err2, err1, terms3, terms2):
    out[...] = jnp.zeros_like(out)
    pooled = jnp.sum(gathered[...], axis=0, keepdims=True)[:, :HALF] / cells
    errors = jnp.sum(head[...] * pooled, axis=1, keepdims=True) - targets[...]
    out[GH : GH + 4, :HALF] = errors * pooled * share
    loss = 0.5 * jnp.sum(errors * errors, axis=0, keepdims=True) * share
    out[GL : GL + 1, :] = jnp.broadcast_to(loss, (1, LANES))
    line = jnp.sum(errors * head[...], axis=0, keepdims=True) / cells
    spot = lax.broadcasted_iota(jnp.int32, (HALF, HALF), 0) == lane_of((HALF, HALF))
    back_pool = jnp.sum(jnp.where(spot, line, 0.0), axis=1, keepdims=True)

    third, third_z = s3[...], of_z[:, at(2)].astype(f32)
    slopes3 = [third, from_above(third, of_y[:, at(2)]),
               third_z, from_above(third_z, of_corner[:, at(1)])]
    for k in range(4):
        err3[:HALF, at(k)] = (back_pool * slopes3[k]).astype(bf16)
    err3[HALF:, :] = jnp.zeros((HALF, 4 * LANES), bf16)
    err2[HALF:, :] = jnp.zeros((HALF, 9 * LANES), bf16)
    err1[HALF:, :] = jnp.zeros((HALF, 16 * LANES), bf16)

    terms3[...] = dot(tt3[...], err3[...])
    order = [(0, 0), (0, 1), (1, 0), (1, 1), (0, 2), (1, 2), (2, 0), (2, 1), (2, 2)]
    for k, (z, y) in enumerate(order):
        if z < 2:
            own = s2[:, at(z * 2 + (y if y < 2 else 0))]
            slope = own if y < 2 else from_above(own, of_y[:, at(z)])
        else:
            own = of_z[:, at(y if y < 2 else 0)].astype(f32)
            slope = own if y < 2 else from_above(own, of_corner[:, at(0)])
        back = back_cell(terms3, z, y, 96, 64, lambda i, j: i * 2 + j)
        err2[:HALF, at(k)] = (back * slope).astype(bf16)

    terms2[...] = dot(tt2[...], err2[...])
    for z in range(4):
        for y in range(4):
            back = back_cell(terms2, z, y, 80, 64, lambda i, j: order.index((i, j)))
            k = at(z * 4 + y)
            err1[:HALF, k] = (back * s1[:, k]).astype(bf16)

    grad = dot_nt(p3[...], err3[:, at(0)])
    taps = [96 * ab + 32 * ((e + 2) % 3) for ab in range(9) for e in range(3)]
    for k, top in enumerate(taps[:14]):
        block = grad[top : top + 32]
        if k + 14 < 27:
            other = taps[k + 14]
            block = block + pltpu.roll(grad[other : other + 32], HALF, 1)
        out[G3 + 32 * k : G3 + 32 * k + 32, :] = block

    grad = dot_nt(p2[...], err2[:, : 4 * LANES])
    blocks = []
    for ab in range(9):
        x = [grad[80 * ab + 16 * i : 80 * ab + 16 * i + 16] for i in range(5)]
        for first, second in ((4, 1), (0, 2), (1, 3)):
            block = x[first] + pltpu.roll(x[second], LANES - 32, 1)
            blocks.append(jnp.where(lane_of(block.shape) < 32, block, 0.0))
    for k in range(7):
        block = blocks[k]
        for m in range(1, 4):
            if k + 7 * m < 27:
                block = block + pltpu.roll(blocks[k + 7 * m], 32 * m, 1)
        out[G2 + 16 * k : G2 + 16 * k + 16, :] = block

    grad = dot_nt(p1[...], err1[...])
    blocks = []
    for ab in range(9):
        x = [grad[48 * ab + 8 * i : 48 * ab + 8 * i + 8] for i in range(6)]
        both, low = x[0], x[5]
        for m in range(1, 4):
            both = both + pltpu.roll(x[m], LANES - 16 * m, 1)
            low = low + pltpu.roll(x[m - 1], LANES - 16 * m, 1)
        low = jnp.where(lax.broadcasted_iota(jnp.int32, low.shape, 0) >= 4, low, 0.0)
        block = jnp.concatenate([both, low], axis=0)
        blocks.append(jnp.where(lane_of(block.shape) < 16, block, 0.0))
    block = blocks[0]
    for m in range(1, 8):
        block = block + pltpu.roll(blocks[m], 16 * m, 1)
    out[G1 : G1 + 16, :] = block
    out[G1 + 16 : G1 + 32, :] = blocks[8]


def update_body(total, u1, u2, u3, uh, loss):
    def scale(start, stop, count):
        squares = total[start:stop] * total[start:stop]
        mean = jnp.sum(jnp.sum(squares, axis=0, keepdims=True), axis=1, keepdims=True) / count
        return 1.0 / jnp.sqrt(mean + epsilon)

    factor = scale(G3, G2, 64 * 32 * 27)
    for k in range(14):
        block = total[G3 + 32 * k : G3 + 32 * k + 32] * factor
        u3[k] = block[:, :HALF]
        if k + 14 < 27:
            u3[k + 14] = pltpu.roll(block, HALF, 1)[:, :HALF]
    factor = scale(G2, G1, 32 * 16 * 27)
    for k in range(7):
        block = total[G2 + 16 * k : G2 + 16 * k + 16] * factor
        for m in range(4):
            if k + 7 * m < 27:
                u2[k + 7 * m] = (pltpu.roll(block, LANES - 32 * m, 1) if m else block)[:, :32]
    factor = scale(G1, GH, 16 * 4 * 27)
    for ab in range(9):
        m = ab % 8
        block = total[G1 + 16 * (ab // 8) : G1 + 16 * (ab // 8) + 16] * factor
        block = (pltpu.roll(block, LANES - 16 * m, 1) if m else block)[:, :16]
        u1[3 * ab] = block[12:16]
        u1[3 * ab + 1] = block[0:4]
        u1[3 * ab + 2] = block[4:8]
    uh[...] = total[GH : GH + 4, :HALF] * scale(GH, GL, 4 * 64)
    loss[...] = total[GL : GL + 1, :]


def neighbours(by):
    gz, gy = lax.axis_size("gz"), lax.axis_size("gy")
    z = [(i, i + by) for i in range(gz) if 0 <= i + by < gz]
    y = [(i, i + by) for i in range(gy) if 0 <= i + by < gy]
    corner = [(i * gy + j, k * gy + l) for i, k in z for j, l in y]
    return y, z, corner


def exchange(row, plane, corner, by):
    y, z, both = neighbours(by)
    return (lax.ppermute(row, "gy", y), lax.ppermute(plane, "gz", z),
            lax.ppermute(corner, ("gz", "gy"), both))


def gathered(x, axes):
    count = lax.axis_size(axes)
    return lax.all_to_all(jnp.broadcast_to(x[None], (count,) + x.shape), axes, 0, 0)


def summed_over_all(flat):
    columns = lax.axis_size("gy")
    flat = flat.reshape(columns, ROWS // columns, LANES)
    own = jnp.sum(lax.all_to_all(flat, "gy", 0, 0), axis=0)
    own = lax.psum(own, "batch")
    own = jnp.sum(gathered(own, "gz"), axis=0)
    return gathered(own, "gy").reshape(ROWS, LANES)


def local(volume, conv_one, conv_two, conv_three, head_weight, targets):
    devices = lax.axis_size("gz") * lax.axis_size("gy")
    cells = float(devices * LANES)

    def taps(w):
        w = jnp.transpose(w, (2, 3, 4, 1, 0)).astype(f32)
        return jnp.pad(w.reshape((27,) + w.shape[3:]), ((0, 0), (0, 0), (0, LANES - w.shape[4])))

    w1 = taps(conv_one).reshape(9, 3, 4, LANES)
    both = w1[:, 1:].reshape(9, 1, 8, LANES)
    low = jnp.pad(w1[:, :1], ((0, 0), (0, 0), (4, 0), (0, 0)))
    t1, t2, t3, tt2, tt3 = call(
        weights_body,
        [((64, 432), bf16), ((64, 720), bf16), ((64, 864), bf16), ((720, LANES), bf16), ((864, LANES), bf16)],
        (jnp.concatenate([both, low], axis=1), taps(conv_two), taps(conv_three)),
    )
    a0, row, plane, corner = call(
        arrange_body,
        [((8, 8, 32, LANES), bf16), ((8, 32, LANES), bf16), ((8, 32, LANES), bf16), ((32, LANES), bf16)],
        (volume.reshape(512, 512),),
        [((512, 512), f32)],
    )
    row, plane, corner = exchange(row, plane, corner, 1)
    p1, a1, s1, row, plane, corner = call(
        one_body,
        [((432, 2048), bf16), ((64, 2048), bf16), ((64, 2048), f32),
         ((64, 512), bf16), ((64, 512), bf16), ((64, LANES), bf16)],
        (a0, row, plane, corner, t1),
    )
    row, plane, corner = exchange(row, plane, corner, 1)
    p2, a2, s2, row, plane, corner = call(
        two_body,
        [((720, 512), bf16), ((64, 512), bf16), ((64, 512), f32),
         ((64, 256), bf16), ((64, 256), bf16), ((64, LANES), bf16)],
        (a1, row, plane, corner, t2),
    )
    row, plane, corner = exchange(row, plane, corner, 1)
    p3, s3, sums, to_z, to_y, to_corner = call(
        three_body,
        [((864, LANES), bf16), ((64, LANES), f32), ((devices, LANES), f32),
         ((64, 384), bf16), ((64, 384), bf16), ((64, 256), bf16)],
        (a2, row, plane, corner, t3, s2),
    )
    of_y, of_z, of_corner = exchange(to_y, to_z, to_corner, -1)
    pooled = lax.all_to_all(sums, ("gz", "gy"), 0, 0, tiled=True)
    (flat,) = call(
        functools.partial(backward_body, cells, 1.0 / devices),
        [((ROWS, LANES), f32)],
        (pooled, head_weight, targets.reshape(4, 1), s1, s2, s3, of_z, of_y, of_corner, p1, p2, p3, tt2, tt3),
        [((LANES, 4 * LANES), bf16), ((LANES, 9 * LANES), bf16), ((LANES, 16 * LANES), bf16),
         ((864, 4 * LANES), f32), ((720, 9 * LANES), f32)],
    )
    u1, u2, u3, uh, loss = call(
        update_body,
        [((27, 4, 16), f32), ((27, 16, 32), f32), ((27, 32, 64), f32), ((4, 64), f32), ((1, LANES), f32)],
        (summed_over_all(flat),),
    )

    def kernel_form(u):
        return jnp.transpose(u.reshape((3, 3, 3) + u.shape[1:]), (4, 3, 0, 1, 2))

    return kernel_form(u1), kernel_form(u2), kernel_form(u3), uh, loss[0, 0]


def solution(mesh):
    in_specs = (P("batch", None, "gz", "gy", None), P(), P(), P(), P(), P("batch", None))
    out_specs = (P(), P(), P(), P(), P())
    return jax.shard_map(local, mesh=mesh, in_specs=in_specs, out_specs=out_specs, check_vma=False)
```

time: 1040 us -> 134 us (0.13)
  blocking collectives: 392 us -> 49.6 us
  waiting for transfers between devices: 227 us -> 8.16 us
  matrix products: 149 us -> 0 us
  local copies, waits for them, and re-layouts: 151 us -> 7.91 us
  between operations: 18.6 us -> 0.9 us
  starting transfers between devices: 73 us -> 56.3 us
  other arithmetic: 17.4 us -> 1.95 us
    psum x2 -> x1, blocking collectives: 392 us -> 3.42 us  [summed_over_all(): own = lax.psum(own, 'batch')]
    psum x1 -> x0, waiting for transfers between devices: 212 us -> none  [local(): lax.psum((head_term, grad_three, grad_two, grad_one, loss_term), ('batch'...]
    conv_general_dilated x8 -> x0, matrix products: 149 us -> none  [the longest x5 110 us: exact_conv(): lax.conv_general_dilated(extended[None], kernel, (2, 2, 2), [(0, 0), (0,...]
    broadcast_in_dim x13 -> x2, local copies, waits for them, and re-layouts: 93.5 us -> 0.04 us  [gathered(): jnp.broadcast_to(x[None], (count,) + x.shape)]
    all_to_all x0 -> x3, blocking collectives: none -> 46.2 us  [the longest x2 28.2 us: gathered(): lax.all_to_all(jnp.broadcast_to(x[None], (count,) + x.shape), axes, 0, 0)]
    conv_general_dilated x16 -> x0, local copies, waits for them, and re-layouts: 35.6 us -> none  [the longest x10 27.3 us: local_conv(): lax.conv_general_dilated(extended[None], kernel, (2, 2, 2), [(0, 0), (0,...]
    ppermute x10 -> x12, starting transfers between devices: 72.9 us -> 42 us  [the longest x4 14.7 us: exchange(): lax.ppermute(corner, ('gz', 'gy'), both)]
    all_to_all x0 -> x1, starting transfers between devices: none -> 14.3 us  [local(): pooled = lax.all_to_all(sums, ('gz', 'gy'), 0, 0, tiled=True)]
  transfers between devices with their start and end apart: 11 -> 13, of which waited for: 9 -> 3; matrix products, arithmetic and copies ran while one was open for 12% -> 3% of each run, Pallas kernels for 0% -> 0%
where the time goes in v2:
time: 134 us; the launch traced here: 133 us
  starting transfers between devices  56.3 us (42%)
  blocking collectives  49.6 us (37%)
  waiting for transfers between devices  8.16 us (6%)
  local copies, waits for them, and re-layouts  7.91 us (6%)
  Pallas kernels  7.76 us (6%)
  other arithmetic  1.95 us (1%)
    all_to_all x2, blocking collectives, gathered(): lax.all_to_all(jnp.broadcast_to(x[None], (count,) + x.shape), axes, 0, 0)  28.2 us
    all_to_all x1, blocking collectives, summed_over_all(): own = jnp.sum(lax.all_to_all(flat, 'gy', 0, 0), axis=0)  18 us
    ppermute x4, starting transfers between devices, exchange(): lax.ppermute(corner, ('gz', 'gy'), both)  14.7 us
    ppermute x4, starting transfers between devices, exchange(): lax.ppermute(plane, 'gz', z)  14.6 us
    all_to_all x1, starting transfers between devices, local(): pooled = lax.all_to_all(sums, ('gz', 'gy'), 0, 0, tiled=True)  14.3 us
    ppermute x4, starting transfers between devices, exchange(): lax.ppermute(row, 'gy', y)  12.6 us
    ppermute x4, waiting for transfers between devices, exchange(): lax.ppermute(corner, ('gz', 'gy'), both)  8.14 us
    pallas_call x7, Pallas kernels, call(): pl.pallas_call(body, out_shape=[jax.ShapeDtypeStruct(s, d) for s, d in ou...  7.76 us
  transfers between devices with their start and end apart: 13, of which 3 were waited for; matrix products, arithmetic and copies ran while one was open for 3% of the time, Pallas kernels for 0%

profile of v2, /device:TPU:32, one launch (start us, length us, event | category | flops | bytes accessed | tf_op | source)
XLA Modules:
  0.0 132.6 jit_solution(2511735513070942893)
XLA Ops:
  0.6 1.2 copy-done
  2.4 4.8 %collective-permute-start.2 = (bf16[32,128]{1,0:T(8,128)(2,1)S(1)}, bf16[32,128]{1,0:T(8,128)(2,1)S(1)}, u32[]{:S(2)}, u32[]{:S(2)}) collective-permute-start(bf16[32,128]{1,0:T(8,128)(2,1)S(1)} %get-tuple-element.40), channel_id=1, source_target_pairs={{0,17},{1,18},{2,19},{3,20},{4,21},{5,22},{6,23},{7,24},{8,25},{9,... | collective-permute-start | bytes 24584 | tf_op jit(solution)/shard_map/ppermute | solution.py:331
  7.3 3.5 %collective-permute-start = (bf16[8,32,128]{2,1,0:T(8,128)(2,1)S(1)}, bf16[8,32,128]{2,1,0:T(8,128)(2,1)S(1)}, u32[]{:S(2)}, u32[]{:S(2)}) collective-permute-start(bf16[8,32,128]{2,1,0:T(8,128)(2,1)S(1)} %get-tuple-element.38), channel_id=1, source_target_pairs={{0,1},{1,2},{2,3},{3,4},{4,5},{5,6},{6,7},{7,8},{8,9},{9,10},{10,1... | collective-permute-start | bytes 196616 | tf_op jit(solution)/shard_map/ppermute | solution.py:330
  10.8 3.8 %collective-permute-start.1 = (bf16[8,32,128]{2,1,0:T(8,128)(2,1)S(1)}, bf16[8,32,128]{2,1,0:T(8,128)(2,1)S(1)}, u32[]{:S(2)}, u32[]{:S(2)}) collective-permute-start(bf16[8,32,128]{2,1,0:T(8,128)(2,1)S(1)} %get-tuple-element.39), channel_id=1, source_target_pairs={{0,16},{16,32},{32,48},{48,64},{64,80},{80,96},{96,112},{1,17},{17... | collective-permute-start | bytes 196616 | tf_op jit(solution)/shard_map/ppermute | solution.py:330
  18.7 3.2 %collective-permute-start.3 = (bf16[64,512]{1,0:T(8,128)(2,1)S(1)}, bf16[64,512]{1,0:T(8,128)(2,1)S(1)}, u32[]{:S(2)}, u32[]{:S(2)}) collective-permute-start(bf16[64,512]{1,0:T(8,128)(2,1)S(1)} %get-tuple-element.43), channel_id=1, source_target_pairs={{0,1},{1,2},{2,3},{3,4},{4,5},{5,6},{6,7},{7,8},{8,9},{9,10},{10,1... | collective-permute-start | bytes 196616 | tf_op jit(solution)/shard_map/ppermute | solution.py:330
  21.9 5.0 %collective-permute-start.4 = (bf16[64,512]{1,0:T(8,128)(2,1)S(1)}, bf16[64,512]{1,0:T(8,128)(2,1)S(1)}, u32[]{:S(2)}, u32[]{:S(2)}) collective-permute-start(bf16[64,512]{1,0:T(8,128)(2,1)S(1)} %get-tuple-element.44), channel_id=1, source_target_pairs={{0,16},{16,32},{32,48},{48,64},{64,80},{80,96},{96,112},{1,17},{17... | collective-permute-start | bytes 196616 | tf_op jit(solution)/shard_map/ppermute | solution.py:330
  27.0 3.5 %collective-permute-start.5 = (bf16[64,128]{1,0:T(8,128)(2,1)S(1)}, bf16[64,128]{1,0:T(8,128)(2,1)S(1)}, u32[]{:S(2)}, u32[]{:S(2)}) collective-permute-start(bf16[64,128]{1,0:T(8,128)(2,1)S(1)} %get-tuple-element.45), channel_id=1, source_target_pairs={{0,17},{1,18},{2,19},{3,20},{4,21},{5,22},{6,23},{7,24},{8,25},{9,... | collective-permute-start | bytes 49160 | tf_op jit(solution)/shard_map/ppermute | solution.py:331
  30.5 1.4 %collective-permute-done.5.corner = bf16[64,128]{1,0:T(8,128)(2,1)S(1)} collective-permute-done((bf16[64,128]{1,0:T(8,128)(2,1)S(1)}, bf16[64,128]{1,0:T(8,128)(2,1)S(1)}, u32[]{:S(2)}, u32[]{:S(2)}) %collective-permute-start.5) | collective-permute-done | bytes 16416 | tf_op jit(solution)/shard_map/ppermute | solution.py:331
  32.4 4.6 %collective-permute-start.6 = (bf16[64,256]{1,0:T(8,128)(2,1)S(1)}, bf16[64,256]{1,0:T(8,128)(2,1)S(1)}, u32[]{:S(2)}, u32[]{:S(2)}) collective-permute-start(bf16[64,256]{1,0:T(8,128)(2,1)S(1)} %get-tuple-element.48), channel_id=1, source_target_pairs={{0,1},{1,2},{2,3},{3,4},{4,5},{5,6},{6,7},{7,8},{8,9},{9,10},{10,1... | collective-permute-start | bytes 98312 | tf_op jit(solution)/shard_map/ppermute | solution.py:330
  37.0 3.0 %collective-permute-start.7 = (bf16[64,256]{1,0:T(8,128)(2,1)S(1)}, bf16[64,256]{1,0:T(8,128)(2,1)S(1)}, u32[]{:S(2)}, u32[]{:S(2)}) collective-permute-start(bf16[64,256]{1,0:T(8,128)(2,1)S(1)} %get-tuple-element.49), channel_id=1, source_target_pairs={{0,16},{16,32},{32,48},{48,64},{64,80},{80,96},{96,112},{1,17},{17... | collective-permute-start | bytes 98312 | tf_op jit(solution)/shard_map/ppermute | solution.py:330
  40.0 5.1 %collective-permute-start.8 = (bf16[64,128]{1,0:T(8,128)(2,1)S(1)}, bf16[64,128]{1,0:T(8,128)(2,1)S(1)}, u32[]{:S(2)}, u32[]{:S(2)}) collective-permute-start(bf16[64,128]{1,0:T(8,128)(2,1)S(1)} %get-tuple-element.50), channel_id=1, source_target_pairs={{0,17},{1,18},{2,19},{3,20},{4,21},{5,22},{6,23},{7,24},{8,25},{9,... | collective-permute-start | bytes 49160 | tf_op jit(solution)/shard_map/ppermute | solution.py:331
  45.2 1.4 %collective-permute-done.8.corner = bf16[64,128]{1,0:T(8,128)(2,1)S(1)} collective-permute-done((bf16[64,128]{1,0:T(8,128)(2,1)S(1)}, bf16[64,128]{1,0:T(8,128)(2,1)S(1)}, u32[]{:S(2)}, u32[]{:S(2)}) %collective-permute-start.8) | collective-permute-done | bytes 16416 | tf_op jit(solution)/shard_map/ppermute | solution.py:331
  46.6 1.1 shard_map.105
  50.2 14.3 %all-to-all-start = ((f32[128,1,128]{2,1,0:T(1,128)}), f32[128,1,128]{2,1,0:T(1,128)S(1)}, u32[]{:S(2)}, u32[]{:S(2)}) async-start(f32[128,1,128]{2,1,0:T(1,128)} %bitcast.12), calls=%async_computation | async-start | bytes 131072 | tf_op jit(solution)/shard_map/all_to_all | solution.py:392
  64.5 2.8 %collective-permute-start.9 = (bf16[64,384]{1,0:T(8,128)(2,1)}, bf16[64,384]{1,0:T(8,128)(2,1)S(1)}, u32[]{:S(2)}, u32[]{:S(2)}) collective-permute-start(bf16[64,384]{1,0:T(8,128)(2,1)} %get-tuple-element.56), channel_id=1, source_target_pairs={{16,0},{32,16},{48,32},{64,48},{80,64},{96,80},{112,96},{17,1},{33... | collective-permute-start | bytes 147464 | tf_op jit(solution)/shard_map/ppermute | solution.py:330
  67.3 1.3 collective-permute-start.10
  68.6 1.3 collective-permute-start.11
  70.6 5.3 %collective-permute-done.11.of_corner = bf16[64,256]{1,0:T(8,128)(2,1)} collective-permute-done((bf16[64,256]{1,0:T(8,128)(2,1)}, bf16[64,256]{1,0:T(8,128)(2,1)}, u32[]{:S(2)}, u32[]{:S(2)}) %collective-permute-start.11) | collective-permute-done | bytes 32800 | tf_op jit(solution)/shard_map/ppermute | solution.py:331
  78.6 3.3 %shard_map.106 = f32[640,128]{1,0:T(8,128)S(1)} custom-call(f32[128,128]{1,0:T(8,128)S(1)} %bitcast.36, f32[4,64]{1,0:T(4,128)S(1)} %copy-done.7, f32[4,1]{1,0:T(4,128)S(1)} %copy.18.targets, f32[64,2048]{1,0:T(8,128)S(1)} %get-tuple-element.54.s1, f32[64,512]{1,0:T(8,128)S(1)} %get-tuple-element.52.slope2.s2, f32[64,128]{1,0:T(8,128)S(1)} %copy-done.6, ...), custom_call_target="tpu_custom_call" | custom-call | tf_op jit(solution)/shard_map/pallas_call | solution.py:18
  81.8 18.0 %all_to_all.26 = f32[16,40,128]{2,1,0:T(8,128)S(1)} all-to-all(f32[16,40,128]{2,1,0:T(8,128)S(1)} %bitcast.33), channel_id=1, replica_groups=mesh['batch'=2,'gz'=8,'gy'=16] {'gy'}, dimensions={0} | all-to-all | bytes 655360 | tf_op jit(solution)/shard_map/all_to_all | solution.py:342
  99.9 3.4 %psum.7 = f32[40,128]{1,0:T(8,128)S(1)} all-reduce(f32[40,128]{1,0:T(8,128)S(1)} %reduce_sum.18), channel_id=1, replica_groups=mesh['batch'=2,'gz'=8,'gy'=16] {'batch'}, use_global_device_ids=true, to_apply=%region_1.2 | all-reduce | flops 5120 | bytes 40960 | tf_op jit(solution)/shard_map/psum | solution.py:343
  103.3 15.9 %all_to_all.27 = f32[8,40,128]{2,1,0:T(8,128)S(1)} all-to-all(f32[8,40,128]{2,1,0:T(8,128)S(1)} %broadcast_in_dim.4), channel_id=1, replica_groups=mesh['batch'=2,'gz'=8,'gy'=16] {'gz'}, dimensions={0} | all-to-all | bytes 327680 | tf_op jit(solution)/shard_map/all_to_all | solution.py:336
  119.3 12.3 %all_to_all.28 = f32[16,40,128]{2,1,0:T(8,128)S(1)} all-to-all(f32[16,40,128]{2,1,0:T(8,128)S(1)} %broadcast_in_dim.5), channel_id=1, replica_groups=mesh['batch'=2,'gz'=8,'gy'=16] {'gy'}, dimensions={0} | all-to-all | bytes 655360 | tf_op jit(solution)/shard_map/all_to_all | solution.py:336
  131.6 1.1 shard_map.107
  (44 shorter events, 11.0 us)
Async XLA Ops:
  0.6 1.2 copy-start
  2.4 15.3 %collective-permute-start.2 = (bf16[32,128]{1,0:T(8,128)(2,1)S(1)}, bf16[32,128]{1,0:T(8,128)(2,1)S(1)}, u32[]{:S(2)}, u32[]{:S(2)}) collective-permute-start(bf16[32,128]{1,0:T(8,128)(2,1)S(1)} %get-tuple-element.40), channel_id=1, source_target_pairs={{0,17},{1,18},{2,19},{3,20},{4,21},{5,22},{6,23},{7,24},{8,25},{9,... | collective-permute-start | bytes 24584 | tf_op jit(solution)/shard_map/ppermute | solution.py:331
  7.3 10.5 %collective-permute-start = (bf16[8,32,128]{2,1,0:T(8,128)(2,1)S(1)}, bf16[8,32,128]{2,1,0:T(8,128)(2,1)S(1)}, u32[]{:S(2)}, u32[]{:S(2)}) collective-permute-start(bf16[8,32,128]{2,1,0:T(8,128)(2,1)S(1)} %get-tuple-element.38), channel_id=1, source_target_pairs={{0,1},{1,2},{2,3},{3,4},{4,5},{5,6},{6,7},{7,8},{8,9},{9,10},{10,1... | collective-permute-start | bytes 196616 | tf_op jit(solution)/shard_map/ppermute | solution.py:330
  10.8 7.0 %collective-permute-start.1 = (bf16[8,32,128]{2,1,0:T(8,128)(2,1)S(1)}, bf16[8,32,128]{2,1,0:T(8,128)(2,1)S(1)}, u32[]{:S(2)}, u32[]{:S(2)}) collective-permute-start(bf16[8,32,128]{2,1,0:T(8,128)(2,1)S(1)} %get-tuple-element.39), channel_id=1, source_target_pairs={{0,16},{16,32},{32,48},{48,64},{64,80},{80,96},{96,112},{1,17},{17... | collective-permute-start | bytes 196616 | tf_op jit(solution)/shard_map/ppermute | solution.py:330
  15.4 60.5 %copy-start.7 = (f32[4,64]{1,0:T(4,128)S(1)}, f32[4,64]{1,0:T(4,128)}, u32[]{:S(2)}) copy-start(f32[4,64]{1,0:T(4,128)} %head.1) | copy-start | bytes 3076
  17.8 29.9 %copy-start.3 = (bf16[720,128]{1,0:T(8,128)(2,1)}, bf16[720,128]{1,0:T(8,128)(2,1)S(1)}, u32[]{:S(2)}) copy-start(bf16[720,128]{1,0:T(8,128)(2,1)S(1)} %get-tuple-element.62.tt2) | copy-start | bytes 552964
  18.7 13.2 %collective-permute-start.3 = (bf16[64,512]{1,0:T(8,128)(2,1)S(1)}, bf16[64,512]{1,0:T(8,128)(2,1)S(1)}, u32[]{:S(2)}, u32[]{:S(2)}) collective-permute-start(bf16[64,512]{1,0:T(8,128)(2,1)S(1)} %get-tuple-element.43), channel_id=1, source_target_pairs={{0,1},{1,2},{2,3},{3,4},{4,5},{5,6},{6,7},{7,8},{8,9},{9,10},{10,1... | collective-permute-start | bytes 196616 | tf_op jit(solution)/shard_map/ppermute | solution.py:330
  21.9 10.0 %collective-permute-start.4 = (bf16[64,512]{1,0:T(8,128)(2,1)S(1)}, bf16[64,512]{1,0:T(8,128)(2,1)S(1)}, u32[]{:S(2)}, u32[]{:S(2)}) collective-permute-start(bf16[64,512]{1,0:T(8,128)(2,1)S(1)} %get-tuple-element.44), channel_id=1, source_target_pairs={{0,16},{16,32},{32,48},{48,64},{64,80},{80,96},{96,112},{1,17},{17... | collective-permute-start | bytes 196616 | tf_op jit(solution)/shard_map/ppermute | solution.py:330
  27.0 5.0 %collective-permute-start.5 = (bf16[64,128]{1,0:T(8,128)(2,1)S(1)}, bf16[64,128]{1,0:T(8,128)(2,1)S(1)}, u32[]{:S(2)}, u32[]{:S(2)}) collective-permute-start(bf16[64,128]{1,0:T(8,128)(2,1)S(1)} %get-tuple-element.45), channel_id=1, source_target_pairs={{0,17},{1,18},{2,19},{3,20},{4,21},{5,22},{6,23},{7,24},{8,25},{9,... | collective-permute-start | bytes 49160 | tf_op jit(solution)/shard_map/ppermute | solution.py:331
  32.4 14.2 %collective-permute-start.6 = (bf16[64,256]{1,0:T(8,128)(2,1)S(1)}, bf16[64,256]{1,0:T(8,128)(2,1)S(1)}, u32[]{:S(2)}, u32[]{:S(2)}) collective-permute-start(bf16[64,256]{1,0:T(8,128)(2,1)S(1)} %get-tuple-element.48), channel_id=1, source_target_pairs={{0,1},{1,2},{2,3},{3,4},{4,5},{5,6},{6,7},{7,8},{8,9},{9,10},{10,1... | collective-permute-start | bytes 98312 | tf_op jit(solution)/shard_map/ppermute | solution.py:330
  37.0 9.5 %collective-permute-start.7 = (bf16[64,256]{1,0:T(8,128)(2,1)S(1)}, bf16[64,256]{1,0:T(8,128)(2,1)S(1)}, u32[]{:S(2)}, u32[]{:S(2)}) collective-permute-start(bf16[64,256]{1,0:T(8,128)(2,1)S(1)} %get-tuple-element.49), channel_id=1, source_target_pairs={{0,16},{16,32},{32,48},{48,64},{64,80},{80,96},{96,112},{1,17},{17... | collective-permute-start | bytes 98312 | tf_op jit(solution)/shard_map/ppermute | solution.py:330
  40.0 6.5 %collective-permute-start.8 = (bf16[64,128]{1,0:T(8,128)(2,1)S(1)}, bf16[64,128]{1,0:T(8,128)(2,1)S(1)}, u32[]{:S(2)}, u32[]{:S(2)}) collective-permute-start(bf16[64,128]{1,0:T(8,128)(2,1)S(1)} %get-tuple-element.50), channel_id=1, source_target_pairs={{0,17},{1,18},{2,19},{3,20},{4,21},{5,22},{6,23},{7,24},{8,25},{9,... | collective-permute-start | bytes 49160 | tf_op jit(solution)/shard_map/ppermute | solution.py:331
  47.6 0.7 copy-start.1
  48.3 0.6 copy-start.5
  48.9 0.6 copy-start.8
  49.5 0.6 copy-start.9
  50.2 25.8 %all-to-all-start = ((f32[128,1,128]{2,1,0:T(1,128)}), f32[128,1,128]{2,1,0:T(1,128)S(1)}, u32[]{:S(2)}, u32[]{:S(2)}) async-start(f32[128,1,128]{2,1,0:T(1,128)} %bitcast.12), calls=%async_computation | async-start | bytes 131072 | tf_op jit(solution)/shard_map/all_to_all | solution.py:392
  64.5 11.4 %collective-permute-start.9 = (bf16[64,384]{1,0:T(8,128)(2,1)}, bf16[64,384]{1,0:T(8,128)(2,1)S(1)}, u32[]{:S(2)}, u32[]{:S(2)}) collective-permute-start(bf16[64,384]{1,0:T(8,128)(2,1)} %get-tuple-element.56), channel_id=1, source_target_pairs={{16,0},{32,16},{48,32},{64,48},{80,64},{96,80},{112,96},{17,1},{33... | collective-permute-start | bytes 147464 | tf_op jit(solution)/shard_map/ppermute | solution.py:330
  67.3 8.6 %collective-permute-start.10 = (bf16[64,384]{1,0:T(8,128)(2,1)}, bf16[64,384]{1,0:T(8,128)(2,1)S(1)}, u32[]{:S(2)}, u32[]{:S(2)}) collective-permute-start(bf16[64,384]{1,0:T(8,128)(2,1)} %copy-done.8), channel_id=1, source_target_pairs={{1,0},{2,1},{3,2},{4,3},{5,4},{6,5},{7,6},{8,7},{9,8},{10,9},{11,1... | collective-permute-start | bytes 147464 | tf_op jit(solution)/shard_map/ppermute | solution.py:330
  68.6 7.3 %collective-permute-start.11 = (bf16[64,256]{1,0:T(8,128)(2,1)}, bf16[64,256]{1,0:T(8,128)(2,1)}, u32[]{:S(2)}, u32[]{:S(2)}) collective-permute-start(bf16[64,256]{1,0:T(8,128)(2,1)} %copy-done.9), channel_id=1, source_target_pairs={{17,0},{18,1},{19,2},{20,3},{21,4},{22,5},{23,6},{24,7},{25,8},{26... | collective-permute-start | bytes 98312 | tf_op jit(solution)/shard_map/ppermute | solution.py:331
  75.9 0.9 copy-start.2
  76.9 0.9 copy-start.4
  77.8 0.8 copy-start.6

commit v3 on v2

v3 whole, which is shorter than its diff:
```python
import functools
import jax
import jax.numpy as jnp
from jax import lax
from jax.experimental import pallas as pl
from jax.experimental.pallas import tpu as pltpu
from jax.sharding import PartitionSpec as P

epsilon = 1e-06
f32 = jnp.float32
bf16 = jnp.bfloat16
LANES = 128
HALF = 64
CHUNKS, ROWS, HIGH, LOW = 16, 48, 40, 41


def call(body, outs, args, scratch=()):
    return pl.pallas_call(
        body,
        out_shape=[jax.ShapeDtypeStruct(s, d) for s, d in outs],
        in_specs=[pl.BlockSpec(memory_space=pltpu.VMEM)] * len(args),
        out_specs=[pl.BlockSpec(memory_space=pltpu.VMEM)] * len(outs),
        scratch_shapes=[pltpu.VMEM(s, d) for s, d in scratch],
        compiler_params=pltpu.CompilerParams(vmem_limit_bytes=48 * 1024 * 1024),
    )(*args)


def lane_of(shape):
    return lax.broadcasted_iota(jnp.int32, shape, len(shape) - 1)


def dot(a, b):
    return lax.dot_general(a, b, (((1,), (0,)), ((), ())), preferred_element_type=f32)


def dot_nt(a, b):
    return lax.dot_general(a, b, (((1,), (1,)), ((), ())), preferred_element_type=f32)


def upper_half(tile):
    top, bottom = tile[:16].astype(f32), tile[16:].astype(f32)
    return jnp.where(lane_of(top.shape) < HALF, pltpu.roll(top, HALF, 1), bottom).astype(bf16)


def row_below(own, received):
    turned, got = pltpu.roll(own.astype(f32), HALF, 1), received.astype(f32)
    low = lane_of(got.shape) < HALF
    top = jnp.where(low, got, turned[:16])
    bottom = jnp.where(low, pltpu.roll(got, HALF, 1), turned[16:])
    return jnp.concatenate([top, bottom], axis=0).astype(bf16)


def x_before(rows):
    return jnp.where(lane_of(rows.shape) % HALF == 0, 0.0, pltpu.roll(rows, 1, 1))


def x_after(rows):
    return jnp.where(lane_of(rows.shape) % HALF == HALF - 1, 0.0, pltpu.roll(rows, LANES - 1, 1))


def at(group):
    return slice(group * LANES, (group + 1) * LANES)


def arrange_body(vol, a0, row, plane, corner, rows):
    for z in range(8):
        tops = [c * 128 + z * 16 + yb * 8 for yb in range(2) for c in range(4)]
        cube = jnp.stack([vol[top : top + 8, :] for top in tops], axis=0)
        rows[z * 64 : z * 64 + 64, :] = jnp.transpose(cube, (1, 0, 2)).reshape(64, 512)
    x_at = lax.broadcasted_iota(jnp.int32, (512, 512), 0)
    to = lax.broadcasted_iota(jnp.int32, (512, 512), 1)
    move = jnp.where(x_at == (to % HALF) * 8 + to // HALF, 1.0, 0.0).astype(bf16)
    phased = dot(rows[...].astype(bf16), move)
    parts = []
    for j in range(4):
        part = phased[:, at(j)].reshape(64, 8, LANES)
        turned = pltpu.roll(pltpu.roll(part, 4, 1), HALF, 2)
        sub = lax.broadcasted_iota(jnp.int32, part.shape, 1)
        parts.append(jnp.where((sub < 4) == (lane_of(part.shape) < HALF), part, turned))
    whole = jnp.concatenate(parts, axis=1).astype(bf16)
    a0[...] = whole.reshape(8, 8, 32, LANES)
    plane[...] = a0[1:]
    for z in range(8):
        for yp in range(1, 8):
            half = upper_half(a0[z, yp])
            row[z, 16 * yp - 16 : 16 * yp, :] = half
            if z > 0:
                corner[z - 1, 16 * yp - 16 : 16 * yp, :] = half


def weights_body(w1, w2, w3, t1, t2, t3, tt2, tt3):
    eye = jnp.where(
        lax.broadcasted_iota(jnp.int32, (HALF, LANES), 0) == lane_of((HALF, LANES)), 1.0, 0.0
    ).astype(bf16)
    blocks = []
    for ab in range(9):
        both, low = w1[ab, 0], w1[ab, 1]
        for m in range(4):
            block = pltpu.roll(both, 16 * m, 1) if m else both
            if m < 3:
                block = block + pltpu.roll(low, 16 * (m + 1), 1)
            blocks.append(block)
        blocks += [jnp.zeros_like(low), low]
    t1[...] = dot_nt(eye, jnp.concatenate(blocks, axis=0).astype(bf16)).astype(bf16)
    blocks = []
    for ab in range(9):
        e0, e1, e2 = w2[3 * ab], w2[3 * ab + 1], w2[3 * ab + 2]
        blocks += [e1, e2 + pltpu.roll(e0, 32, 1), pltpu.roll(e1, 32, 1), pltpu.roll(e2, 32, 1), e0]
    tt2[...] = jnp.concatenate(blocks, axis=0).astype(bf16)
    t2[...] = dot_nt(eye, tt2[...]).astype(bf16)
    blocks = []
    for ab in range(9):
        blocks += [w3[3 * ab + 1], w3[3 * ab + 2], w3[3 * ab]]
    tt3[...] = jnp.concatenate(blocks, axis=0).astype(bf16)
    t3[...] = dot_nt(eye, tt3[...]).astype(bf16)


def fill_patches(tile, low, high, rows, moved, out):
    step, count = rows + moved, high - low + 1
    for zz in range(2 * low - 1, 2 * high + 2):
        for yy in range(2 * low - 1, 2 * high + 2):
            cell = tile(zz, yy)
            shifted = x_before(cell[rows - moved :].astype(f32)).astype(bf16)
            for a in range(3):
                for b in range(3):
                    i, j = zz + 1 - a, yy + 1 - b
                    if i % 2 or j % 2:
                        continue
                    i, j = i // 2 - low, j // 2 - low
                    if not (0 <= i < count and 0 <= j < count):
                        continue
                    top = (a * 3 + b) * step
                    out[top : top + rows, at(i * count + j)] = cell
                    out[top + rows : top + step, at(i * count + j)] = shifted


def finish(pre):
    root = jnp.sqrt(pre * pre + 1.0)
    return 0.65 * pre + 0.35 * (root - 1.0), 0.65 + 0.35 * pre / root


def forward_body(a0, row, plane, corner, t1, t2, t3, p1, p2, p3, s1, s2, s3, sums, a1, a2):
    def tile_one(zz, yy):
        own = a0[zz, yy % 8] if zz >= 0 else plane[zz + 7, yy % 8]
        if yy >= 0:
            return own
        part = slice(16 * (yy + 7), 16 * (yy + 8))
        return row_below(own, row[zz, part, :] if zz >= 0 else corner[zz + 7, part, :])

    fill_patches(tile_one, -3, 3, 32, 16, p1)
    act, s1[...] = finish(dot(t1[...], p1[...]))
    a1[...] = act.astype(bf16)
    fill_patches(lambda z, y: a1[:, at((z + 3) * 7 + y + 3)], -1, 1, 64, 16, p2)
    act, s2[...] = finish(dot(t2[...], p2[...]))
    a2[...] = act.astype(bf16)
    fill_patches(lambda z, y: a2[:, at((z + 1) * 3 + y + 1)], 0, 0, 64, 32, p3)
    act, s3[...] = finish(dot(t3[...], p3[...]))
    column = jnp.sum(act.astype(bf16).astype(f32), axis=1, keepdims=True)
    spot = lax.broadcasted_iota(jnp.int32, (HALF, LANES), 0) == lane_of((HALF, LANES))
    line = jnp.sum(jnp.where(spot, column, 0.0), axis=0, keepdims=True)
    sums[...] = jnp.broadcast_to(line, sums.shape)


def reach(index):
    return [(1, index // 2)] if index % 2 == 0 else [(2, index // 2), (0, index // 2 + 1)]


def back_cell(terms, z, y, step, rows, low, high):
    total = None
    for a, i in reach(z):
        for b, j in reach(y):
            if low <= i <= high and low <= j <= high:
                top = (a * 3 + b) * step
                part = terms[top : top + step, at((i - low) * (high - low + 1) + j - low)]
                total = part if total is None else total + part
    moved = step - rows
    last = total[rows - moved : rows] + x_after(total[rows:])
    return jnp.concatenate([total[: rows - moved], last], axis=0)


def backward_body(cells, share, gathered, head, targets, s1, s2, s3, p1, p2, p3, tt2, tt3,
                  result, out, err3, err2, err1, terms3, terms2):
    out[...] = jnp.zeros_like(out)
    pooled = jnp.sum(gathered[...], axis=0, keepdims=True)[:, :HALF] / cells
    errors = jnp.sum(head[...] * pooled, axis=1, keepdims=True) - targets[...]
    outer = errors * pooled * share
    loss = 0.5 * jnp.sum(errors * errors, axis=0, keepdims=True) * share
    exact = [jnp.concatenate([outer[0:1], outer[1:2]], axis=1),
             jnp.concatenate([outer[2:3], outer[3:4]], axis=1),
             jnp.broadcast_to(loss, (1, LANES))]
    for k, value in enumerate(exact):
        first = value.astype(bf16).astype(f32)
        out[k, HIGH : HIGH + 1, :] = first
        out[k, LOW : LOW + 1, :] = value - first
    line = jnp.sum(errors * head[...], axis=0, keepdims=True) / cells
    spot = lax.broadcasted_iota(jnp.int32, (HALF, HALF), 0) == lane_of((HALF, HALF))
    back_pool = jnp.sum(jnp.where(spot, line, 0.0), axis=1, keepdims=True)

    err3[:HALF, :] = (back_pool * s3[...]).astype(bf16)
    err3[HALF:, :] = jnp.zeros((HALF, LANES), bf16)
    err2[HALF:, :] = jnp.zeros((HALF, 9 * LANES), bf16)
    err1[HALF:, :] = jnp.zeros((HALF, 49 * LANES), bf16)
    terms3[...] = dot(tt3[...], err3[...])
    for k in range(9):
        back = back_cell(terms3, k // 3 - 1, k % 3 - 1, 96, 64, 0, 0)
        err2[:HALF, at(k)] = (back * s2[:, at(k)]).astype(bf16)
    terms2[...] = dot(tt2[...], err2[...])
    for k in range(49):
        back = back_cell(terms2, k // 7 - 3, k % 7 - 3, 80, 64, -1, 1)
        err1[:HALF, at(k)] = (back * s1[:, at(k)]).astype(bf16)

    grad = dot_nt(p3[...], err3[...])
    taps = [96 * ab + 32 * ((e + 2) % 3) for ab in range(9) for e in range(3)]
    for k, top in enumerate(taps[:14]):
        block = grad[top : top + 32]
        if k + 14 < 27:
            other = taps[k + 14]
            block = block + pltpu.roll(grad[other : other + 32], HALF, 1)
        out[k, :32, :] = block

    grad = dot_nt(p2[...], err2[...])
    blocks = []
    for ab in range(9):
        x = [grad[80 * ab + 16 * i : 80 * ab + 16 * i + 16] for i in range(5)]
        for first, second in ((4, 1), (0, 2), (1, 3)):
            block = x[first] + pltpu.roll(x[second], LANES - 32, 1)
            blocks.append(jnp.where(lane_of(block.shape) < 32, block, 0.0))
    for k in range(7):
        block = blocks[k]
        for m in range(1, 4):
            if k + 7 * m < 27:
                block = block + pltpu.roll(blocks[k + 7 * m], 32 * m, 1)
        for i, (chunk, top) in enumerate(places_two(k)):
            out[chunk, top : top + 8, :] = block[8 * i : 8 * i + 8]

    grad = dot_nt(p1[...], err1[...])
    blocks = []
    for ab in range(9):
        x = [grad[48 * ab + 8 * i : 48 * ab + 8 * i + 8] for i in range(6)]
        both, low = x[0], x[5]
        for m in range(1, 4):
            both = both + pltpu.roll(x[m], LANES - 16 * m, 1)
            low = low + pltpu.roll(x[m - 1], LANES - 16 * m, 1)
        low = jnp.where(lax.broadcasted_iota(jnp.int32, low.shape, 0) >= 4, low, 0.0)
        block = jnp.concatenate([both, low], axis=0)
        blocks.append(jnp.where(lane_of(block.shape) < 16, block, 0.0))
    block = blocks[0]
    for m in range(1, 8):
        block = block + pltpu.roll(blocks[m], 16 * m, 1)
    for m, block in enumerate((block, blocks[8])):
        for i, (chunk, top) in enumerate(places_one(m)):
            out[chunk, top : top + 8, :] = block[8 * i : 8 * i + 8]
    result[...] = out[...].astype(bf16)


def places_two(k):
    if k < 4:
        return [(14 + k // 2, 16 * (k % 2)), (14 + k // 2, 16 * (k % 2) + 8)]
    return [(2 * k - 8, 32), (2 * k - 7, 32)]


def places_one(m):
    return [(6 + 2 * m, 32), (7 + 2 * m, 32)]


def total_body(parts, out):
    total = parts[0].astype(f32)
    for k in range(1, parts.shape[0]):
        total = total + parts[k].astype(f32)
    exact = total[HIGH : HIGH + 1] + total[LOW : LOW + 1]
    first = exact.astype(bf16).astype(f32)
    at_row = lax.broadcasted_iota(jnp.int32, total.shape, 0)
    total = jnp.where(at_row == HIGH, first, jnp.where(at_row == LOW, exact - first, total))
    total = total.astype(bf16)
    for k in range(out.shape[0]):
        out[k] = total


def update_body(sent, u1, u2, u3, uh, loss, total):
    total[...] = sent[...].astype(f32)

    def scale(blocks, count):
        mean = 0.0
        for block in blocks:
            squares = jnp.sum(block * block, axis=0, keepdims=True)
            mean = mean + jnp.sum(squares, axis=1, keepdims=True) / count
        return 1.0 / jnp.sqrt(mean + epsilon)

    def read(places):
        return jnp.concatenate([total[chunk, top : top + 8, :] for chunk, top in places], axis=0)

    blocks = [total[k, :32, :] for k in range(14)]
    factor = scale(blocks, 64 * 32 * 27)
    for k, block in enumerate(blocks):
        block = block * factor
        u3[k] = block[:, :HALF]
        if k + 14 < 27:
            u3[k + 14] = pltpu.roll(block, HALF, 1)[:, :HALF]
    blocks = [read(places_two(k)) for k in range(7)]
    factor = scale(blocks, 32 * 16 * 27)
    for k, block in enumerate(blocks):
        block = block * factor
        for m in range(4):
            if k + 7 * m < 27:
                u2[k + 7 * m] = (pltpu.roll(block, LANES - 32 * m, 1) if m else block)[:, :32]
    blocks = [read(places_one(m)) for m in range(2)]
    factor = scale(blocks, 16 * 4 * 27)
    for ab in range(9):
        m = ab % 8
        block = blocks[ab // 8] * factor
        block = (pltpu.roll(block, LANES - 16 * m, 1) if m else block)[:, :16]
        u1[3 * ab] = block[12:16]
        u1[3 * ab + 1] = block[0:4]
        u1[3 * ab + 2] = block[4:8]
    exact = [total[k, HIGH : HIGH + 1, :] + total[k, LOW : LOW + 1, :] for k in range(3)]
    factor = scale(exact[:2], 4 * 64)
    for k in range(2):
        line = exact[k] * factor
        uh[2 * k : 2 * k + 1, :] = line[:, :HALF]
        uh[2 * k + 1 : 2 * k + 2, :] = pltpu.roll(line, HALF, 1)[:, :HALF]
    loss[...] = exact[2]


def neighbours(by):
    gz, gy = lax.axis_size("gz"), lax.axis_size("gy")
    z = [(i, i + by) for i in range(gz) if 0 <= i + by < gz]
    y = [(i, i + by) for i in range(gy) if 0 <= i + by < gy]
    corner = [(i * gy + j, k * gy + l) for i, k in z for j, l in y]
    return y, z, corner


def exchange(row, plane, corner, by):
    y, z, both = neighbours(by)
    return (lax.ppermute(row, "gy", y), lax.ppermute(plane, "gz", z),
            lax.ppermute(corner, ("gz", "gy"), both))


def summed_over_all(parts):
    beyond = lax.axis_size(("batch", "gz"))
    parts = lax.all_to_all(parts, "gy", 0, 0, tiled=True)
    (parts,) = call(total_body, [((beyond, ROWS, LANES), bf16)], (parts,))
    parts = lax.all_to_all(parts, ("batch", "gz"), 0, 0, tiled=True)
    (parts,) = call(total_body, [((CHUNKS, ROWS, LANES), bf16)], (parts,))
    return lax.all_to_all(parts, "gy", 0, 0, tiled=True)


def local(volume, conv_one, conv_two, conv_three, head_weight, targets):
    devices = lax.axis_size("gz") * lax.axis_size("gy")
    cells = float(devices * LANES)

    def taps(w):
        w = jnp.transpose(w, (2, 3, 4, 1, 0)).astype(f32)
        return jnp.pad(w.reshape((27,) + w.shape[3:]), ((0, 0), (0, 0), (0, LANES - w.shape[4])))

    w1 = taps(conv_one).reshape(9, 3, 4, LANES)
    both = w1[:, 1:].reshape(9, 1, 8, LANES)
    low = jnp.pad(w1[:, :1], ((0, 0), (0, 0), (4, 0), (0, 0)))
    t1, t2, t3, tt2, tt3 = call(
        weights_body,
        [((64, 432), bf16), ((64, 720), bf16), ((64, 864), bf16), ((720, LANES), bf16), ((864, LANES), bf16)],
        (jnp.concatenate([both, low], axis=1), taps(conv_two), taps(conv_three)),
    )
    a0, row, plane, corner = call(
        arrange_body,
        [((8, 8, 32, LANES), bf16), ((8, 112, LANES), bf16), ((7, 8, 32, LANES), bf16), ((7, 112, LANES), bf16)],
        (volume.reshape(512, 512),),
        [((512, 512), f32)],
    )
    row, plane, corner = exchange(row, plane, corner, 1)
    p1, p2, p3, s1, s2, s3, sums = call(
        forward_body,
        [((432, 49 * LANES), bf16), ((720, 9 * LANES), bf16), ((864, LANES), bf16),
         ((64, 49 * LANES), f32), ((64, 9 * LANES), f32), ((64, LANES), f32), ((devices, LANES), f32)],
        (a0, row, plane, corner, t1, t2, t3),
        [((64, 49 * LANES), bf16), ((64, 9 * LANES), bf16)],
    )
    pooled = lax.all_to_all(sums, ("gz", "gy"), 0, 0, tiled=True)
    (flat,) = call(
        functools.partial(backward_body, cells, 1.0 / devices),
        [((CHUNKS, ROWS, LANES), bf16)],
        (pooled, head_weight, targets.reshape(4, 1), s1, s2, s3, p1, p2, p3, tt2, tt3),
        [((CHUNKS, ROWS, LANES), f32), ((LANES, LANES), bf16), ((LANES, 9 * LANES), bf16),
         ((LANES, 49 * LANES), bf16), ((864, LANES), f32), ((720, 9 * LANES), f32)],
    )
    u1, u2, u3, uh, loss = call(
        update_body,
        [((27, 4, 16), f32), ((27, 16, 32), f32), ((27, 32, 64), f32), ((4, 64), f32), ((1, LANES), f32)],
        (summed_over_all(flat),),
        [((CHUNKS, ROWS, LANES), f32)],
    )

    def kernel_form(u):
        return jnp.transpose(u.reshape((3, 3, 3) + u.shape[1:]), (4, 3, 0, 1, 2))

    return kernel_form(u1), kernel_form(u2), kernel_form(u3), uh, loss[0, 0]


def solution(mesh):
    in_specs = (P("batch", None, "gz", "gy", None), P(), P(), P(), P(), P("batch", None))
    out_specs = (P(), P(), P(), P(), P())
    return jax.shard_map(local, mesh=mesh, in_specs=in_specs, out_specs=out_specs, check_vma=False)
```

time: 134 us -> 104 us (0.78)
  starting transfers between devices: 56.3 us -> 28.9 us
  blocking collectives: 49.6 us -> 35.7 us
  waiting for transfers between devices: 8.16 us -> 14.2 us
  Pallas kernels: 7.76 us -> 13.6 us
  local copies, waits for them, and re-layouts: 7.91 us -> 9.63 us
    ppermute x4 -> x1, starting transfers between devices: 14.6 us -> 3.82 us  [exchange(): lax.ppermute(plane, 'gz', z)]
    all_to_all x1, waiting for transfers between devices: 0.01 us -> 10.7 us  [local(): pooled = lax.all_to_all(sums, ('gz', 'gy'), 0, 0, tiled=True)]
    all_to_all x3, blocking collectives: 46.2 us -> 35.7 us  [the longest x1 13.3 us: summed_over_all(): parts = lax.all_to_all(parts, ('batch', 'gz'), 0, 0, tiled=True)]
    ppermute x4 -> x1, starting transfers between devices: 14.7 us -> 4.84 us  [exchange(): lax.ppermute(corner, ('gz', 'gy'), both)]
    ppermute x4 -> x1, starting transfers between devices: 12.6 us -> 3.5 us  [exchange(): lax.ppermute(row, 'gy', y)]
    pallas_call x7, Pallas kernels: 7.76 us -> 13.6 us  [call(): pl.pallas_call(body, out_shape=[jax.ShapeDtypeStruct(s, d) for s, d in ou...]
    ppermute x4 -> x1, waiting for transfers between devices: 8.14 us -> 3.47 us  [exchange(): lax.ppermute(corner, ('gz', 'gy'), both)]
    psum x1 -> x0, blocking collectives: 3.42 us -> none  [summed_over_all(): own = lax.psum(own, 'batch')]
  transfers between devices with their start and end apart: 13 -> 4, of which waited for: 3 -> 2; matrix products, arithmetic and copies ran while one was open for 3% -> 2% of each run, Pallas kernels for 0% -> 0%
where the time goes in v3:
time: 104 us
  blocking collectives  35.7 us (34%)
  starting transfers between devices  28.9 us (28%)
  waiting for transfers between devices  14.2 us (14%)
  Pallas kernels  13.6 us (13%)
  local copies, waits for them, and re-layouts  9.63 us (9%)
    all_to_all x1, starting transfers between devices, local(): pooled = lax.all_to_all(sums, ('gz', 'gy'), 0, 0, tiled=True)  16.8 us
    pallas_call x7, Pallas kernels, call(): pl.pallas_call(body, out_shape=[jax.ShapeDtypeStruct(s, d) for s, d in ou...  13.6 us
    all_to_all x1, blocking collectives, summed_over_all(): parts = lax.all_to_all(parts, ('batch', 'gz'), 0, 0, tiled=True)  13.3 us
    all_to_all x1, blocking collectives, summed_over_all(): return lax.all_to_all(parts, 'gy', 0, 0, tiled=True)  11.6 us
    all_to_all x1, blocking collectives, summed_over_all(): parts = lax.all_to_all(parts, 'gy', 0, 0, tiled=True)  10.8 us
    all_to_all x1, waiting for transfers between devices, local(): pooled = lax.all_to_all(sums, ('gz', 'gy'), 0, 0, tiled=True)  10.7 us
    unnamed x24, local copies, waits for them, and re-layouts  8.11 us
    ppermute x1, starting transfers between devices, exchange(): lax.ppermute(corner, ('gz', 'gy'), both)  4.84 us
  transfers between devices with their start and end apart: 4, of which 2 were waited for; matrix products, arithmetic and copies ran while one was open for 2% of the time, Pallas kernels for 0%

profile of v3, /device:TPU:32, one launch (start us, length us, event | category | flops | bytes accessed | tf_op | source)
XLA Modules:
  0.0 103.8 jit_solution(7387106534374278229)
XLA Ops:
  0.6 1.2 %copy-done = f32[1,4,8,16,512]{4,3,2,1,0:T(8,128)S(1)} copy-done((f32[1,4,8,16,512]{4,3,2,1,0:T(8,128)S(1)}, f32[1,4,8,16,512]{4,3,2,1,0:T(8,128)}, u32[]{:S(2)}) %copy-start) | copy-done | bytes 1048600
  1.9 0.7 shard_map.101
  2.6 3.8 %collective-permute-start.1 = (bf16[7,8,32,128]{3,2,1,0:T(8,128)(2,1)S(1)}, bf16[7,8,32,128]{3,2,1,0:T(8,128)(2,1)S(1)}, u32[]{:S(2)}, u32[]{:S(2)}) collective-permute-start(bf16[7,8,32,128]{3,2,1,0:T(8,128)(2,1)S(1)} %get-tuple-element.28), channel_id=1, source_target_pairs={{0,16},{16,32},{32,48},{48,64},{64,80},{80,96},{96,112},{1,17},{17... | collective-permute-start | bytes 1376264 | tf_op jit(solution)/shard_map/ppermute | solution.py:334
  6.4 3.5 %collective-permute-start = (bf16[8,112,128]{2,1,0:T(8,128)(2,1)S(1)}, bf16[8,112,128]{2,1,0:T(8,128)(2,1)S(1)}, u32[]{:S(2)}, u32[]{:S(2)}) collective-permute-start(bf16[8,112,128]{2,1,0:T(8,128)(2,1)S(1)} %get-tuple-element.27), channel_id=1, source_target_pairs={{0,1},{1,2},{2,3},{3,4},{4,5},{5,6},{6,7},{7,8},{8,9},{9,10},{10,1... | collective-permute-start | bytes 688136 | tf_op jit(solution)/shard_map/ppermute | solution.py:334
  9.9 4.8 %collective-permute-start.2 = (bf16[7,112,128]{2,1,0:T(8,128)(2,1)S(1)}, bf16[7,112,128]{2,1,0:T(8,128)(2,1)S(1)}, u32[]{:S(2)}, u32[]{:S(2)}) collective-permute-start(bf16[7,112,128]{2,1,0:T(8,128)(2,1)S(1)} %get-tuple-element.29), channel_id=1, source_target_pairs={{0,17},{1,18},{2,19},{3,20},{4,21},{5,22},{6,23},{7,24},{8,25},{9,... | collective-permute-start | bytes 602120 | tf_op jit(solution)/shard_map/ppermute | solution.py:335
  14.7 0.8 pad.21
  15.5 0.9 pad_convert_fusion.1.w2
  17.0 3.5 %collective-permute-done.2.corner = bf16[7,112,128]{2,1,0:T(8,128)(2,1)S(1)} collective-permute-done((bf16[7,112,128]{2,1,0:T(8,128)(2,1)S(1)}, bf16[7,112,128]{2,1,0:T(8,128)(2,1)S(1)}, u32[]{:S(2)}, u32[]{:S(2)}) %collective-permute-start.2) | collective-permute-done | bytes 200736 | tf_op jit(solution)/shard_map/ppermute | solution.py:335
  20.4 5.1 %shard_map.103 = (bf16[432,6272]{1,0:T(8,128)(2,1)}, bf16[720,1152]{1,0:T(8,128)(2,1)S(1)}, bf16[864,128]{1,0:T(8,128)(2,1)S(1)}, f32[64,6272]{1,0:T(8,128)S(1)}...) custom-call(bf16[8,8,32,128]{3,2,1,0:T(8,128)(2,1)S(1)} %get-tuple-element.26.a0, ...), custom_call_target="tpu_custom_call" | custom-call | tf_op jit(solution)/shard_map/pallas_call | solution.py:18
  25.6 0.7 copy-done.1
  26.3 0.7 copy-done.3
  28.2 16.8 %all-to-all-start = ((f32[128,1,128]{2,1,0:T(1,128)}), f32[128,1,128]{2,1,0:T(1,128)S(1)}, u32[]{:S(2)}, u32[]{:S(2)}) async-start(f32[128,1,128]{2,1,0:T(1,128)} %bitcast.33), calls=%async_computation | async-start | bytes 131072 | tf_op jit(solution)/shard_map/all_to_all | solution.py:377
  45.0 0.7 copy.15.targets
  45.7 10.7 %all-to-all-done = f32[128,1,128]{2,1,0:T(1,128)S(1)} async-done(((f32[128,1,128]{2,1,0:T(1,128)}), f32[128,1,128]{2,1,0:T(1,128)S(1)}, u32[]{:S(2)}, u32[]{:S(2)}) %all-to-all-start) | async-done | bytes 65568 | tf_op jit(solution)/shard_map/all_to_all | solution.py:377
  56.4 1.0 copy-done.2
  57.4 0.9 copy-done.4
  58.3 0.9 copy-done.6
  59.3 0.8 copy-done.9
  60.0 0.7 copy-done.10
  60.7 6.1 %shard_map.104 = bf16[16,48,128]{2,1,0:T(8,128)(2,1)S(1)} custom-call(f32[128,128]{1,0:T(8,128)S(1)} %bitcast.32, f32[4,64]{1,0:T(4,128)S(1)} %copy-done.10, f32[4,1]{1,0:T(4,128)S(1)} %copy.15.targets, f32[64,6272]{1,0:T(8,128)S(1)} %get-tuple-element.34.s1, f32[64,1152]{1,0:T(8,128)S(1)} %copy-done.2, f32[64,128]{1,0:T(8,128)S(1)} %copy-done.9, ...), custom_call_target="tpu_custom_call" | custom-call | tf_op jit(solution)/shard_map/pallas_call | solution.py:18
  66.8 10.8 %all_to_all.26.parts = bf16[16,48,128]{2,1,0:T(8,128)(2,1)S(1)} all-to-all(bf16[16,48,128]{2,1,0:T(8,128)(2,1)S(1)} %shard_map.104), channel_id=1, replica_groups=mesh['batch'=2,'gz'=8,'gy'=16] {'gy'}, dimensions={0} | all-to-all | bytes 393216 | tf_op jit(solution)/shard_map/all_to_all | solution.py:340
  77.7 13.3 %all_to_all.27.parts = bf16[16,48,128]{2,1,0:T(8,128)(2,1)S(1)} all-to-all(bf16[16,48,128]{2,1,0:T(8,128)(2,1)S(1)} %shard_map.105), channel_id=1, replica_groups=mesh['batch'=2,'gz'=8,'gy'=16] {'batch','gz'}, dimensions={0} | all-to-all | bytes 393216 | tf_op jit(solution)/shard_map/all_to_all | solution.py:342
  91.0 11.6 %all_to_all.28.sent = bf16[16,48,128]{2,1,0:T(8,128)(2,1)S(1)} all-to-all(bf16[16,48,128]{2,1,0:T(8,128)(2,1)S(1)} %shard_map.106), channel_id=1, replica_groups=mesh['batch'=2,'gz'=8,'gy'=16] {'gy'}, dimensions={0} | all-to-all | bytes 393216 | tf_op jit(solution)/shard_map/all_to_all | solution.py:344
  102.6 1.2 %shard_map.107 = (f32[27,4,16]{2,1,0:T(4,128)}, f32[27,16,32]{2,1,0:T(8,128)}, f32[27,32,64]{2,1,0:T(8,128)}, f32[4,64]{1,0:T(4,128)}, f32[1,128]{1,0:T(1,128)}) custom-call(bf16[16,48,128]{2,1,0:T(8,128)(2,1)S(1)} %all_to_all.28.sent), custom_call_target="tpu_custom_call" | custom-call | tf_op jit(solution)/shard_map/pallas_call | solution.py:18
  (25 shorter events, 1.8 us)
Async XLA Ops:
  0.6 1.2 %copy-start = (f32[1,4,8,16,512]{4,3,2,1,0:T(8,128)S(1)}, f32[1,4,8,16,512]{4,3,2,1,0:T(8,128)}, u32[]{:S(2)}) copy-start(f32[1,4,8,16,512]{4,3,2,1,0:T(8,128)} %param.6) | copy-start | bytes 3145732
  1.9 14.6 %copy-start.11 = (bf16[64,32,3,3,3]{0,1,4,3,2:T(8,128)(2,1)S(1)}, bf16[64,32,3,3,3]{0,1,4,3,2:T(8,128)(2,1)}, u32[]{:S(2)}) copy-start(bf16[64,32,3,3,3]{0,1,4,3,2:T(8,128)(2,1)} %param.9) | copy-start | bytes 331780
  2.6 17.9 %collective-permute-start.1 = (bf16[7,8,32,128]{3,2,1,0:T(8,128)(2,1)S(1)}, bf16[7,8,32,128]{3,2,1,0:T(8,128)(2,1)S(1)}, u32[]{:S(2)}, u32[]{:S(2)}) collective-permute-start(bf16[7,8,32,128]{3,2,1,0:T(8,128)(2,1)S(1)} %get-tuple-element.28), channel_id=1, source_target_pairs={{0,16},{16,32},{32,48},{48,64},{64,80},{80,96},{96,112},{1,17},{17... | collective-permute-start | bytes 1376264 | tf_op jit(solution)/shard_map/ppermute | solution.py:334
  6.4 14.1 %collective-permute-start = (bf16[8,112,128]{2,1,0:T(8,128)(2,1)S(1)}, bf16[8,112,128]{2,1,0:T(8,128)(2,1)S(1)}, u32[]{:S(2)}, u32[]{:S(2)}) collective-permute-start(bf16[8,112,128]{2,1,0:T(8,128)(2,1)S(1)} %get-tuple-element.27), channel_id=1, source_target_pairs={{0,1},{1,2},{2,3},{3,4},{4,5},{5,6},{6,7},{7,8},{8,9},{9,10},{10,1... | collective-permute-start | bytes 688136 | tf_op jit(solution)/shard_map/ppermute | solution.py:334
  9.9 10.6 %collective-permute-start.2 = (bf16[7,112,128]{2,1,0:T(8,128)(2,1)S(1)}, bf16[7,112,128]{2,1,0:T(8,128)(2,1)S(1)}, u32[]{:S(2)}, u32[]{:S(2)}) collective-permute-start(bf16[7,112,128]{2,1,0:T(8,128)(2,1)S(1)} %get-tuple-element.29), channel_id=1, source_target_pairs={{0,17},{1,18},{2,19},{3,20},{4,21},{5,22},{6,23},{7,24},{8,25},{9,... | collective-permute-start | bytes 602120 | tf_op jit(solution)/shard_map/ppermute | solution.py:335
  17.0 8.6 %copy-start.5 = (bf16[720,128]{1,0:T(8,128)(2,1)}, bf16[720,128]{1,0:T(8,128)(2,1)S(1)}, u32[]{:S(2)}) copy-start(bf16[720,128]{1,0:T(8,128)(2,1)S(1)} %get-tuple-element.40.tt2) | copy-start | bytes 552964
  25.6 0.7 copy-start.1
  26.3 0.7 copy-start.3
  27.0 0.6 copy-start.8
  27.6 0.6 copy-start.7
  28.2 28.2 %all-to-all-start = ((f32[128,1,128]{2,1,0:T(1,128)}), f32[128,1,128]{2,1,0:T(1,128)S(1)}, u32[]{:S(2)}, u32[]{:S(2)}) async-start(f32[128,1,128]{2,1,0:T(1,128)} %bitcast.33), calls=%async_computation | async-start | bytes 131072 | tf_op jit(solution)/shard_map/all_to_all | solution.py:377
  56.4 1.0 copy-start.2
  57.4 0.9 copy-start.4
  58.3 0.9 copy-start.6
  59.2 0.8 copy-start.9
  60.0 0.7 copy-start.10

commit v4 on v3

--- a/solution.py
+++ b/solution.py
@@ -12,16 +12,17 @@
 LANES = 128
 HALF = 64
 CHUNKS, ROWS, HIGH, LOW = 16, 48, 40, 41
-
-
-def call(body, outs, args, scratch=()):
+AT_TWO, AT_HEAD = 49 * LANES, 59 * LANES
+
+
+def call(body, outs, args, scratch=(), mib=8):
     return pl.pallas_call(
         body,
         out_shape=[jax.ShapeDtypeStruct(s, d) for s, d in outs],
         in_specs=[pl.BlockSpec(memory_space=pltpu.VMEM)] * len(args),
         out_specs=[pl.BlockSpec(memory_space=pltpu.VMEM)] * len(outs),
         scratch_shapes=[pltpu.VMEM(s, d) for s, d in scratch],
-        compiler_params=pltpu.CompilerParams(vmem_limit_bytes=48 * 1024 * 1024),
+        compiler_params=pltpu.CompilerParams(vmem_limit_bytes=mib * 1024 * 1024),
     )(*args)
 
 
@@ -139,7 +140,8 @@
     return 0.65 * pre + 0.35 * (root - 1.0), 0.65 + 0.35 * pre / root
 
 
-def forward_body(a0, row, plane, corner, t1, t2, t3, p1, p2, p3, s1, s2, s3, sums, a1, a2):
+def forward_body(a0, row, plane, corner, t1, t2, t3, tt2, tt3, head, targets,
+                 p1, kept, slopes, sums, a1, a2):
     def tile_one(zz, yy):
         own = a0[zz, yy % 8] if zz >= 0 else plane[zz + 7, yy % 8]
         if yy >= 0:
@@ -148,17 +150,23 @@
         return row_below(own, row[zz, part, :] if zz >= 0 else corner[zz + 7, part, :])
 
     fill_patches(tile_one, -3, 3, 32, 16, p1)
-    act, s1[...] = finish(dot(t1[...], p1[...]))
+    act, slopes[:, : 49 * LANES] = finish(dot(t1[...], p1[...]))
     a1[...] = act.astype(bf16)
-    fill_patches(lambda z, y: a1[:, at((z + 3) * 7 + y + 3)], -1, 1, 64, 16, p2)
-    act, s2[...] = finish(dot(t2[...], p2[...]))
+    fill_patches(lambda z, y: a1[:, at((z + 3) * 7 + y + 3)], -1, 1, 64, 16, kept)
+    act, slopes[:, AT_TWO : AT_TWO + 9 * LANES] = finish(dot(t2[...], kept[:720, : 9 * LANES]))
     a2[...] = act.astype(bf16)
-    fill_patches(lambda z, y: a2[:, at((z + 1) * 3 + y + 1)], 0, 0, 64, 32, p3)
-    act, s3[...] = finish(dot(t3[...], p3[...]))
+    fill_patches(lambda z, y: a2[:, at((z + 1) * 3 + y + 1)], 0, 0, 64, 32, kept.at[:, at(9)])
+    act, slopes[:, at(58)] = finish(dot(t3[...], kept[:, at(9)]))
     column = jnp.sum(act.astype(bf16).astype(f32), axis=1, keepdims=True)
     spot = lax.broadcasted_iota(jnp.int32, (HALF, LANES), 0) == lane_of((HALF, LANES))
     line = jnp.sum(jnp.where(spot, column, 0.0), axis=0, keepdims=True)
     sums[...] = jnp.broadcast_to(line, sums.shape)
+    kept[:720, at(10)] = tt2[...]
+    kept[:, at(11)] = tt3[...]
+    slopes[:4, AT_HEAD : AT_HEAD + HALF] = head[...]
+    spot = lax.broadcasted_iota(jnp.int32, (4, 4), 0) == lane_of((4, 4))
+    column = jnp.sum(jnp.where(spot, targets[...], 0.0), axis=1, keepdims=True)
+    slopes[8:12, AT_HEAD : AT_HEAD + LANES] = jnp.broadcast_to(column, (4, LANES))
 
 
 def reach(index):
@@ -178,11 +186,13 @@
     return jnp.concatenate([total[: rows - moved], last], axis=0)
 
 
-def backward_body(cells, share, gathered, head, targets, s1, s2, s3, p1, p2, p3, tt2, tt3,
+def backward_body(cells, share, gathered, p1, kept, slopes,
                   result, out, err3, err2, err1, terms3, terms2):
+    head = slopes[:4, AT_HEAD : AT_HEAD + HALF]
+    targets = slopes[8:12, AT_HEAD : AT_HEAD + 1]
     out[...] = jnp.zeros_like(out)
     pooled = jnp.sum(gathered[...], axis=0, keepdims=True)[:, :HALF] / cells
-    errors = jnp.sum(head[...] * pooled, axis=1, keepdims=True) - targets[...]
+    errors = jnp.sum(head * pooled, axis=1, keepdims=True) - targets
     outer = errors * pooled * share
     loss = 0.5 * jnp.sum(errors * errors, axis=0, keepdims=True) * share
     exact = [jnp.concatenate([outer[0:1], outer[1:2]], axis=1),
@@ -192,24 +202,24 @@
         first = value.astype(bf16).astype(f32)
         out[k, HIGH : HIGH + 1, :] = first
         out[k, LOW : LOW + 1, :] = value - first
-    line = jnp.sum(errors * head[...], axis=0, keepdims=True) / cells
+    line = jnp.sum(errors * head, axis=0, keepdims=True) / cells
     spot = lax.broadcasted_iota(jnp.int32, (HALF, HALF), 0) == lane_of((HALF, HALF))
     back_pool = jnp.sum(jnp.where(spot, line, 0.0), axis=1, keepdims=True)
 
-    err3[:HALF, :] = (back_pool * s3[...]).astype(bf16)
+    err3[:HALF, :] = (back_pool * slopes[:, at(58)]).astype(bf16)
     err3[HALF:, :] = jnp.zeros((HALF, LANES), bf16)
     err2[HALF:, :] = jnp.zeros((HALF, 9 * LANES), bf16)
     err1[HALF:, :] = jnp.zeros((HALF, 49 * LANES), bf16)
-    terms3[...] = dot(tt3[...], err3[...])
+    terms3[...] = dot(kept[:, at(11)], err3[...])
     for k in range(9):
         back = back_cell(terms3, k // 3 - 1, k % 3 - 1, 96, 64, 0, 0)
-        err2[:HALF, at(k)] = (back * s2[:, at(k)]).astype(bf16)
-    terms2[...] = dot(tt2[...], err2[...])
+        err2[:HALF, at(k)] = (back * slopes[:, at(49 + k)]).astype(bf16)
+    terms2[...] = dot(kept[:720, at(10)], err2[...])
     for k in range(49):
         back = back_cell(terms2, k // 7 - 3, k % 7 - 3, 80, 64, -1, 1)
-        err1[:HALF, at(k)] = (back * s1[:, at(k)]).astype(bf16)
-
-    grad = dot_nt(p3[...], err3[...])
+        err1[:HALF, at(k)] = (back * slopes[:, at(k)]).astype(bf16)
+
+    grad = dot_nt(kept[:, at(9)], err3[...])
     taps = [96 * ab + 32 * ((e + 2) % 3) for ab in range(9) for e in range(3)]
     for k, top in enumerate(taps[:14]):
         block = grad[top : top + 32]
@@ -218,7 +228,7 @@
             block = block + pltpu.roll(grad[other : other + 32], HALF, 1)
         out[k, :32, :] = block
 
-    grad = dot_nt(p2[...], err2[...])
+    grad = dot_nt(kept[:720, : 9 * LANES], err2[...])
     blocks = []
     for ab in range(9):
         x = [grad[80 * ab + 16 * i : 80 * ab + 16 * i + 16] for i in range(5)]
@@ -331,8 +341,9 @@
 
 def exchange(row, plane, corner, by):
     y, z, both = neighbours(by)
-    return (lax.ppermute(row, "gy", y), lax.ppermute(plane, "gz", z),
-            lax.ppermute(corner, ("gz", "gy"), both))
+    plane = lax.ppermute(plane, "gz", z)
+    corner = lax.ppermute(corner, ("gz", "gy"), both)
+    return lax.ppermute(row, "gy", y), plane, corner
 
 
 def summed_over_all(parts):
@@ -367,20 +378,21 @@
         [((512, 512), f32)],
     )
     row, plane, corner = exchange(row, plane, corner, 1)
-    p1, p2, p3, s1, s2, s3, sums = call(
+    p1, kept, slopes, sums = call(
         forward_body,
-        [((432, 49 * LANES), bf16), ((720, 9 * LANES), bf16), ((864, LANES), bf16),
-         ((64, 49 * LANES), f32), ((64, 9 * LANES), f32), ((64, LANES), f32), ((devices, LANES), f32)],
-        (a0, row, plane, corner, t1, t2, t3),
+        [((432, 49 * LANES), bf16), ((864, 12 * LANES), bf16), ((64, 60 * LANES), f32), ((devices, LANES), f32)],
+        (a0, row, plane, corner, t1, t2, t3, tt2, tt3, head_weight, targets),
         [((64, 49 * LANES), bf16), ((64, 9 * LANES), bf16)],
+        24,
     )
     pooled = lax.all_to_all(sums, ("gz", "gy"), 0, 0, tiled=True)
     (flat,) = call(
         functools.partial(backward_body, cells, 1.0 / devices),
         [((CHUNKS, ROWS, LANES), bf16)],
-        (pooled, head_weight, targets.reshape(4, 1), s1, s2, s3, p1, p2, p3, tt2, tt3),
+        (pooled, p1, kept, slopes),
         [((CHUNKS, ROWS, LANES), f32), ((LANES, LANES), bf16), ((LANES, 9 * LANES), bf16),
          ((LANES, 49 * LANES), bf16), ((864, LANES), f32), ((720, 9 * LANES), f32)],
+        24,
     )
     u1, u2, u3, uh, loss = call(
         update_body,

time: 104 us -> 92.6 us (0.89)
  blocking collectives: 35.7 us -> 60.8 us
  starting transfers between devices: 28.9 us -> 12.1 us
  waiting for transfers between devices: 14.2 us -> 5.43 us
  local copies, waits for them, and re-layouts: 9.63 us -> 2.01 us
  Pallas kernels: 13.6 us -> 9.08 us
    all_to_all x0 -> x1, blocking collectives: none -> 25.2 us  [local(): pooled = lax.all_to_all(sums, ('gz', 'gy'), 0, 0, tiled=True)]
    all_to_all x1 -> x0, starting transfers between devices: 16.8 us -> none  [local(): pooled = lax.all_to_all(sums, ('gz', 'gy'), 0, 0, tiled=True)]
    all_to_all x1 -> x0, waiting for transfers between devices: 10.7 us -> none  [local(): pooled = lax.all_to_all(sums, ('gz', 'gy'), 0, 0, tiled=True)]
    unnamed x24 -> x6, local copies, waits for them, and re-layouts: 8.11 us -> 1.23 us
    pallas_call x7, Pallas kernels: 13.6 us -> 9.08 us  [call(): pl.pallas_call(body, out_shape=[jax.ShapeDtypeStruct(s, d) for s, d in ou...]
    ppermute x3, waiting for transfers between devices: 3.48 us -> 5.43 us  [the longest x1 2.82 us: exchange(): return (lax.ppermute(row, 'gy', y), plane, corner)]
  transfers between devices with their start and end apart: 4 -> 3, of which waited for: 2 -> 2; matrix products, arithmetic and copies ran while one was open for 2% -> 3% of each run, Pallas kernels for 0% -> 0%
where the time goes in v4:
time: 92.6 us; the launch traced here: 92.1 us
  blocking collectives  60.8 us (66%)
  starting transfers between devices  12.1 us (13%)
  Pallas kernels  9.08 us (10%)
  waiting for transfers between devices  5.43 us (6%)
  local copies, waits for them, and re-layouts  2.01 us (2%)
  other arithmetic  1.91 us (2%)
    all_to_all x1, blocking collectives, local(): pooled = lax.all_to_all(sums, ('gz', 'gy'), 0, 0, tiled=True)  25.2 us
    all_to_all x1, blocking collectives, summed_over_all(): parts = lax.all_to_all(parts, ('batch', 'gz'), 0, 0, tiled=True)  13.3 us
    all_to_all x1, blocking collectives, summed_over_all(): return lax.all_to_all(parts, 'gy', 0, 0, tiled=True)  11.6 us
    all_to_all x1, blocking collectives, summed_over_all(): parts = lax.all_to_all(parts, 'gy', 0, 0, tiled=True)  10.8 us
    pallas_call x7, Pallas kernels, call(): pl.pallas_call(body, out_shape=[jax.ShapeDtypeStruct(s, d) for s, d in ou...  9.08 us
    ppermute x1, starting transfers between devices, exchange(): corner = lax.ppermute(corner, ('gz', 'gy'), both)  4.85 us
    ppermute x1, starting transfers between devices, exchange(): plane = lax.ppermute(plane, 'gz', z)  3.82 us
    ppermute x1, starting transfers between devices, exchange(): return (lax.ppermute(row, 'gy', y), plane, corner)  3.48 us
  transfers between devices with their start and end apart: 3, of which 2 were waited for; matrix products, arithmetic and copies ran while one was open for 3% of the time, Pallas kernels for 0%

profile of v4, /device:TPU:32, one launch (start us, length us, event | category | flops | bytes accessed | tf_op | source)
XLA Modules:
  0.0 92.1 jit_solution(17538522331387413513)
XLA Ops:
  0.6 0.0 copy-start.2
  0.6 0.0 copy-start
  0.7 1.2 %copy-done = f32[1,4,8,16,512]{4,3,2,1,0:T(8,128)S(1)} copy-done((f32[1,4,8,16,512]{4,3,2,1,0:T(8,128)S(1)}, f32[1,4,8,16,512]{4,3,2,1,0:T(8,128)}, u32[]{:S(2)}) %copy-start) | copy-done | bytes 1048600
  1.9 0.0 copy-start.1
  1.9 0.7 shard_map.101
  2.6 3.8 %collective-permute-start.1 = (bf16[7,8,32,128]{3,2,1,0:T(8,128)(2,1)S(1)}, bf16[7,8,32,128]{3,2,1,0:T(8,128)(2,1)S(1)}, u32[]{:S(2)}, u32[]{:S(2)}) collective-permute-start(bf16[7,8,32,128]{3,2,1,0:T(8,128)(2,1)S(1)} %get-tuple-element.25), channel_id=1, source_target_pairs={{0,16},{16,32},{32,48},{48,64},{64,80},{80,96},{96,112},{1,17},{17... | collective-permute-start | bytes 1376264 | tf_op jit(solution)/shard_map/ppermute | solution.py:344
  6.4 4.8 %collective-permute-start.2 = (bf16[7,112,128]{2,1,0:T(8,128)(2,1)S(1)}, bf16[7,112,128]{2,1,0:T(8,128)(2,1)S(1)}, u32[]{:S(2)}, u32[]{:S(2)}) collective-permute-start(bf16[7,112,128]{2,1,0:T(8,128)(2,1)S(1)} %get-tuple-element.26), channel_id=1, source_target_pairs={{0,17},{1,18},{2,19},{3,20},{4,21},{5,22},{6,23},{7,24},{8,25},{9,... | collective-permute-start | bytes 602120 | tf_op jit(solution)/shard_map/ppermute | solution.py:345
  11.2 3.5 %collective-permute-start = (bf16[8,112,128]{2,1,0:T(8,128)(2,1)S(1)}, bf16[8,112,128]{2,1,0:T(8,128)(2,1)S(1)}, u32[]{:S(2)}, u32[]{:S(2)}) collective-permute-start(bf16[8,112,128]{2,1,0:T(8,128)(2,1)S(1)} %get-tuple-element.24), channel_id=1, source_target_pairs={{0,1},{1,2},{2,3},{3,4},{4,5},{5,6},{6,7},{7,8},{8,9},{9,10},{10,1... | collective-permute-start | bytes 688136 | tf_op jit(solution)/shard_map/ppermute | solution.py:346
  14.7 0.8 pad.21
  15.5 0.9 pad_convert_fusion.1.w2
  16.5 1.0 %pad_convert_fusion.w3 = f32[27,32,128]{2,1,0:T(8,128)S(1)} fusion(bf16[27,32,64]{2,1,0:T(8,128)(2,1)} %bitcast.35), kind=kLoop, calls=%fused_computation | loop fusion | flops 110592 | bytes 552960 | tf_op jit(solution)/shard_map/jit(_pad)/pad | solution.py:364
  17.5 0.4 shard_map.102
  17.9 2.6 %collective-permute-done.2.corner = bf16[7,112,128]{2,1,0:T(8,128)(2,1)S(1)} collective-permute-done((bf16[7,112,128]{2,1,0:T(8,128)(2,1)S(1)}, bf16[7,112,128]{2,1,0:T(8,128)(2,1)S(1)}, u32[]{:S(2)}, u32[]{:S(2)}) %collective-permute-start.2) | collective-permute-done | bytes 200736 | tf_op jit(solution)/shard_map/ppermute | solution.py:345
  20.5 2.8 %collective-permute-done.row = bf16[8,112,128]{2,1,0:T(8,128)(2,1)S(1)} collective-permute-done((bf16[8,112,128]{2,1,0:T(8,128)(2,1)S(1)}, bf16[8,112,128]{2,1,0:T(8,128)(2,1)S(1)}, u32[]{:S(2)}, u32[]{:S(2)}) %collective-permute-start) | collective-permute-done | bytes 229408 | tf_op jit(solution)/shard_map/ppermute | solution.py:346
  23.3 0.0 collective-permute-done.1.plane
  23.3 0.0 copy-done.2
  23.3 0.0 copy-done.1
  23.3 3.1 %shard_map.103 = (bf16[432,6272]{1,0:T(8,128)(2,1)S(1)}, bf16[864,1536]{1,0:T(8,128)(2,1)S(1)}, f32[64,7680]{1,0:T(8,128)S(1)}, f32[128,128]{1,0:T(8,128)S(1)}) custom-call(bf16[8,8,32,128]{3,2,1,0:T(8,128)(2,1)S(1)} %get-tuple-element.23.a0, bf16[8,112,128]{2,1,0:T(8,128)(2,1)S(1)} %collective-permute-done.row, ...), custom_call_target="tpu_custom_call" | custom-call | tf_op jit(solution)/shard_map/pallas_call | solution.py:19
  26.4 25.2 %all_to_all.26 = f32[128,1,128]{2,1,0:T(1,128)S(1)} all-to-all(f32[128,1,128]{2,1,0:T(1,128)S(1)} %bitcast.32), channel_id=1, replica_groups=mesh['batch'=2,'gz'=8,'gy'=16] {'gz','gy'}, dimensions={0} | all-to-all | bytes 131072 | tf_op jit(solution)/shard_map/all_to_all | solution.py:388
  51.6 3.6 %shard_map.104 = bf16[16,48,128]{2,1,0:T(8,128)(2,1)S(1)} custom-call(f32[128,128]{1,0:T(8,128)S(1)} %bitcast.31, bf16[432,6272]{1,0:T(8,128)(2,1)S(1)} %get-tuple-element.33.p1, bf16[864,1536]{1,0:T(8,128)(2,1)S(1)} %get-tuple-element.34.kept, f32[64,7680]{1,0:T(8,128)S(1)} %get-tuple-element.35.slopes), custom_call_target="tpu_custom_call" | custom-call | tf_op jit(solution)/shard_map/pallas_call | solution.py:19
  55.2 10.8 %all_to_all.27.parts = bf16[16,48,128]{2,1,0:T(8,128)(2,1)S(1)} all-to-all(bf16[16,48,128]{2,1,0:T(8,128)(2,1)S(1)} %shard_map.104), channel_id=1, replica_groups=mesh['batch'=2,'gz'=8,'gy'=16] {'gy'}, dimensions={0} | all-to-all | bytes 393216 | tf_op jit(solution)/shard_map/all_to_all | solution.py:351
  66.1 13.3 %all_to_all.28.parts = bf16[16,48,128]{2,1,0:T(8,128)(2,1)S(1)} all-to-all(bf16[16,48,128]{2,1,0:T(8,128)(2,1)S(1)} %shard_map.105), channel_id=1, replica_groups=mesh['batch'=2,'gz'=8,'gy'=16] {'batch','gz'}, dimensions={0} | all-to-all | bytes 393216 | tf_op jit(solution)/shard_map/all_to_all | solution.py:353
  79.4 11.6 %all_to_all.29.sent = bf16[16,48,128]{2,1,0:T(8,128)(2,1)S(1)} all-to-all(bf16[16,48,128]{2,1,0:T(8,128)(2,1)S(1)} %shard_map.106), channel_id=1, replica_groups=mesh['batch'=2,'gz'=8,'gy'=16] {'gy'}, dimensions={0} | all-to-all | bytes 393216 | tf_op jit(solution)/shard_map/all_to_all | solution.py:355
  91.0 1.2 %shard_map.107 = (f32[27,4,16]{2,1,0:T(4,128)}, f32[27,16,32]{2,1,0:T(8,128)}, f32[27,32,64]{2,1,0:T(8,128)}, f32[4,64]{1,0:T(4,128)}, f32[1,128]{1,0:T(1,128)}) custom-call(bf16[16,48,128]{2,1,0:T(8,128)(2,1)S(1)} %all_to_all.29.sent), custom_call_target="tpu_custom_call" | custom-call | tf_op jit(solution)/shard_map/pallas_call | solution.py:19
  (5 shorter events, 0.1 us)
Async XLA Ops:
  0.6 22.7 %copy-start.2 = (f32[1,4]{1,0:T(1,128)S(1)}, f32[1,4]{1,0:T(1,128)}, u32[]{:S(2)}) copy-start(f32[1,4]{1,0:T(1,128)} %targets.1) | copy-start | bytes 52
  0.6 1.2 %copy-start = (f32[1,4,8,16,512]{4,3,2,1,0:T(8,128)S(1)}, f32[1,4,8,16,512]{4,3,2,1,0:T(8,128)}, u32[]{:S(2)}) copy-start(f32[1,4,8,16,512]{4,3,2,1,0:T(8,128)} %param.6) | copy-start | bytes 3145732
  1.9 21.4 %copy-start.1 = (f32[4,64]{1,0:T(4,128)S(1)}, f32[4,64]{1,0:T(4,128)}, u32[]{:S(2)}) copy-start(f32[4,64]{1,0:T(4,128)} %head.1) | copy-start | bytes 3076
  2.6 20.7 %collective-permute-start.1 = (bf16[7,8,32,128]{3,2,1,0:T(8,128)(2,1)S(1)}, bf16[7,8,32,128]{3,2,1,0:T(8,128)(2,1)S(1)}, u32[]{:S(2)}, u32[]{:S(2)}) collective-permute-start(bf16[7,8,32,128]{3,2,1,0:T(8,128)(2,1)S(1)} %get-tuple-element.25), channel_id=1, source_target_pairs={{0,16},{16,32},{32,48},{48,64},{64,80},{80,96},{96,112},{1,17},{17... | collective-permute-start | bytes 1376264 | tf_op jit(solution)/shard_map/ppermute | solution.py:344
  6.4 14.1 %collective-permute-start.2 = (bf16[7,112,128]{2,1,0:T(8,128)(2,1)S(1)}, bf16[7,112,128]{2,1,0:T(8,128)(2,1)S(1)}, u32[]{:S(2)}, u32[]{:S(2)}) collective-permute-start(bf16[7,112,128]{2,1,0:T(8,128)(2,1)S(1)} %get-tuple-element.26), channel_id=1, source_target_pairs={{0,17},{1,18},{2,19},{3,20},{4,21},{5,22},{6,23},{7,24},{8,25},{9,... | collective-permute-start | bytes 602120 | tf_op jit(solution)/shard_map/ppermute | solution.py:345
  11.2 12.1 %collective-permute-start = (bf16[8,112,128]{2,1,0:T(8,128)(2,1)S(1)}, bf16[8,112,128]{2,1,0:T(8,128)(2,1)S(1)}, u32[]{:S(2)}, u32[]{:S(2)}) collective-permute-start(bf16[8,112,128]{2,1,0:T(8,128)(2,1)S(1)} %get-tuple-element.24), channel_id=1, source_target_pairs={{0,1},{1,2},{2,3},{3,4},{4,5},{5,6},{6,7},{7,8},{8,9},{9,10},{10,1... | collective-permute-start | bytes 688136 | tf_op jit(solution)/shard_map/ppermute | solution.py:346

commit v5 on v4

--- a/solution.py
+++ b/solution.py
@@ -11,17 +11,18 @@
 bf16 = jnp.bfloat16
 LANES = 128
 HALF = 64
-CHUNKS, ROWS, HIGH, LOW = 16, 48, 40, 41
-AT_TWO, AT_HEAD = 49 * LANES, 59 * LANES
-
-
-def call(body, outs, args, scratch=(), mib=8):
+CHUNKS, ROWS = 16, 40
+EXACT, HIGH, LOW = 10, 32, 35
+AT_TWO, AT_THREE, AT_HEAD = 49, 58, 59 * LANES
+
+
+def call(body, outs, args, scratch=(), mib=8, spaces=None):
     return pl.pallas_call(
         body,
         out_shape=[jax.ShapeDtypeStruct(s, d) for s, d in outs],
-        in_specs=[pl.BlockSpec(memory_space=pltpu.VMEM)] * len(args),
+        in_specs=[pl.BlockSpec(memory_space=m) for m in spaces or [pltpu.VMEM] * len(args)],
         out_specs=[pl.BlockSpec(memory_space=pltpu.VMEM)] * len(outs),
-        scratch_shapes=[pltpu.VMEM(s, d) for s, d in scratch],
+        scratch_shapes=[pltpu.VMEM(*s) if isinstance(s, tuple) else s for s in scratch],
         compiler_params=pltpu.CompilerParams(vmem_limit_bytes=mib * 1024 * 1024),
     )(*args)
 
@@ -43,11 +44,16 @@
     return jnp.where(lane_of(top.shape) < HALF, pltpu.roll(top, HALF, 1), bottom).astype(bf16)
 
 
-def row_below(own, received):
-    turned, got = pltpu.roll(own.astype(f32), HALF, 1), received.astype(f32)
+def lower_half(tile):
+    top, bottom = tile[:16].astype(f32), tile[16:].astype(f32)
+    return jnp.where(lane_of(top.shape) < HALF, top, pltpu.roll(bottom, HALF, 1)).astype(bf16)
+
+
+def joined(received, inside, upper):
+    got = received.astype(f32) * inside
     low = lane_of(got.shape) < HALF
-    top = jnp.where(low, got, turned[:16])
-    bottom = jnp.where(low, pltpu.roll(got, HALF, 1), turned[16:])
+    top = jnp.where(low, got, upper[:16])
+    bottom = jnp.where(low, pltpu.roll(got, HALF, 1), upper[16:])
     return jnp.concatenate([top, bottom], axis=0).astype(bf16)
 
 
@@ -63,7 +69,7 @@
     return slice(group * LANES, (group + 1) * LANES)
 
 
-def arrange_body(vol, a0, row, plane, corner, rows):
+def arrange_body(vol, a0, row, below, corner, rows):
     for z in range(8):
         tops = [c * 128 + z * 16 + yb * 8 for yb in range(2) for c in range(4)]
         cube = jnp.stack([vol[top : top + 8, :] for top in tops], axis=0)
@@ -80,8 +86,10 @@
         parts.append(jnp.where((sub < 4) == (lane_of(part.shape) < HALF), part, turned))
     whole = jnp.concatenate(parts, axis=1).astype(bf16)
     a0[...] = whole.reshape(8, 8, 32, LANES)
-    plane[...] = a0[1:]
     for z in range(8):
+        for yp in range(8):
+            if z > 0:
+                below[z - 1, 16 * yp : 16 * yp + 16, :] = lower_half(a0[z, yp])
         for yp in range(1, 8):
             half = upper_half(a0[z, yp])
             row[z, 16 * yp - 16 : 16 * yp, :] = half
@@ -116,10 +124,11 @@
     t3[...] = dot_nt(eye, tt3[...]).astype(bf16)
 
 
-def fill_patches(tile, low, high, rows, moved, out):
-    step, count = rows + moved, high - low + 1
-    for zz in range(2 * low - 1, 2 * high + 2):
-        for yy in range(2 * low - 1, 2 * high + 2):
+def fill_patches(tile, z_range, y_range, rows, moved, out):
+    (z_low, z_high), (y_low, y_high) = z_range, y_range
+    step, deep, wide = rows + moved, z_high - z_low + 1, y_high - y_low + 1
+    for zz in range(2 * z_low - 1, 2 * z_high + 2):
+        for yy in range(2 * y_low - 1, 2 * y_high + 2):
             cell = tile(zz, yy)
             shifted = x_before(cell[rows - moved :].astype(f32)).astype(bf16)
             for a in range(3):
@@ -127,12 +136,12 @@
                     i, j = zz + 1 - a, yy + 1 - b
                     if i % 2 or j % 2:
                         continue
-                    i, j = i // 2 - low, j // 2 - low
-                    if not (0 <= i < count and 0 <= j < count):
+                    i, j = i // 2 - z_low, j // 2 - y_low
+                    if not (0 <= i < deep and 0 <= j < wide):
                         continue
                     top = (a * 3 + b) * step
-                    out[top : top + rows, at(i * count + j)] = cell
-                    out[top + rows : top + step, at(i * count + j)] = shifted
+                    out[top : top + rows, at(i * wide + j)] = cell
+                    out[top + rows : top + step, at(i * wide + j)] = shifted
 
 
 def finish(pre):
@@ -140,23 +149,35 @@
     return 0.65 * pre + 0.35 * (root - 1.0), 0.65 + 0.35 * pre / root
 
 
-def forward_body(a0, row, plane, corner, t1, t2, t3, tt2, tt3, head, targets,
+def forward_body(a0, above, row, below, corner, t1, t2, t3, tt2, tt3, head, targets, inside,
                  p1, kept, slopes, sums, a1, a2):
+    in_upper = jnp.full((32, LANES), inside[0], f32)
+    in_row = jnp.full((16, LANES), inside[1], f32)
+    in_below = jnp.full((16, LANES), inside[2], f32)
+    in_corner = in_row * in_below
+
     def tile_one(zz, yy):
-        own = a0[zz, yy % 8] if zz >= 0 else plane[zz + 7, yy % 8]
-        if yy >= 0:
-            return own
+        yp = yy % 8
         part = slice(16 * (yy + 7), 16 * (yy + 8))
-        return row_below(own, row[zz, part, :] if zz >= 0 else corner[zz + 7, part, :])
-
-    fill_patches(tile_one, -3, 3, 32, 16, p1)
+        if zz >= 0:
+            upper = above[zz, yp].astype(f32)
+            if yy < 0:
+                return joined(row[zz, part, :], in_row, pltpu.roll(upper, HALF, 1))
+            own = a0[zz, yp].astype(f32)
+            return jnp.where(lane_of(own.shape) < HALF, own, upper).astype(bf16)
+        upper = a0[zz + 8, yp].astype(f32) * in_upper
+        if yy < 0:
+            return joined(corner[zz + 7, part, :], in_corner, pltpu.roll(upper, HALF, 1))
+        return joined(below[zz + 7, 16 * yp : 16 * yp + 16, :], in_below, upper)
+
+    fill_patches(tile_one, (-3, 3), (-3, 3), 32, 16, p1)
     act, slopes[:, : 49 * LANES] = finish(dot(t1[...], p1[...]))
     a1[...] = act.astype(bf16)
-    fill_patches(lambda z, y: a1[:, at((z + 3) * 7 + y + 3)], -1, 1, 64, 16, kept)
-    act, slopes[:, AT_TWO : AT_TWO + 9 * LANES] = finish(dot(t2[...], kept[:720, : 9 * LANES]))
+    fill_patches(lambda z, y: a1[:, at((z + 3) * 7 + y + 3)], (-1, 1), (-1, 1), 64, 16, kept)
+    act, slopes[:, AT_TWO * LANES : AT_THREE * LANES] = finish(dot(t2[...], kept[:720, : 9 * LANES]))
     a2[...] = act.astype(bf16)
-    fill_patches(lambda z, y: a2[:, at((z + 1) * 3 + y + 1)], 0, 0, 64, 32, kept.at[:, at(9)])
-    act, slopes[:, at(58)] = finish(dot(t3[...], kept[:, at(9)]))
+    fill_patches(lambda z, y: a2[:, at((z + 1) * 3 + y + 1)], (0, 0), (0, 0), 64, 32, kept.at[:, at(9)])
+    act, slopes[:, at(AT_THREE)] = finish(dot(t3[...], kept[:, at(9)]))
     column = jnp.sum(act.astype(bf16).astype(f32), axis=1, keepdims=True)
     spot = lax.broadcasted_iota(jnp.int32, (HALF, LANES), 0) == lane_of((HALF, LANES))
     line = jnp.sum(jnp.where(spot, column, 0.0), axis=0, keepdims=True)
@@ -200,20 +221,20 @@
              jnp.broadcast_to(loss, (1, LANES))]
     for k, value in enumerate(exact):
         first = value.astype(bf16).astype(f32)
-        out[k, HIGH : HIGH + 1, :] = first
-        out[k, LOW : LOW + 1, :] = value - first
+        out[EXACT, HIGH + k : HIGH + k + 1, :] = first
+        out[EXACT, LOW + k : LOW + k + 1, :] = value - first
     line = jnp.sum(errors * head, axis=0, keepdims=True) / cells
     spot = lax.broadcasted_iota(jnp.int32, (HALF, HALF), 0) == lane_of((HALF, HALF))
     back_pool = jnp.sum(jnp.where(spot, line, 0.0), axis=1, keepdims=True)
 
-    err3[:HALF, :] = (back_pool * slopes[:, at(58)]).astype(bf16)
+    err3[:HALF, :] = (back_pool * slopes[:, at(AT_THREE)]).astype(bf16)
     err3[HALF:, :] = jnp.zeros((HALF, LANES), bf16)
     err2[HALF:, :] = jnp.zeros((HALF, 9 * LANES), bf16)
     err1[HALF:, :] = jnp.zeros((HALF, 49 * LANES), bf16)
     terms3[...] = dot(kept[:, at(11)], err3[...])
     for k in range(9):
         back = back_cell(terms3, k // 3 - 1, k % 3 - 1, 96, 64, 0, 0)
-        err2[:HALF, at(k)] = (back * slopes[:, at(49 + k)]).astype(bf16)
+        err2[:HALF, at(k)] = (back * slopes[:, at(AT_TWO + k)]).astype(bf16)
     terms2[...] = dot(kept[:720, at(10)], err2[...])
     for k in range(49):
         back = back_cell(terms2, k // 7 - 3, k % 7 - 3, 80, 64, -1, 1)
@@ -273,15 +294,15 @@
     return [(6 + 2 * m, 32), (7 + 2 * m, 32)]
 
 
-def total_body(parts, out):
+def total_body(parts, chunk, out):
     total = parts[0].astype(f32)
     for k in range(1, parts.shape[0]):
         total = total + parts[k].astype(f32)
-    exact = total[HIGH : HIGH + 1] + total[LOW : LOW + 1]
+    exact = total[HIGH:LOW] + total[LOW : LOW + 3]
     first = exact.astype(bf16).astype(f32)
-    at_row = lax.broadcasted_iota(jnp.int32, total.shape, 0)
-    total = jnp.where(at_row == HIGH, first, jnp.where(at_row == LOW, exact - first, total))
-    total = total.astype(bf16)
+    tail = jnp.concatenate([first, exact - first, total[LOW + 3 :]], axis=0)
+    tail = jnp.where(chunk[0] == EXACT, tail, total[HIGH:])
+    total = jnp.concatenate([total[:HIGH], tail], axis=0).astype(bf16)
     for k in range(out.shape[0]):
         out[k] = total
 
@@ -322,7 +343,8 @@
         u1[3 * ab] = block[12:16]
         u1[3 * ab + 1] = block[0:4]
         u1[3 * ab + 2] = block[4:8]
-    exact = [total[k, HIGH : HIGH + 1, :] + total[k, LOW : LOW + 1, :] for k in range(3)]
+    exact = [total[EXACT, HIGH + k : HIGH + k + 1, :] + total[EXACT, LOW + k : LOW + k + 1, :]
+             for k in range(3)]
     factor = scale(exact[:2], 4 * 64)
     for k in range(2):
         line = exact[k] * factor
@@ -331,33 +353,33 @@
     loss[...] = exact[2]
 
 
-def neighbours(by):
+def exchange(whole, row, below, corner):
     gz, gy = lax.axis_size("gz"), lax.axis_size("gy")
-    z = [(i, i + by) for i in range(gz) if 0 <= i + by < gz]
-    y = [(i, i + by) for i in range(gy) if 0 <= i + by < gy]
-    corner = [(i * gy + j, k * gy + l) for i, k in z for j, l in y]
-    return y, z, corner
-
-
-def exchange(row, plane, corner, by):
-    y, z, both = neighbours(by)
-    plane = lax.ppermute(plane, "gz", z)
+    z, y = [(i, (i + 1) % gz) for i in range(gz)], [(i, (i + 1) % gy) for i in range(gy)]
+    both = [(i * gy + j, k * gy + l) for i, k in z for j, l in y]
+    above = lax.ppermute(whole, "gz", [(k, i) for i, k in z])
+    below = lax.ppermute(below, "gz", z)
     corner = lax.ppermute(corner, ("gz", "gy"), both)
-    return lax.ppermute(row, "gy", y), plane, corner
-
-
-def summed_over_all(parts):
+    return above, lax.ppermute(row, "gy", y), below, corner
+
+
+def summed_over_all(parts, chunk):
     beyond = lax.axis_size(("batch", "gz"))
+    spaces = (pltpu.VMEM, pltpu.SMEM)
     parts = lax.all_to_all(parts, "gy", 0, 0, tiled=True)
-    (parts,) = call(total_body, [((beyond, ROWS, LANES), bf16)], (parts,))
+    (parts,) = call(total_body, [((beyond, ROWS, LANES), bf16)], (parts, chunk), spaces=spaces)
     parts = lax.all_to_all(parts, ("batch", "gz"), 0, 0, tiled=True)
-    (parts,) = call(total_body, [((CHUNKS, ROWS, LANES), bf16)], (parts,))
+    (parts,) = call(total_body, [((CHUNKS, ROWS, LANES), bf16)], (parts, chunk), spaces=spaces)
     return lax.all_to_all(parts, "gy", 0, 0, tiled=True)
 
 
 def local(volume, conv_one, conv_two, conv_three, head_weight, targets):
     devices = lax.axis_size("gz") * lax.axis_size("gy")
     cells = float(devices * LANES)
+    z_at, y_at = lax.axis_index("gz"), lax.axis_index("gy")
+    inside = jnp.stack([z_at < lax.axis_size("gz") - 1, y_at > 0, z_at > 0]).astype(f32)
+    chunk = y_at.astype(jnp.int32).reshape(1)
+    volume, chunk, inside = lax.optimization_barrier((volume, chunk, inside))
 
     def taps(w):
         w = jnp.transpose(w, (2, 3, 4, 1, 0)).astype(f32)
@@ -371,19 +393,20 @@
         [((64, 432), bf16), ((64, 720), bf16), ((64, 864), bf16), ((720, LANES), bf16), ((864, LANES), bf16)],
         (jnp.concatenate([both, low], axis=1), taps(conv_two), taps(conv_three)),
     )
-    a0, row, plane, corner = call(
+    a0, row, below, corner = call(
         arrange_body,
-        [((8, 8, 32, LANES), bf16), ((8, 112, LANES), bf16), ((7, 8, 32, LANES), bf16), ((7, 112, LANES), bf16)],
+        [((8, 8, 32, LANES), bf16), ((8, 112, LANES), bf16), ((7, LANES, LANES), bf16), ((7, 112, LANES), bf16)],
         (volume.reshape(512, 512),),
         [((512, 512), f32)],
     )
-    row, plane, corner = exchange(row, plane, corner, 1)
+    above, row, below, corner = exchange(a0, row, below, corner)
     p1, kept, slopes, sums = call(
         forward_body,
         [((432, 49 * LANES), bf16), ((864, 12 * LANES), bf16), ((64, 60 * LANES), f32), ((devices, LANES), f32)],
-        (a0, row, plane, corner, t1, t2, t3, tt2, tt3, head_weight, targets),
+        (a0, above, row, below, corner, t1, t2, t3, tt2, tt3, head_weight, targets, inside),
         [((64, 49 * LANES), bf16), ((64, 9 * LANES), bf16)],
         24,
+        [pltpu.VMEM] * 12 + [pltpu.SMEM],
     )
     pooled = lax.all_to_all(sums, ("gz", "gy"), 0, 0, tiled=True)
     (flat,) = call(
@@ -397,7 +420,7 @@
     u1, u2, u3, uh, loss = call(
         update_body,
         [((27, 4, 16), f32), ((27, 16, 32), f32), ((27, 32, 64), f32), ((4, 64), f32), ((1, LANES), f32)],
-        (summed_over_all(flat),),
+        (summed_over_all(flat, chunk),),
         [((CHUNKS, ROWS, LANES), f32)],
     )
 

time: 92.6 us -> 86.6 us (0.935)
  starting transfers between devices: 12.1 us -> 6.61 us
  blocking collectives: 60.8 us -> 57 us
  waiting for transfers between devices: 5.43 us -> 8.03 us
    ppermute x1, waiting for transfers between devices: 2.61 us -> 6.78 us  [exchange(): corner = lax.ppermute(corner, ('gz', 'gy'), both)]
    ppermute x1, starting transfers between devices: 4.85 us -> 1.19 us  [exchange(): corner = lax.ppermute(corner, ('gz', 'gy'), both)]
    all_to_all x1, blocking collectives: 25.2 us -> 22.4 us  [local(): pooled = lax.all_to_all(sums, ('gz', 'gy'), 0, 0, tiled=True)]
    ppermute x2 -> x3, starting transfers between devices: 7.3 us -> 5.42 us  [the longest x1 1.92 us: exchange(): above = lax.ppermute(whole, 'gz', [(k, i) for i, k in z])]
    ppermute x2 -> x3, waiting for transfers between devices: 2.82 us -> 1.25 us  [the longest x1 1.25 us: exchange(): return (above, lax.ppermute(row, 'gy', y), below, corner)]
  transfers between devices with their start and end apart: 3 -> 4, of which waited for: 2 -> 2; matrix products, arithmetic and copies ran while one was open for 3% -> 3% of each run, Pallas kernels for 0% -> 0%
where the time goes in v5:
time: 86.6 us; the launch traced here: 86.2 us
  blocking collectives  57 us (66%)
  Pallas kernels  9.85 us (11%)
  waiting for transfers between devices  8.03 us (9%)
  starting transfers between devices  6.61 us (8%)
  local copies, waits for them, and re-layouts  2.01 us (2%)
  other arithmetic  1.99 us (2%)
    all_to_all x1, blocking collectives, local(): pooled = lax.all_to_all(sums, ('gz', 'gy'), 0, 0, tiled=True)  22.4 us
    all_to_all x1, blocking collectives, summed_over_all(): parts = lax.all_to_all(parts, ('batch', 'gz'), 0, 0, tiled=True)  12.5 us
    all_to_all x1, blocking collectives, summed_over_all(): return lax.all_to_all(parts, 'gy', 0, 0, tiled=True)  11.4 us
    all_to_all x1, blocking collectives, summed_over_all(): parts = lax.all_to_all(parts, 'gy', 0, 0, tiled=True)  10.7 us
    pallas_call x7, Pallas kernels, call(): pl.pallas_call(body, out_shape=[jax.ShapeDtypeStruct(s, d) for s, d in ou...  9.85 us
    ppermute x1, waiting for transfers between devices, exchange(): corner = lax.ppermute(corner, ('gz', 'gy'), both)  6.78 us
    ppermute x1, starting transfers between devices, exchange(): above = lax.ppermute(whole, 'gz', [(k, i) for i, k in z])  1.92 us
    ppermute x1, starting transfers between devices, exchange(): below = lax.ppermute(below, 'gz', z)  1.92 us
  transfers between devices with their start and end apart: 4, of which 2 were waited for; matrix products, arithmetic and copies ran while one was open for 3% of the time, Pallas kernels for 0%

profile of v5, /device:TPU:32, one launch (start us, length us, event | category | flops | bytes accessed | tf_op | source)
XLA Modules:
  0.0 86.2 jit_solution(4792597414101147003)
XLA Ops:
  0.6 0.0 copy-start.2
  0.6 0.0 copy-start.1
  0.7 0.1 add_convert_fusion.inside
  0.7 1.2 %copy-done = f32[1,4,8,16,512]{4,3,2,1,0:T(8,128)S(1)} copy-done((f32[1,4,8,16,512]{4,3,2,1,0:T(8,128)S(1)}, f32[1,4,8,16,512]{4,3,2,1,0:T(8,128)}, u32[]{:S(2)}) %copy-start) | copy-done | bytes 1048600
  2.0 0.7 shard_map.101
  2.7 1.9 %collective-permute-start = (bf16[8,8,32,128]{3,2,1,0:T(8,128)(2,1)S(1)}, bf16[8,8,32,128]{3,2,1,0:T(8,128)(2,1)S(1)}, u32[]{:S(2)}, u32[]{:S(2)}) collective-permute-start(bf16[8,8,32,128]{3,2,1,0:T(8,128)(2,1)S(1)} %get-tuple-element.27.a0), channel_id=1, source_target_pairs={{16,0},{32,16},{48,32},{64,48},{80,64},{96,80},{112,96},{0,112},{1... | collective-permute-start | bytes 1572872 | tf_op jit(solution)/shard_map/ppermute | solution.py:360
  4.6 1.2 %collective-permute-start.3 = (bf16[7,112,128]{2,1,0:T(8,128)(2,1)S(1)}, bf16[7,112,128]{2,1,0:T(8,128)(2,1)S(1)}, u32[]{:S(2)}, u32[]{:S(2)}) collective-permute-start(bf16[7,112,128]{2,1,0:T(8,128)(2,1)S(1)} %get-tuple-element.30), channel_id=1, source_target_pairs={{0,17},{1,18},{2,19},{3,20},{4,21},{5,22},{6,23},{7,24},{8,25},{9,... | collective-permute-start | bytes 602120 | tf_op jit(solution)/shard_map/ppermute | solution.py:362
  5.8 1.6 %collective-permute-start.1 = (bf16[8,112,128]{2,1,0:T(8,128)(2,1)S(1)}, bf16[8,112,128]{2,1,0:T(8,128)(2,1)S(1)}, u32[]{:S(2)}, u32[]{:S(2)}) collective-permute-start(bf16[8,112,128]{2,1,0:T(8,128)(2,1)S(1)} %get-tuple-element.28), channel_id=1, source_target_pairs={{0,1},{1,2},{2,3},{3,4},{4,5},{5,6},{6,7},{7,8},{8,9},{9,10},{10,1... | collective-permute-start | bytes 688136 | tf_op jit(solution)/shard_map/ppermute | solution.py:363
  7.3 1.9 %collective-permute-start.2 = (bf16[7,128,128]{2,1,0:T(8,128)(2,1)S(1)}, bf16[7,128,128]{2,1,0:T(8,128)(2,1)S(1)}, u32[]{:S(2)}, u32[]{:S(2)}) collective-permute-start(bf16[7,128,128]{2,1,0:T(8,128)(2,1)S(1)} %get-tuple-element.29), channel_id=1, source_target_pairs={{0,16},{16,32},{32,48},{48,64},{64,80},{80,96},{96,112},{112,0},{1... | collective-permute-start | bytes 688136 | tf_op jit(solution)/shard_map/ppermute | solution.py:361
  9.3 0.8 pad.21
  10.1 0.9 %pad_convert_fusion.1.w2 = f32[27,16,128]{2,1,0:T(8,128)S(1)} fusion(bf16[27,16,32]{2,1,0:T(8,128)(2,1)} %bitcast.41), kind=kLoop, calls=%fused_computation.1 | loop fusion | flops 55296 | bytes 248832 | tf_op jit(solution)/shard_map/jit(_pad)/pad | solution.py:386
  11.0 1.0 %pad_convert_fusion.w3 = f32[27,32,128]{2,1,0:T(8,128)S(1)} fusion(bf16[27,32,64]{2,1,0:T(8,128)(2,1)} %bitcast.39), kind=kLoop, calls=%fused_computation | loop fusion | flops 110592 | bytes 552960 | tf_op jit(solution)/shard_map/jit(_pad)/pad | solution.py:386
  12.0 0.4 shard_map.102
  12.4 6.8 %collective-permute-done.3.corner = bf16[7,112,128]{2,1,0:T(8,128)(2,1)S(1)} collective-permute-done((bf16[7,112,128]{2,1,0:T(8,128)(2,1)S(1)}, bf16[7,112,128]{2,1,0:T(8,128)(2,1)S(1)}, u32[]{:S(2)}, u32[]{:S(2)}) %collective-permute-start.3) | collective-permute-done | bytes 200736 | tf_op jit(solution)/shard_map/ppermute | solution.py:362
  19.2 1.2 %collective-permute-done.1.row = bf16[8,112,128]{2,1,0:T(8,128)(2,1)S(1)} collective-permute-done((bf16[8,112,128]{2,1,0:T(8,128)(2,1)S(1)}, bf16[8,112,128]{2,1,0:T(8,128)(2,1)S(1)}, u32[]{:S(2)}, u32[]{:S(2)}) %collective-permute-start.1) | collective-permute-done | bytes 229408 | tf_op jit(solution)/shard_map/ppermute | solution.py:363
  20.4 0.0 collective-permute-done.2.below
  20.4 0.0 collective-permute-done.above
  20.5 3.8 %shard_map.103 = (bf16[432,6272]{1,0:T(8,128)(2,1)S(1)}, bf16[864,1536]{1,0:T(8,128)(2,1)S(1)}, f32[64,7680]{1,0:T(8,128)S(1)}, f32[128,128]{1,0:T(8,128)S(1)}) custom-call(bf16[8,8,32,128]{3,2,1,0:T(8,128)(2,1)S(1)} %get-tuple-element.27.a0, bf16[8,8,32,128]{3,2,1,0:T(8,128)(2,1)S(1)} %collective-permute-done.above, ...), custom_call_target="tpu_custom_call" | custom-call | tf_op jit(solution)/shard_map/pallas_call | solution.py:20
  24.3 22.4 %all_to_all.26 = f32[128,1,128]{2,1,0:T(1,128)S(1)} all-to-all(f32[128,1,128]{2,1,0:T(1,128)S(1)} %bitcast.36), channel_id=1, replica_groups=mesh['batch'=2,'gz'=8,'gy'=16] {'gz','gy'}, dimensions={0} | all-to-all | bytes 131072 | tf_op jit(solution)/shard_map/all_to_all | solution.py:411
  46.7 3.6 %shard_map.104 = bf16[16,40,128]{2,1,0:T(8,128)(2,1)S(1)} custom-call(f32[128,128]{1,0:T(8,128)S(1)} %bitcast.35, bf16[432,6272]{1,0:T(8,128)(2,1)S(1)} %get-tuple-element.38.p1, bf16[864,1536]{1,0:T(8,128)(2,1)S(1)} %get-tuple-element.39.kept, f32[64,7680]{1,0:T(8,128)S(1)} %get-tuple-element.40.slopes), custom_call_target="tpu_custom_call" | custom-call | tf_op jit(solution)/shard_map/pallas_call | solution.py:20
  50.3 10.7 %all_to_all.27.parts = bf16[16,40,128]{2,1,0:T(8,128)(2,1)S(1)} all-to-all(bf16[16,40,128]{2,1,0:T(8,128)(2,1)S(1)} %shard_map.104), channel_id=1, replica_groups=mesh['batch'=2,'gz'=8,'gy'=16] {'gy'}, dimensions={0} | all-to-all | bytes 327680 | tf_op jit(solution)/shard_map/all_to_all | solution.py:369
  61.1 12.5 %all_to_all.28.parts = bf16[16,40,128]{2,1,0:T(8,128)(2,1)S(1)} all-to-all(bf16[16,40,128]{2,1,0:T(8,128)(2,1)S(1)} %shard_map.105), channel_id=1, replica_groups=mesh['batch'=2,'gz'=8,'gy'=16] {'batch','gz'}, dimensions={0} | all-to-all | bytes 327680 | tf_op jit(solution)/shard_map/all_to_all | solution.py:371
  73.6 11.4 %all_to_all.29.sent = bf16[16,40,128]{2,1,0:T(8,128)(2,1)S(1)} all-to-all(bf16[16,40,128]{2,1,0:T(8,128)(2,1)S(1)} %shard_map.106), channel_id=1, replica_groups=mesh['batch'=2,'gz'=8,'gy'=16] {'gy'}, dimensions={0} | all-to-all | bytes 327680 | tf_op jit(solution)/shard_map/all_to_all | solution.py:373
  85.0 1.2 %shard_map.107 = (f32[27,4,16]{2,1,0:T(4,128)}, f32[27,16,32]{2,1,0:T(8,128)}, f32[27,32,64]{2,1,0:T(8,128)}, f32[4,64]{1,0:T(4,128)}, f32[1,128]{1,0:T(1,128)}) custom-call(bf16[16,40,128]{2,1,0:T(8,128)(2,1)S(1)} %all_to_all.29.sent), custom_call_target="tpu_custom_call" | custom-call | tf_op jit(solution)/shard_map/pallas_call | solution.py:20
  (8 shorter events, 0.1 us)
Async XLA Ops:
  0.6 19.8 %copy-start.2 = (f32[1,4]{1,0:T(1,128)S(1)}, f32[1,4]{1,0:T(1,128)}, u32[]{:S(2)}) copy-start(f32[1,4]{1,0:T(1,128)} %targets.1) | copy-start | bytes 52
  0.6 19.8 %copy-start.1 = (f32[4,64]{1,0:T(4,128)S(1)}, f32[4,64]{1,0:T(4,128)}, u32[]{:S(2)}) copy-start(f32[4,64]{1,0:T(4,128)} %head.1) | copy-start | bytes 3076
  0.7 1.2 %copy-start = (f32[1,4,8,16,512]{4,3,2,1,0:T(8,128)S(1)}, f32[1,4,8,16,512]{4,3,2,1,0:T(8,128)}, u32[]{:S(2)}) copy-start(f32[1,4,8,16,512]{4,3,2,1,0:T(8,128)} %param.6) | copy-start | bytes 3145732
  2.7 17.8 %collective-permute-start = (bf16[8,8,32,128]{3,2,1,0:T(8,128)(2,1)S(1)}, bf16[8,8,32,128]{3,2,1,0:T(8,128)(2,1)S(1)}, u32[]{:S(2)}, u32[]{:S(2)}) collective-permute-start(bf16[8,8,32,128]{3,2,1,0:T(8,128)(2,1)S(1)} %get-tuple-element.27.a0), channel_id=1, source_target_pairs={{16,0},{32,16},{48,32},{64,48},{80,64},{96,80},{112,96},{0,112},{1... | collective-permute-start | bytes 1572872 | tf_op jit(solution)/shard_map/ppermute | solution.py:360
  4.6 14.6 %collective-permute-start.3 = (bf16[7,112,128]{2,1,0:T(8,128)(2,1)S(1)}, bf16[7,112,128]{2,1,0:T(8,128)(2,1)S(1)}, u32[]{:S(2)}, u32[]{:S(2)}) collective-permute-start(bf16[7,112,128]{2,1,0:T(8,128)(2,1)S(1)} %get-tuple-element.30), channel_id=1, source_target_pairs={{0,17},{1,18},{2,19},{3,20},{4,21},{5,22},{6,23},{7,24},{8,25},{9,... | collective-permute-start | bytes 602120 | tf_op jit(solution)/shard_map/ppermute | solution.py:362
  5.8 14.7 %collective-permute-start.1 = (bf16[8,112,128]{2,1,0:T(8,128)(2,1)S(1)}, bf16[8,112,128]{2,1,0:T(8,128)(2,1)S(1)}, u32[]{:S(2)}, u32[]{:S(2)}) collective-permute-start(bf16[8,112,128]{2,1,0:T(8,128)(2,1)S(1)} %get-tuple-element.28), channel_id=1, source_target_pairs={{0,1},{1,2},{2,3},{3,4},{4,5},{5,6},{6,7},{7,8},{8,9},{9,10},{10,1... | collective-permute-start | bytes 688136 | tf_op jit(solution)/shard_map/ppermute | solution.py:363
  7.3 13.1 %collective-permute-start.2 = (bf16[7,128,128]{2,1,0:T(8,128)(2,1)S(1)}, bf16[7,128,128]{2,1,0:T(8,128)(2,1)S(1)}, u32[]{:S(2)}, u32[]{:S(2)}) collective-permute-start(bf16[7,128,128]{2,1,0:T(8,128)(2,1)S(1)} %get-tuple-element.29), channel_id=1, source_target_pairs={{0,16},{16,32},{32,48},{48,64},{64,80},{80,96},{96,112},{112,0},{1... | collective-permute-start | bytes 688136 | tf_op jit(solution)/shard_map/ppermute | solution.py:361

commit v6 on v5

--- a/solution.py
+++ b/solution.py
@@ -49,12 +49,13 @@
     return jnp.where(lane_of(top.shape) < HALF, top, pltpu.roll(bottom, HALF, 1)).astype(bf16)
 
 
-def joined(received, inside, upper):
-    got = received.astype(f32) * inside
-    low = lane_of(got.shape) < HALF
-    top = jnp.where(low, got, upper[:16])
-    bottom = jnp.where(low, pltpu.roll(got, HALF, 1), upper[16:])
-    return jnp.concatenate([top, bottom], axis=0).astype(bf16)
+def unpacked(received):
+    turned = pltpu.roll(received.astype(f32), HALF, 1).astype(bf16)
+    return jnp.concatenate([received, turned], axis=0)
+
+
+def half_turned(tile):
+    return pltpu.roll(tile.astype(f32), HALF, 1).astype(bf16)
 
 
 def x_before(rows):
@@ -145,30 +146,33 @@
 
 
 def finish(pre):
-    root = jnp.sqrt(pre * pre + 1.0)
-    return 0.65 * pre + 0.35 * (root - 1.0), 0.65 + 0.35 * pre / root
+    square = pre * pre + 1.0
+    inverse = lax.rsqrt(square)
+    return 0.65 * pre + 0.35 * (square * inverse - 1.0), 0.65 + 0.35 * (pre * inverse)
 
 
 def forward_body(a0, above, row, below, corner, t1, t2, t3, tt2, tt3, head, targets, inside,
                  p1, kept, slopes, sums, a1, a2):
-    in_upper = jnp.full((32, LANES), inside[0], f32)
-    in_row = jnp.full((16, LANES), inside[1], f32)
-    in_below = jnp.full((16, LANES), inside[2], f32)
-    in_corner = in_row * in_below
+    low = jnp.where(lane_of((32, LANES)) < HALF, 1.0, 0.0)
+    upper = (1.0 - low).astype(bf16)
+    upper_below = ((1.0 - low) * inside[0]).astype(bf16)
+    low_row = (low * inside[1]).astype(bf16)
+    low_below = (low * inside[2]).astype(bf16)
+    low_corner = (low * inside[1] * inside[2]).astype(bf16)
+    low = low.astype(bf16)
 
     def tile_one(zz, yy):
         yp = yy % 8
         part = slice(16 * (yy + 7), 16 * (yy + 8))
+        if zz >= 0 and yy >= 0:
+            return a0[zz, yp] * low + above[zz, yp] * upper
         if zz >= 0:
-            upper = above[zz, yp].astype(f32)
-            if yy < 0:
-                return joined(row[zz, part, :], in_row, pltpu.roll(upper, HALF, 1))
-            own = a0[zz, yp].astype(f32)
-            return jnp.where(lane_of(own.shape) < HALF, own, upper).astype(bf16)
-        upper = a0[zz + 8, yp].astype(f32) * in_upper
-        if yy < 0:
-            return joined(corner[zz + 7, part, :], in_corner, pltpu.roll(upper, HALF, 1))
-        return joined(below[zz + 7, 16 * yp : 16 * yp + 16, :], in_below, upper)
+            return unpacked(row[zz, part, :]) * low_row + half_turned(above[zz, yp]) * upper
+        if yy >= 0:
+            got = unpacked(below[zz + 7, 16 * yp : 16 * yp + 16, :])
+            return got * low_below + a0[zz + 8, yp] * upper_below
+        got = unpacked(corner[zz + 7, part, :])
+        return got * low_corner + half_turned(a0[zz + 8, yp]) * upper_below
 
     fill_patches(tile_one, (-3, 3), (-3, 3), 32, 16, p1)
     act, slopes[:, : 49 * LANES] = finish(dot(t1[...], p1[...]))

time: 86.6 us -> 86.3 us (level)
  no operation moved by 1% of the time
where the time goes in v6:
time: 86.3 us; the launch traced here: 85.9 us
  blocking collectives  57 us (66%)
  Pallas kernels  9.51 us (11%)
  waiting for transfers between devices  8.03 us (9%)
  starting transfers between devices  6.61 us (8%)
  local copies, waits for them, and re-layouts  2.01 us (2%)
  other arithmetic  1.99 us (2%)
    all_to_all x1, blocking collectives, local(): pooled = lax.all_to_all(sums, ('gz', 'gy'), 0, 0, tiled=True)  22.4 us
    all_to_all x1, blocking collectives, summed_over_all(): parts = lax.all_to_all(parts, ('batch', 'gz'), 0, 0, tiled=True)  12.5 us
    all_to_all x1, blocking collectives, summed_over_all(): return lax.all_to_all(parts, 'gy', 0, 0, tiled=True)  11.4 us
    all_to_all x1, blocking collectives, summed_over_all(): parts = lax.all_to_all(parts, 'gy', 0, 0, tiled=True)  10.7 us
    pallas_call x7, Pallas kernels, call(): pl.pallas_call(body, out_shape=[jax.ShapeDtypeStruct(s, d) for s, d in ou...  9.51 us
    ppermute x1, waiting for transfers between devices, exchange(): corner = lax.ppermute(corner, ('gz', 'gy'), both)  6.78 us
    ppermute x1, starting transfers between devices, exchange(): above = lax.ppermute(whole, 'gz', [(k, i) for i, k in z])  1.92 us
    ppermute x1, starting transfers between devices, exchange(): below = lax.ppermute(below, 'gz', z)  1.92 us
  transfers between devices with their start and end apart: 4, of which 2 were waited for; matrix products, arithmetic and copies ran while one was open for 3% of the time, Pallas kernels for 0%

profile of v6, /device:TPU:32, one launch (start us, length us, event | category | flops | bytes accessed | tf_op | source)
XLA Modules:
  0.0 85.9 jit_solution(6021012282590751230)
XLA Ops:
  0.6 0.0 copy-start.2
  0.6 0.0 copy-start.1
  0.7 0.1 add_convert_fusion.inside
  0.7 1.2 %copy-done = f32[1,4,8,16,512]{4,3,2,1,0:T(8,128)S(1)} copy-done((f32[1,4,8,16,512]{4,3,2,1,0:T(8,128)S(1)}, f32[1,4,8,16,512]{4,3,2,1,0:T(8,128)}, u32[]{:S(2)}) %copy-start) | copy-done | bytes 1048600
  2.0 0.7 shard_map.101
  2.7 1.9 %collective-permute-start = (bf16[8,8,32,128]{3,2,1,0:T(8,128)(2,1)S(1)}, bf16[8,8,32,128]{3,2,1,0:T(8,128)(2,1)S(1)}, u32[]{:S(2)}, u32[]{:S(2)}) collective-permute-start(bf16[8,8,32,128]{3,2,1,0:T(8,128)(2,1)S(1)} %get-tuple-element.27.a0), channel_id=1, source_target_pairs={{16,0},{32,16},{48,32},{64,48},{80,64},{96,80},{112,96},{0,112},{1... | collective-permute-start | bytes 1572872 | tf_op jit(solution)/shard_map/ppermute | solution.py:364
  4.6 1.2 %collective-permute-start.3 = (bf16[7,112,128]{2,1,0:T(8,128)(2,1)S(1)}, bf16[7,112,128]{2,1,0:T(8,128)(2,1)S(1)}, u32[]{:S(2)}, u32[]{:S(2)}) collective-permute-start(bf16[7,112,128]{2,1,0:T(8,128)(2,1)S(1)} %get-tuple-element.30), channel_id=1, source_target_pairs={{0,17},{1,18},{2,19},{3,20},{4,21},{5,22},{6,23},{7,24},{8,25},{9,... | collective-permute-start | bytes 602120 | tf_op jit(solution)/shard_map/ppermute | solution.py:366
  5.8 1.6 %collective-permute-start.1 = (bf16[8,112,128]{2,1,0:T(8,128)(2,1)S(1)}, bf16[8,112,128]{2,1,0:T(8,128)(2,1)S(1)}, u32[]{:S(2)}, u32[]{:S(2)}) collective-permute-start(bf16[8,112,128]{2,1,0:T(8,128)(2,1)S(1)} %get-tuple-element.28), channel_id=1, source_target_pairs={{0,1},{1,2},{2,3},{3,4},{4,5},{5,6},{6,7},{7,8},{8,9},{9,10},{10,1... | collective-permute-start | bytes 688136 | tf_op jit(solution)/shard_map/ppermute | solution.py:367
  7.3 1.9 %collective-permute-start.2 = (bf16[7,128,128]{2,1,0:T(8,128)(2,1)S(1)}, bf16[7,128,128]{2,1,0:T(8,128)(2,1)S(1)}, u32[]{:S(2)}, u32[]{:S(2)}) collective-permute-start(bf16[7,128,128]{2,1,0:T(8,128)(2,1)S(1)} %get-tuple-element.29), channel_id=1, source_target_pairs={{0,16},{16,32},{32,48},{48,64},{64,80},{80,96},{96,112},{112,0},{1... | collective-permute-start | bytes 688136 | tf_op jit(solution)/shard_map/ppermute | solution.py:365
  9.3 0.8 pad.21
  10.1 0.9 %pad_convert_fusion.1.w2 = f32[27,16,128]{2,1,0:T(8,128)S(1)} fusion(bf16[27,16,32]{2,1,0:T(8,128)(2,1)} %bitcast.41), kind=kLoop, calls=%fused_computation.1 | loop fusion | flops 55296 | bytes 248832 | tf_op jit(solution)/shard_map/jit(_pad)/pad | solution.py:390
  11.0 1.0 %pad_convert_fusion.w3 = f32[27,32,128]{2,1,0:T(8,128)S(1)} fusion(bf16[27,32,64]{2,1,0:T(8,128)(2,1)} %bitcast.39), kind=kLoop, calls=%fused_computation | loop fusion | flops 110592 | bytes 552960 | tf_op jit(solution)/shard_map/jit(_pad)/pad | solution.py:390
  12.0 0.4 shard_map.102
  12.4 6.8 %collective-permute-done.3.corner = bf16[7,112,128]{2,1,0:T(8,128)(2,1)S(1)} collective-permute-done((bf16[7,112,128]{2,1,0:T(8,128)(2,1)S(1)}, bf16[7,112,128]{2,1,0:T(8,128)(2,1)S(1)}, u32[]{:S(2)}, u32[]{:S(2)}) %collective-permute-start.3) | collective-permute-done | bytes 200736 | tf_op jit(solution)/shard_map/ppermute | solution.py:366
  19.2 1.2 %collective-permute-done.1.row = bf16[8,112,128]{2,1,0:T(8,128)(2,1)S(1)} collective-permute-done((bf16[8,112,128]{2,1,0:T(8,128)(2,1)S(1)}, bf16[8,112,128]{2,1,0:T(8,128)(2,1)S(1)}, u32[]{:S(2)}, u32[]{:S(2)}) %collective-permute-start.1) | collective-permute-done | bytes 229408 | tf_op jit(solution)/shard_map/ppermute | solution.py:367
  20.4 0.0 collective-permute-done.2.below
  20.4 0.0 collective-permute-done.above
  20.5 3.5 %shard_map.103 = (bf16[432,6272]{1,0:T(8,128)(2,1)S(1)}, bf16[864,1536]{1,0:T(8,128)(2,1)S(1)}, f32[64,7680]{1,0:T(8,128)S(1)}, f32[128,128]{1,0:T(8,128)S(1)}) custom-call(bf16[8,8,32,128]{3,2,1,0:T(8,128)(2,1)S(1)} %get-tuple-element.27.a0, bf16[8,8,32,128]{3,2,1,0:T(8,128)(2,1)S(1)} %collective-permute-done.above, ...), custom_call_target="tpu_custom_call" | custom-call | tf_op jit(solution)/shard_map/pallas_call | solution.py:20
  24.0 22.4 %all_to_all.26 = f32[128,1,128]{2,1,0:T(1,128)S(1)} all-to-all(f32[128,1,128]{2,1,0:T(1,128)S(1)} %bitcast.36), channel_id=1, replica_groups=mesh['batch'=2,'gz'=8,'gy'=16] {'gz','gy'}, dimensions={0} | all-to-all | bytes 131072 | tf_op jit(solution)/shard_map/all_to_all | solution.py:415
  46.3 3.6 %shard_map.104 = bf16[16,40,128]{2,1,0:T(8,128)(2,1)S(1)} custom-call(f32[128,128]{1,0:T(8,128)S(1)} %bitcast.35, bf16[432,6272]{1,0:T(8,128)(2,1)S(1)} %get-tuple-element.38.p1, bf16[864,1536]{1,0:T(8,128)(2,1)S(1)} %get-tuple-element.39.kept, f32[64,7680]{1,0:T(8,128)S(1)} %get-tuple-element.40.slopes), custom_call_target="tpu_custom_call" | custom-call | tf_op jit(solution)/shard_map/pallas_call | solution.py:20
  50.0 10.7 %all_to_all.27.parts = bf16[16,40,128]{2,1,0:T(8,128)(2,1)S(1)} all-to-all(bf16[16,40,128]{2,1,0:T(8,128)(2,1)S(1)} %shard_map.104), channel_id=1, replica_groups=mesh['batch'=2,'gz'=8,'gy'=16] {'gy'}, dimensions={0} | all-to-all | bytes 327680 | tf_op jit(solution)/shard_map/all_to_all | solution.py:373
  60.7 12.5 %all_to_all.28.parts = bf16[16,40,128]{2,1,0:T(8,128)(2,1)S(1)} all-to-all(bf16[16,40,128]{2,1,0:T(8,128)(2,1)S(1)} %shard_map.105), channel_id=1, replica_groups=mesh['batch'=2,'gz'=8,'gy'=16] {'batch','gz'}, dimensions={0} | all-to-all | bytes 327680 | tf_op jit(solution)/shard_map/all_to_all | solution.py:375
  73.3 11.4 %all_to_all.29.sent = bf16[16,40,128]{2,1,0:T(8,128)(2,1)S(1)} all-to-all(bf16[16,40,128]{2,1,0:T(8,128)(2,1)S(1)} %shard_map.106), channel_id=1, replica_groups=mesh['batch'=2,'gz'=8,'gy'=16] {'gy'}, dimensions={0} | all-to-all | bytes 327680 | tf_op jit(solution)/shard_map/all_to_all | solution.py:377
  84.7 1.2 %shard_map.107 = (f32[27,4,16]{2,1,0:T(4,128)}, f32[27,16,32]{2,1,0:T(8,128)}, f32[27,32,64]{2,1,0:T(8,128)}, f32[4,64]{1,0:T(4,128)}, f32[1,128]{1,0:T(1,128)}) custom-call(bf16[16,40,128]{2,1,0:T(8,128)(2,1)S(1)} %all_to_all.29.sent), custom_call_target="tpu_custom_call" | custom-call | tf_op jit(solution)/shard_map/pallas_call | solution.py:20
  (8 shorter events, 0.1 us)
Async XLA Ops:
  0.6 19.8 %copy-start.2 = (f32[1,4]{1,0:T(1,128)S(1)}, f32[1,4]{1,0:T(1,128)}, u32[]{:S(2)}) copy-start(f32[1,4]{1,0:T(1,128)} %targets.1) | copy-start | bytes 52
  0.6 19.8 %copy-start.1 = (f32[4,64]{1,0:T(4,128)S(1)}, f32[4,64]{1,0:T(4,128)}, u32[]{:S(2)}) copy-start(f32[4,64]{1,0:T(4,128)} %head.1) | copy-start | bytes 3076
  0.7 1.2 %copy-start = (f32[1,4,8,16,512]{4,3,2,1,0:T(8,128)S(1)}, f32[1,4,8,16,512]{4,3,2,1,0:T(8,128)}, u32[]{:S(2)}) copy-start(f32[1,4,8,16,512]{4,3,2,1,0:T(8,128)} %param.6) | copy-start | bytes 3145732
  2.7 17.8 %collective-permute-start = (bf16[8,8,32,128]{3,2,1,0:T(8,128)(2,1)S(1)}, bf16[8,8,32,128]{3,2,1,0:T(8,128)(2,1)S(1)}, u32[]{:S(2)}, u32[]{:S(2)}) collective-permute-start(bf16[8,8,32,128]{3,2,1,0:T(8,128)(2,1)S(1)} %get-tuple-element.27.a0), channel_id=1, source_target_pairs={{16,0},{32,16},{48,32},{64,48},{80,64},{96,80},{112,96},{0,112},{1... | collective-permute-start | bytes 1572872 | tf_op jit(solution)/shard_map/ppermute | solution.py:364
  4.6 14.6 %collective-permute-start.3 = (bf16[7,112,128]{2,1,0:T(8,128)(2,1)S(1)}, bf16[7,112,128]{2,1,0:T(8,128)(2,1)S(1)}, u32[]{:S(2)}, u32[]{:S(2)}) collective-permute-start(bf16[7,112,128]{2,1,0:T(8,128)(2,1)S(1)} %get-tuple-element.30), channel_id=1, source_target_pairs={{0,17},{1,18},{2,19},{3,20},{4,21},{5,22},{6,23},{7,24},{8,25},{9,... | collective-permute-start | bytes 602120 | tf_op jit(solution)/shard_map/ppermute | solution.py:366
  5.8 14.7 %collective-permute-start.1 = (bf16[8,112,128]{2,1,0:T(8,128)(2,1)S(1)}, bf16[8,112,128]{2,1,0:T(8,128)(2,1)S(1)}, u32[]{:S(2)}, u32[]{:S(2)}) collective-permute-start(bf16[8,112,128]{2,1,0:T(8,128)(2,1)S(1)} %get-tuple-element.28), channel_id=1, source_target_pairs={{0,1},{1,2},{2,3},{3,4},{4,5},{5,6},{6,7},{7,8},{8,9},{9,10},{10,1... | collective-permute-start | bytes 688136 | tf_op jit(solution)/shard_map/ppermute | solution.py:367
  7.3 13.1 %collective-permute-start.2 = (bf16[7,128,128]{2,1,0:T(8,128)(2,1)S(1)}, bf16[7,128,128]{2,1,0:T(8,128)(2,1)S(1)}, u32[]{:S(2)}, u32[]{:S(2)}) collective-permute-start(bf16[7,128,128]{2,1,0:T(8,128)(2,1)S(1)} %get-tuple-element.29), channel_id=1, source_target_pairs={{0,16},{16,32},{32,48},{48,64},{64,80},{80,96},{96,112},{112,0},{1... | collective-permute-start | bytes 688136 | tf_op jit(solution)/shard_map/ppermute | solution.py:365

commit v7 on v6

--- a/solution.py
+++ b/solution.py
@@ -70,7 +70,7 @@
     return slice(group * LANES, (group + 1) * LANES)
 
 
-def arrange_body(vol, a0, row, below, corner, rows):
+def arrange_body(vol, a0, up, row, below, corner, rows):
     for z in range(8):
         tops = [c * 128 + z * 16 + yb * 8 for yb in range(2) for c in range(4)]
         cube = jnp.stack([vol[top : top + 8, :] for top in tops], axis=0)
@@ -88,7 +88,10 @@
     whole = jnp.concatenate(parts, axis=1).astype(bf16)
     a0[...] = whole.reshape(8, 8, 32, LANES)
     for z in range(8):
+        up[z, :16, :] = upper_half(a0[z, 0])
         for yp in range(8):
+            if yp > 0:
+                up[z, 32 * yp - 16 : 32 * yp + 16, :] = a0[z, yp]
             if z > 0:
                 below[z - 1, 16 * yp : 16 * yp + 16, :] = lower_half(a0[z, yp])
         for yp in range(1, 8):
@@ -165,9 +168,12 @@
         yp = yy % 8
         part = slice(16 * (yy + 7), 16 * (yy + 8))
         if zz >= 0 and yy >= 0:
-            return a0[zz, yp] * low + above[zz, yp] * upper
+            if yp > 0:
+                return a0[zz, yp] * low + above[zz, 32 * yp - 16 : 32 * yp + 16, :] * upper
+            got = above[zz, :16, :]
+            return a0[zz, yp] * low + jnp.concatenate([half_turned(got), got], axis=0) * upper
         if zz >= 0:
-            return unpacked(row[zz, part, :]) * low_row + half_turned(above[zz, yp]) * upper
+            return unpacked(row[zz, part, :]) * low_row + half_turned(above[zz, 32 * yp - 16 : 32 * yp + 16, :]) * upper
         if yy >= 0:
             got = unpacked(below[zz + 7, 16 * yp : 16 * yp + 16, :])
             return got * low_below + a0[zz + 8, yp] * upper_below
@@ -397,13 +403,13 @@
         [((64, 432), bf16), ((64, 720), bf16), ((64, 864), bf16), ((720, LANES), bf16), ((864, LANES), bf16)],
         (jnp.concatenate([both, low], axis=1), taps(conv_two), taps(conv_three)),
     )
-    a0, row, below, corner = call(
+    a0, up, row, below, corner = call(
         arrange_body,
-        [((8, 8, 32, LANES), bf16), ((8, 112, LANES), bf16), ((7, LANES, LANES), bf16), ((7, 112, LANES), bf16)],
+        [((8, 8, 32, LANES), bf16), ((8, 240, LANES), bf16), ((8, 112, LANES), bf16), ((7, LANES, LANES), bf16), ((7, 112, LANES), bf16)],
         (volume.reshape(512, 512),),
         [((512, 512), f32)],
     )
-    above, row, below, corner = exchange(a0, row, below, corner)
+    above, row, below, corner = exchange(up, row, below, corner)
     p1, kept, slopes, sums = call(
         forward_body,
         [((432, 49 * LANES), bf16), ((864, 12 * LANES), bf16), ((64, 60 * LANES), f32), ((devices, LANES), f32)],

time: 86.3 us -> 86.3 us (level)
  no operation moved by 1% of the time
where the time goes in v7:
time: 86.3 us; the launch traced here: 85.9 us
  blocking collectives  57 us (66%)
  Pallas kernels  9.57 us (11%)
  waiting for transfers between devices  8.03 us (9%)
  starting transfers between devices  6.61 us (8%)
  local copies, waits for them, and re-layouts  2.01 us (2%)
  other arithmetic  1.99 us (2%)
    all_to_all x1, blocking collectives, local(): pooled = lax.all_to_all(sums, ('gz', 'gy'), 0, 0, tiled=True)  22.4 us
    all_to_all x1, blocking collectives, summed_over_all(): parts = lax.all_to_all(parts, ('batch', 'gz'), 0, 0, tiled=True)  12.5 us
    all_to_all x1, blocking collectives, summed_over_all(): return lax.all_to_all(parts, 'gy', 0, 0, tiled=True)  11.4 us
    all_to_all x1, blocking collectives, summed_over_all(): parts = lax.all_to_all(parts, 'gy', 0, 0, tiled=True)  10.7 us
    pallas_call x7, Pallas kernels, call(): pl.pallas_call(body, out_shape=[jax.ShapeDtypeStruct(s, d) for s, d in ou...  9.57 us
    ppermute x1, waiting for transfers between devices, exchange(): corner = lax.ppermute(corner, ('gz', 'gy'), both)  6.78 us
    ppermute x1, starting transfers between devices, exchange(): above = lax.ppermute(whole, 'gz', [(k, i) for i, k in z])  1.92 us
    ppermute x1, starting transfers between devices, exchange(): below = lax.ppermute(below, 'gz', z)  1.92 us
  transfers between devices with their start and end apart: 4, of which 2 were waited for; matrix products, arithmetic and copies ran while one was open for 3% of the time, Pallas kernels for 0%

profile of v7, /device:TPU:32, one launch (start us, length us, event | category | flops | bytes accessed | tf_op | source)
XLA Modules:
  0.0 85.9 jit_solution(13244608181545794632)
XLA Ops:
  0.6 0.0 copy-start.2
  0.6 0.0 copy-start.1
  0.7 0.1 add_convert_fusion.inside
  0.7 1.2 %copy-done = f32[1,4,8,16,512]{4,3,2,1,0:T(8,128)S(1)} copy-done((f32[1,4,8,16,512]{4,3,2,1,0:T(8,128)S(1)}, f32[1,4,8,16,512]{4,3,2,1,0:T(8,128)}, u32[]{:S(2)}) %copy-start) | copy-done | bytes 1048600
  2.0 0.7 shard_map.101
  2.7 1.9 %collective-permute-start = (bf16[8,240,128]{2,1,0:T(8,128)(2,1)S(1)}, bf16[8,240,128]{2,1,0:T(8,128)(2,1)S(1)}, u32[]{:S(2)}, u32[]{:S(2)}) collective-permute-start(bf16[8,240,128]{2,1,0:T(8,128)(2,1)S(1)} %get-tuple-element.29), channel_id=1, source_target_pairs={{16,0},{32,16},{48,32},{64,48},{80,64},{96,80},{112,96},{0,112},{1... | collective-permute-start | bytes 1474568 | tf_op jit(solution)/shard_map/ppermute | solution.py:370
  4.6 1.2 %collective-permute-start.3 = (bf16[7,112,128]{2,1,0:T(8,128)(2,1)S(1)}, bf16[7,112,128]{2,1,0:T(8,128)(2,1)S(1)}, u32[]{:S(2)}, u32[]{:S(2)}) collective-permute-start(bf16[7,112,128]{2,1,0:T(8,128)(2,1)S(1)} %get-tuple-element.32), channel_id=1, source_target_pairs={{0,17},{1,18},{2,19},{3,20},{4,21},{5,22},{6,23},{7,24},{8,25},{9,... | collective-permute-start | bytes 602120 | tf_op jit(solution)/shard_map/ppermute | solution.py:372
  5.8 1.6 %collective-permute-start.1 = (bf16[8,112,128]{2,1,0:T(8,128)(2,1)S(1)}, bf16[8,112,128]{2,1,0:T(8,128)(2,1)S(1)}, u32[]{:S(2)}, u32[]{:S(2)}) collective-permute-start(bf16[8,112,128]{2,1,0:T(8,128)(2,1)S(1)} %get-tuple-element.30), channel_id=1, source_target_pairs={{0,1},{1,2},{2,3},{3,4},{4,5},{5,6},{6,7},{7,8},{8,9},{9,10},{10,1... | collective-permute-start | bytes 688136 | tf_op jit(solution)/shard_map/ppermute | solution.py:373
  7.4 1.9 %collective-permute-start.2 = (bf16[7,128,128]{2,1,0:T(8,128)(2,1)S(1)}, bf16[7,128,128]{2,1,0:T(8,128)(2,1)S(1)}, u32[]{:S(2)}, u32[]{:S(2)}) collective-permute-start(bf16[7,128,128]{2,1,0:T(8,128)(2,1)S(1)} %get-tuple-element.31), channel_id=1, source_target_pairs={{0,16},{16,32},{32,48},{48,64},{64,80},{80,96},{96,112},{112,0},{1... | collective-permute-start | bytes 688136 | tf_op jit(solution)/shard_map/ppermute | solution.py:371
  9.3 0.8 pad.21
  10.1 0.9 %pad_convert_fusion.1.w2 = f32[27,16,128]{2,1,0:T(8,128)S(1)} fusion(bf16[27,16,32]{2,1,0:T(8,128)(2,1)} %bitcast.41), kind=kLoop, calls=%fused_computation.1 | loop fusion | flops 55296 | bytes 248832 | tf_op jit(solution)/shard_map/jit(_pad)/pad | solution.py:396
  11.1 1.0 %pad_convert_fusion.w3 = f32[27,32,128]{2,1,0:T(8,128)S(1)} fusion(bf16[27,32,64]{2,1,0:T(8,128)(2,1)} %bitcast.39), kind=kLoop, calls=%fused_computation | loop fusion | flops 110592 | bytes 552960 | tf_op jit(solution)/shard_map/jit(_pad)/pad | solution.py:396
  12.0 0.4 shard_map.102
  12.5 6.8 %collective-permute-done.3.corner = bf16[7,112,128]{2,1,0:T(8,128)(2,1)S(1)} collective-permute-done((bf16[7,112,128]{2,1,0:T(8,128)(2,1)S(1)}, bf16[7,112,128]{2,1,0:T(8,128)(2,1)S(1)}, u32[]{:S(2)}, u32[]{:S(2)}) %collective-permute-start.3) | collective-permute-done | bytes 200736 | tf_op jit(solution)/shard_map/ppermute | solution.py:372
  19.3 1.2 %collective-permute-done.1.row = bf16[8,112,128]{2,1,0:T(8,128)(2,1)S(1)} collective-permute-done((bf16[8,112,128]{2,1,0:T(8,128)(2,1)S(1)}, bf16[8,112,128]{2,1,0:T(8,128)(2,1)S(1)}, u32[]{:S(2)}, u32[]{:S(2)}) %collective-permute-start.1) | collective-permute-done | bytes 229408 | tf_op jit(solution)/shard_map/ppermute | solution.py:373
  20.5 0.0 collective-permute-done.2.below
  20.5 0.0 collective-permute-done.above
  20.5 3.5 %shard_map.103 = (bf16[432,6272]{1,0:T(8,128)(2,1)S(1)}, bf16[864,1536]{1,0:T(8,128)(2,1)S(1)}, f32[64,7680]{1,0:T(8,128)S(1)}, f32[128,128]{1,0:T(8,128)S(1)}) custom-call(bf16[8,8,32,128]{3,2,1,0:T(8,128)(2,1)S(1)} %get-tuple-element.28.a0, bf16[8,240,128]{2,1,0:T(8,128)(2,1)S(1)} %collective-permute-done.above, ...), custom_call_target="tpu_custom_call" | custom-call | tf_op jit(solution)/shard_map/pallas_call | solution.py:20
  24.0 22.4 %all_to_all.26 = f32[128,1,128]{2,1,0:T(1,128)S(1)} all-to-all(f32[128,1,128]{2,1,0:T(1,128)S(1)} %bitcast.36), channel_id=1, replica_groups=mesh['batch'=2,'gz'=8,'gy'=16] {'gz','gy'}, dimensions={0} | all-to-all | bytes 131072 | tf_op jit(solution)/shard_map/all_to_all | solution.py:421
  46.4 3.6 %shard_map.104 = bf16[16,40,128]{2,1,0:T(8,128)(2,1)S(1)} custom-call(f32[128,128]{1,0:T(8,128)S(1)} %bitcast.35, bf16[432,6272]{1,0:T(8,128)(2,1)S(1)} %get-tuple-element.40.p1, bf16[864,1536]{1,0:T(8,128)(2,1)S(1)} %get-tuple-element.41.kept, f32[64,7680]{1,0:T(8,128)S(1)} %get-tuple-element.42.slopes), custom_call_target="tpu_custom_call" | custom-call | tf_op jit(solution)/shard_map/pallas_call | solution.py:20
  50.0 10.7 %all_to_all.27.parts = bf16[16,40,128]{2,1,0:T(8,128)(2,1)S(1)} all-to-all(bf16[16,40,128]{2,1,0:T(8,128)(2,1)S(1)} %shard_map.104), channel_id=1, replica_groups=mesh['batch'=2,'gz'=8,'gy'=16] {'gy'}, dimensions={0} | all-to-all | bytes 327680 | tf_op jit(solution)/shard_map/all_to_all | solution.py:379
  60.8 12.5 %all_to_all.28.parts = bf16[16,40,128]{2,1,0:T(8,128)(2,1)S(1)} all-to-all(bf16[16,40,128]{2,1,0:T(8,128)(2,1)S(1)} %shard_map.105), channel_id=1, replica_groups=mesh['batch'=2,'gz'=8,'gy'=16] {'batch','gz'}, dimensions={0} | all-to-all | bytes 327680 | tf_op jit(solution)/shard_map/all_to_all | solution.py:381
  73.4 11.4 %all_to_all.29.sent = bf16[16,40,128]{2,1,0:T(8,128)(2,1)S(1)} all-to-all(bf16[16,40,128]{2,1,0:T(8,128)(2,1)S(1)} %shard_map.106), channel_id=1, replica_groups=mesh['batch'=2,'gz'=8,'gy'=16] {'gy'}, dimensions={0} | all-to-all | bytes 327680 | tf_op jit(solution)/shard_map/all_to_all | solution.py:383
  84.8 1.2 %shard_map.107 = (f32[27,4,16]{2,1,0:T(4,128)}, f32[27,16,32]{2,1,0:T(8,128)}, f32[27,32,64]{2,1,0:T(8,128)}, f32[4,64]{1,0:T(4,128)}, f32[1,128]{1,0:T(1,128)}) custom-call(bf16[16,40,128]{2,1,0:T(8,128)(2,1)S(1)} %all_to_all.29.sent), custom_call_target="tpu_custom_call" | custom-call | tf_op jit(solution)/shard_map/pallas_call | solution.py:20
  (8 shorter events, 0.1 us)
Async XLA Ops:
  0.6 19.9 %copy-start.2 = (f32[1,4]{1,0:T(1,128)S(1)}, f32[1,4]{1,0:T(1,128)}, u32[]{:S(2)}) copy-start(f32[1,4]{1,0:T(1,128)} %targets.1) | copy-start | bytes 52
  0.6 19.9 %copy-start.1 = (f32[4,64]{1,0:T(4,128)S(1)}, f32[4,64]{1,0:T(4,128)}, u32[]{:S(2)}) copy-start(f32[4,64]{1,0:T(4,128)} %head.1) | copy-start | bytes 3076
  0.7 1.2 %copy-start = (f32[1,4,8,16,512]{4,3,2,1,0:T(8,128)S(1)}, f32[1,4,8,16,512]{4,3,2,1,0:T(8,128)}, u32[]{:S(2)}) copy-start(f32[1,4,8,16,512]{4,3,2,1,0:T(8,128)} %param.6) | copy-start | bytes 3145732
  2.7 17.8 %collective-permute-start = (bf16[8,240,128]{2,1,0:T(8,128)(2,1)S(1)}, bf16[8,240,128]{2,1,0:T(8,128)(2,1)S(1)}, u32[]{:S(2)}, u32[]{:S(2)}) collective-permute-start(bf16[8,240,128]{2,1,0:T(8,128)(2,1)S(1)} %get-tuple-element.29), channel_id=1, source_target_pairs={{16,0},{32,16},{48,32},{64,48},{80,64},{96,80},{112,96},{0,112},{1... | collective-permute-start | bytes 1474568 | tf_op jit(solution)/shard_map/ppermute | solution.py:370
  4.6 14.6 %collective-permute-start.3 = (bf16[7,112,128]{2,1,0:T(8,128)(2,1)S(1)}, bf16[7,112,128]{2,1,0:T(8,128)(2,1)S(1)}, u32[]{:S(2)}, u32[]{:S(2)}) collective-permute-start(bf16[7,112,128]{2,1,0:T(8,128)(2,1)S(1)} %get-tuple-element.32), channel_id=1, source_target_pairs={{0,17},{1,18},{2,19},{3,20},{4,21},{5,22},{6,23},{7,24},{8,25},{9,... | collective-permute-start | bytes 602120 | tf_op jit(solution)/shard_map/ppermute | solution.py:372
  5.8 14.7 %collective-permute-start.1 = (bf16[8,112,128]{2,1,0:T(8,128)(2,1)S(1)}, bf16[8,112,128]{2,1,0:T(8,128)(2,1)S(1)}, u32[]{:S(2)}, u32[]{:S(2)}) collective-permute-start(bf16[8,112,128]{2,1,0:T(8,128)(2,1)S(1)} %get-tuple-element.30), channel_id=1, source_target_pairs={{0,1},{1,2},{2,3},{3,4},{4,5},{5,6},{6,7},{7,8},{8,9},{9,10},{10,1... | collective-permute-start | bytes 688136 | tf_op jit(solution)/shard_map/ppermute | solution.py:373
  7.4 13.1 %collective-permute-start.2 = (bf16[7,128,128]{2,1,0:T(8,128)(2,1)S(1)}, bf16[7,128,128]{2,1,0:T(8,128)(2,1)S(1)}, u32[]{:S(2)}, u32[]{:S(2)}) collective-permute-start(bf16[7,128,128]{2,1,0:T(8,128)(2,1)S(1)} %get-tuple-element.31), channel_id=1, source_target_pairs={{0,16},{16,32},{32,48},{48,64},{64,80},{80,96},{96,112},{112,0},{1... | collective-permute-start | bytes 688136 | tf_op jit(solution)/shard_map/ppermute | solution.py:371
